TPU v7x, 32 devices: a whole 2x2x4 slice. The times are simulated.
32 devices in a mesh: inline: 16 (over z, y, x), xline: 2 (over core).
Axes of the slice: x: 2, y: 2, z: 4, core: 2. Of those that a mesh axis runs over, the one named last changes fastest.
Arguments:
- source_field: bfloat16 [4, 2, 2048, 128], P(None, 'xline', 'inline'), may hold values from -6 to 6
- receiver_field: bfloat16 [4, 2, 2048, 128], P(None, 'xline', 'inline'), may hold values from -6 to 6
- sat_mask: int32 [2, 2048, 128], P('xline', 'inline'), may hold values 0 or 1
- offset_range: int32 [16], P('inline'), may hold values from 8 to 32, as said below
Outputs:
- source_adjoint: bfloat16 [4, 2, 2048, 128], P(None, 'xline', 'inline')
- receiver_adjoint: bfloat16 [4, 2, 2048, 128], P(None, 'xline', 'inline')
- semblance: float32 [], replicated
Inputs may be any that keep to these rules, and one draw needn't show every extreme that they name: `offset_range`: some slab has exactly 32.
All inputs are finite; a program needn't handle non-finite values. No bound on the sum of `sat_mask` on one device may be relied on, other than what follows from the above.
Results may differ from a plain program's by a relative error of at most 0.00075.
Values may be sent and summed in bfloat16 or wider, within the bound.
No kernel may reach another device: no remote copies, remote signals or barrier semaphores. Data moves between devices by JAX's collectives and lax.ppermute only.
A program may use at most 64 MiB of HBM per device.

v0:
```python
import functools

import jax
import jax.numpy as jnp
from jax import lax
from jax.experimental import pallas as pl
from jax.experimental.pallas import tpu as pltpu
from jax.sharding import PartitionSpec as P

H = 32
EPSILON = 1e-06
SATURATION = 0.25
REACH = 2 * H
ALWAYS = 8
SHARED = H // 2
ROWS = 8
PAIR = 2 * ROWS
LIMIT_ROWS = 16
PIECES = 4
DEVICES = ("inline", "xline")
GROUP = 8
GRANT = 12 << 20
VMEM = pl.BlockSpec(memory_space=pltpu.VMEM)
SMEM = pl.BlockSpec(memory_space=pltpu.SMEM)


def square_weight(offset):
    relative = (offset / H) ** 2
    return relative * relative


def payload_layout(times, lines):
    mask_at = times * lines * REACH
    return mask_at, mask_at + lines * H


def by_parity(even, odd, work):
    here, size = lax.axis_index("inline"), lax.axis_size("inline")
    parity = lax.rem(here, 2)
    below, above = (here > 0).astype(jnp.float32), (here < size - 1).astype(jnp.float32)

    @pl.when(parity == 0)
    def _():
        work(even, False, above)
        work(odd, True, below)

    @pl.when(parity != 0)
    def _():
        work(even, True, below)
        work(odd, False, above)


def edges(value, axis, width):
    depth = value.shape[-1]
    length = value.shape[axis]
    low = lax.slice_in_dim(value, 0, width, axis=axis).reshape(-1, depth)
    return low, lax.slice_in_dim(value, length - width, length, axis=axis).reshape(-1, depth)


def for_even(low, high):
    return jnp.where(lax.axis_index("inline") % 2 == 0, high, low)


def for_odd(low, high):
    return for_even(high, low)


def payloads(rcv, sat, limit):
    depth = rcv.shape[-1]
    rows = edges(rcv, 2, REACH)
    rows = for_even(*rows), for_odd(*rows)
    *rows, sat = lax.optimization_barrier((*rows, sat))
    masks = edges((sat != 0).astype(jnp.bfloat16), 1, H)
    limits = jnp.full((LIMIT_ROWS, depth), limit[0]).astype(jnp.bfloat16)
    return [
        jnp.concatenate([part, choose(*masks), limits], axis=0) for part, choose in zip(rows, (for_even, for_odd))
    ]


def unpack_marks(times, limit, sat, even_in, odd_in, masks, limits):
    lines, cells, depth = sat.shape
    mask_at, limit_at = payload_layout(times, lines)

    def halo(arrived, low, there):
        row_at = 0 if low else H + cells
        for y in range(lines):
            masks[y, pl.ds(row_at, H), :] = arrived[pl.ds(mask_at + y * H, H), :].astype(jnp.float32)
        value = arrived[pl.ds(limit_at, LIMIT_ROWS), :].astype(jnp.float32)
        for part in range(H // LIMIT_ROWS):
            limits[pl.ds(row_at + part * LIMIT_ROWS, LIMIT_ROWS), :] = value

    by_parity(even_in, odd_in, halo)
    for y in range(lines):
        masks[y, pl.ds(H, cells), :] = (sat[y] != 0).astype(jnp.float32)
    limits[pl.ds(H, cells), :] = jnp.full((cells, depth), limit[0], jnp.int32).astype(jnp.float32)


def unpack_halo(even_in, odd_in, low_out, high_out):
    times, lines, _, depth = low_out.shape
    blank = jnp.zeros((ROWS, depth), jnp.float32)

    def halo(arrived, low, there):
        out, field_at, blank_at = (low_out, 0, REACH) if low else (high_out, ROWS, 0)
        for t in range(times):
            for y in range(lines):
                at = (t * lines + y) * REACH
                out[t, y, pl.ds(field_at, REACH), :] = arrived[pl.ds(at, REACH), :].astype(jnp.float32) * there
                out[t, y, pl.ds(blank_at, ROWS), :] = blank

    by_parity(even_in, odd_in, halo)


def image_of(center, far):
    image = center[0] * far[0]
    for c, f in zip(center[1:], far[1:]):
        image = image + c * f
    return image


def accumulate(center, sums, offsets, far_at, masked, mask_at):
    heavy, plain = sums
    times = range(len(center))
    near = {}
    for offset in offsets:
        far = far_at(offset)
        image = masked(image_of(center, far), offset)
        if abs(offset) <= SHARED:
            terms = [image * f for f in far]
            if abs(offset) in near:
                terms = [a + b for a, b in zip(near.pop(abs(offset)), terms)]
            near[abs(offset)] = terms
            if offset == 0 or -offset not in offsets or offset > 0:
                near.pop(abs(offset))
                plain = [plain[t] + terms[t] for t in times]
                if offset:
                    square = square_weight(offset)
                    heavy = [heavy[t] + terms[t] * square for t in times]
        else:
            square = square_weight(offset)
            weighed = image * jnp.where(mask_at(offset) != 0.0, SATURATION * SATURATION, square)
            plain = [plain[t] + image * far[t] for t in times]
            heavy = [heavy[t] + weighed * far[t] for t in times]
    return heavy, plain


def paired(largest, smallest=0):
    return [sign * size for size in range(smallest, largest + 1) for sign in ((-1, 1) if size else (1,))]


def tiles_of(field, y, base):
    times = field.shape[0]
    both = [field[t, y, pl.ds(base, PAIR), :].astype(jnp.float32) for t in range(times)]
    return [[rows[half * ROWS : (half + 1) * ROWS] for rows in both] for half in range(2)]


def inner_kernel(first, limit, middle, field, sat, heavy_out, plain_out, shifted, masks):
    times, lines, cells, depth = field.shape
    zero = jnp.zeros((ROWS, depth), jnp.float32)
    blank = jnp.zeros((REACH, depth), jnp.float32)
    for t in range(times):
        for y in range(lines):
            shifted[t, y, pl.ds(0, REACH), :] = blank
            shifted[t, y, pl.ds(REACH, cells), :] = field[t, y].astype(jnp.float32)
            shifted[t, y, pl.ds(REACH + cells, REACH), :] = blank
    for y in range(lines):
        masks[y, pl.ds(0, H), :] = blank[:H]
        masks[y, pl.ds(H, cells), :] = (sat[y] != 0).astype(jnp.float32)
        masks[y, pl.ds(H + cells, H), :] = blank[:H]
    inside = [(size <= limit[0]).astype(jnp.float32) for size in range(H + 1)]

    def tile(index, carry):
        base = pl.multiple_of(index * PAIR, PAIR)
        for y in range(lines):
            for half, center in enumerate(tiles_of(middle, y, first + base)):
                at = first + base + half * ROWS

                def add(offsets, sums):
                    return accumulate(
                        center,
                        sums,
                        offsets,
                        lambda h: [shifted[t, y, pl.ds(at + REACH + 2 * h, ROWS), :] for t in range(times)],
                        lambda image, h: image * inside[abs(h)] if abs(h) > ALWAYS else image,
                        lambda h: masks[y, pl.ds(at + H + h, ROWS), :],
                    )

                sums = add(paired(SHARED), ([zero] * times, [zero] * times))
                for low in range(SHARED + 1, H + 1, GROUP):
                    sizes = range(low, min(low + GROUP, H + 1))
                    reaches = (
                        first + base + PAIR - 1 - 2 * low >= 0,
                        first + base + 2 * low < cells,
                    )
                    for sign, reach in zip((-1, 1), reaches):
                        offsets = [sign * size for size in sizes]
                        sums = lax.cond(reach, functools.partial(add, offsets), lambda kept: kept, sums)
                heavy, plain = sums
                rows = pl.ds(base + half * ROWS, ROWS)
                for t in range(times):
                    heavy_out[t, y, rows, :] = heavy[t]
                    plain_out[t, y, rows, :] = plain[t]
        return carry

    lax.fori_loop(0, heavy_out.shape[2] // PAIR, tile, 0)


def within(limits, at):
    def masked(image, offset):
        if abs(offset) <= ALWAYS:
            return image
        return jnp.where(limits[pl.ds(at + H + offset, ROWS), :] >= float(abs(offset)), image, 0.0)

    return masked


def add_outer(middle, heavy, plain, low, high, masks, limits):
    times, lines, cells, depth = middle.shape
    count = heavy[0].shape[2]

    for group in range(REACH // PAIR):

        def tile(index, carry, group=group):
            for side, shifted in ((0, low), (1, high)):

                @pl.when(index == side)
                def _():
                    first = cells - (group + 1) * PAIR if side else group * PAIR
                    number = first // count
                    base = pl.multiple_of(first - number * count + (index - side) * PAIR, PAIR)
                    origin = ROWS - cells if side else REACH
                    for y in range(lines):
                        for half, center in enumerate(tiles_of(middle, y, number * count + base)):
                            rows = pl.ds(base + half * ROWS, ROWS)
                            at = number * count + base + half * ROWS
                            rank = 2 * group + (1 - half if side else half)
                            sizes = range(ROWS // 2 * rank + 1, H + 1)
                            new_heavy, new_plain = accumulate(
                                center,
                                (
                                    [heavy[number][t, y, rows, :] for t in range(times)],
                                    [plain[number][t, y, rows, :] for t in range(times)],
                                ),
                                [size if side else -size for size in sizes],
                                lambda h: [shifted[t, y, pl.ds(at + origin + 2 * h, ROWS), :] for t in range(times)],
                                within(limits, at),
                                lambda h: masks[y, pl.ds(at + H + h, ROWS), :],
                            )
                            for t in range(times):
                                heavy[number][t, y, rows, :] = new_heavy[t]
                                plain[number][t, y, rows, :] = new_plain[t]

            return carry

        lax.fori_loop(0, 2, tile, 0)


def src_outer_kernel(limit, src, sat, even_in, odd_in, heavy_in, plain_in, heavy, plain, sums, low, high, masks, limits):
    times, lines, cells, depth = src.shape
    unpack_marks(times, limit, sat, even_in, odd_in, masks, limits)
    unpack_halo(even_in, odd_in, low, high)
    add_outer(src, [heavy], [plain], low, high, masks, limits)
    zero = jnp.zeros((ROWS, depth), jnp.float32)

    def add(index, totals):
        energy, weighted = totals
        base = pl.multiple_of(index * PAIR, PAIR)
        for y in range(lines):
            for half, center in enumerate(tiles_of(src, y, base)):
                rows = pl.ds(base + half * ROWS, ROWS)
                energy = energy + image_of(center, [plain[t, y, rows, :] for t in range(times)])
                weighted = weighted + image_of(center, [heavy[t, y, rows, :] for t in range(times)])
        return energy, weighted

    energy, weighted = lax.fori_loop(0, cells // PAIR, add, (zero, zero))
    sums[0:1, :] = jnp.full((1, depth), jnp.sum(energy), jnp.float32)
    sums[1:2, :] = jnp.full((1, depth), jnp.sum(weighted), jnp.float32)


def rcv_outer_kernel(limit, rcv, sat, even_marks, odd_marks, even_in, odd_in, *refs):
    parts, (low, high, masks, limits) = refs[len(refs) // 2 - 2 : -4], refs[-4:]
    unpack_marks(rcv.shape[0], limit, sat, even_marks, odd_marks, masks, limits)
    unpack_halo(even_in, odd_in, low, high)
    add_outer(rcv, parts[::2], parts[1::2], low, high, masks, limits)


def combine_kernel(cell_count, sums, src_heavy, src_plain, *refs):
    pieces, (src_out, rcv_out, semblance_out) = refs[:-3], refs[-3:]
    energy, weighted = sums[0:1, :], sums[1:2, :]
    semblance = weighted / energy
    inverse_rms = 1.0 / jnp.sqrt(energy / cell_count + EPSILON)
    semblance_out[...] = semblance

    def put(out, start, heavy, plain):
        times, lines, count, _ = heavy.shape
        for t in range(times):
            for y in range(lines):
                value = inverse_rms * (heavy[t, y] - semblance * plain[t, y])
                out[t, y, pl.ds(start, count), :] = value.astype(jnp.bfloat16)

    put(src_out, 0, src_heavy, src_plain)
    start = 0
    for heavy, plain in zip(pieces[::2], pieces[1::2]):
        put(rcv_out, start, heavy, plain)
        start += heavy.shape[2]


def exchanges(size, lines):
    assert size % 2 == 0 and lines % 2 == 0
    even = [(i, i + 1) for i in range(0, size, 2)]
    odd = [(i, i + 1) for i in range(1, size - 1, 2)]
    routes = []
    for pairs in (even, odd):
        partner = dict(pairs + [(j, i) for i, j in pairs])
        routes.append(
            [
                (i * lines + line, partner[i] * lines + line if i in partner else i * lines + (line ^ 1))
                for i in range(size)
                for line in range(lines)
            ]
        )
    return routes


def reduction_steps(count):
    assert count & (count - 1) == 0
    bits = [1 << bit for bit in range(1, count.bit_length() - 1)]
    groups = [[1]]
    for at in range(0, len(bits), 2):
        low, *high = bits[at : at + 2]
        groups.append([low | high[0], high[0], low] if high else [low])
    return [[[(i, i ^ (mask | 1)) for i in range(count)] for mask in group] for group in groups]


def local(source_field, receiver_field, sat_mask, offset_range):
    times, lines, cells, depth = source_field.shape
    size = lax.axis_size("inline")
    grant = pltpu.CompilerParams(vmem_limit_bytes=GRANT)
    image_cells = lines * cells * depth * (2 * H + 1)
    shape = jax.ShapeDtypeStruct
    total = shape((times, lines, cells, depth), jnp.float32)
    piece = shape((times, lines, cells // PIECES, depth), jnp.float32)
    field_out = shape(source_field.shape, jnp.bfloat16)
    extended = pltpu.VMEM((times, lines, cells + 2 * REACH, depth), jnp.float32)
    edge = pltpu.VMEM((times, lines, ROWS + REACH, depth), jnp.float32)
    masks = pltpu.VMEM((lines, cells + 2 * H, depth), jnp.float32)
    limits = pltpu.VMEM((cells + 2 * H, depth), jnp.float32)

    def call(kernel, name, out_shape, operands, scratch=(), share=0.0, aliases={}):
        return pl.pallas_call(
            kernel,
            out_shape=out_shape,
            in_specs=[SMEM if operand is offset_range else VMEM for operand in operands],
            out_specs=jax.tree.map(lambda _: VMEM, out_shape),
            scratch_shapes=scratch,
            input_output_aliases=aliases,
            cost_estimate=pl.CostEstimate(
                flops=int(24 * image_cells * share), bytes_accessed=1 << 20, transcendentals=0
            ),
            compiler_params=grant,
            name=name,
        )(*operands)

    src, rcv, sat = source_field, receiver_field, sat_mask
    even, odd = payloads(rcv, sat, offset_range)
    even_route, odd_route = exchanges(size, lax.axis_size("xline"))
    odd = lax.ppermute(odd, DEVICES, odd_route)
    even = lax.ppermute(even, DEVICES, even_route)
    heavy, plain = call(
        functools.partial(inner_kernel, 0),
        "src_inner",
        (total, total),
        (offset_range, src, rcv, sat),
        [extended, masks],
        0.85,
    )
    def piece_at(number, src, rcv):
        return call(
            functools.partial(inner_kernel, number * (cells // PIECES)),
            "rcv_inner",
            (piece, piece),
            (offset_range, rcv, src, sat),
            [extended, masks],
            0.85 / PIECES,
        )

    (heavy, plain), ahead = lax.optimization_barrier(((heavy, plain), rcv))
    pieces = list(piece_at(0, src, ahead))
    (heavy, plain), pieces = lax.optimization_barrier(((heavy, plain), pieces))
    pieces = list(pieces)
    heavy, plain, sums = call(
        src_outer_kernel,
        "src_outer",
        (total, total, shape((2, depth), jnp.float32)),
        (offset_range, src, sat, even, odd, heavy, plain),
        [edge, edge, masks, limits],
        0.25,
        {5: 0, 6: 1},
    )

    def late_rows(src):
        low_high = edges(src, 2, REACH)
        return (
            lax.ppermute(for_odd(*low_high), DEVICES, odd_route),
            lax.ppermute(for_even(*low_high), DEVICES, even_route),
        )

    def finish(odd_late, even_late, *pieces):
        return call(
            rcv_outer_kernel,
            "rcv_outer",
            [piece] * len(pieces),
            (offset_range, rcv, sat, even, odd, even_late, odd_late, *pieces),
            [edge, edge, masks, limits],
            0.25,
            {7 + i: i for i in range(len(pieces))},
        )

    steps = reduction_steps(size * lax.axis_size("xline"))
    assert len(steps) >= 3
    for number, routes in enumerate(steps):
        if number == len(steps) - 1:
            sums, late = lax.optimization_barrier((sums, late))
        sums, ahead = lax.optimization_barrier((sums, src))
        arrived = [lax.ppermute(sums, DEVICES, route) for route in routes]
        if number == 0:
            late = late_rows(ahead)
            result = ()
        elif number < len(steps) - 1:
            share = range(1 + (PIECES - 1) * (number - 1) // (len(steps) - 2), 1 + (PIECES - 1) * number // (len(steps) - 2))
            result = [part for i in share for part in piece_at(i, ahead, rcv)]
            pieces += result
        else:
            result = pieces = list(finish(*late, *pieces))
        if len(arrived) == 3:
            both, high, low = arrived
            sums = (sums + low) + (high + both)
        else:
            sums = sums + arrived[0]
        if number:
            sums, result = lax.optimization_barrier((sums, result))
            pieces[len(pieces) - len(result) :] = result

    cell_count = float(lines * lax.axis_size("xline") * cells * size * depth * (2 * H + 1))
    src_adj, rcv_adj, semblance = call(
        functools.partial(combine_kernel, cell_count),
        "combine",
        (field_out, field_out, shape((1, depth), jnp.float32)),
        (sums, heavy, plain, *pieces),
    )
    return src_adj, rcv_adj, semblance[0, 0]


def solution(mesh):
    return jax.shard_map(
        local,
        mesh=mesh,
        in_specs=(
            P(None, "xline", "inline", None),
            P(None, "xline", "inline", None),
            P("xline", "inline", None),
            P("inline"),
        ),
        out_specs=(P(None, "xline", "inline", None), P(None, "xline", "inline", None), P()),
        check_vma=False,
    )
```

profile of v0, /device:TPU:0, one launch (start us, length us, event | category | flops | bytes accessed | tf_op | source)
XLA Modules:
  0.0 29.2 jit_solution(15547244281655765674)
XLA Ops:
  1.3 0.9 %broadcast_select_fusion.2 = (bf16[4,1,64,128]{3,2,1,0:T(8,128)(2,1)S(1)}, bf16[4,1,64,128]{3,2,1,0:T(8,128)(2,1)S(1)}) fusion(pred[]{:T(512)S(6)} %eq.15, bf16[4,1,128,128]{3,2,1,0:T(8,128)(2,1)} %rcv.1), kind=kLoop, calls=%fused_computation.5 | loop fusion | flops 65536 | bytes 262145 | tf_op jit(solution)/shard_map/jit(_where)/select_n | solution.py:61
  2.3 0.1 pad.5.clone
  2.4 0.1 maximum_maximum_fusion.1
  2.5 0.5 %collective-permute-start.1 = (bf16[304,128]{1,0:T(8,128)(2,1)S(1)}, bf16[304,128]{1,0:T(8,128)(2,1)S(1)}, u32[]{:S(2)}, u32[]{:S(2)}) collective-permute-start(bf16[304,128]{1,0:T(8,128)(2,1)S(1)} %get-tuple-element.125), channel_id=1, source_target_pairs={{0,1},{1,0},{2,4},{3,5},{4,2},{5,3},{6,8},{7,9},{8,6},{9,7},{10,12... | collective-permute-start | bytes 233480 | tf_op jit(solution)/shard_map/ppermute | solution.py:366
  3.0 4.0 %collective-permute-start = (bf16[304,128]{1,0:T(8,128)(2,1)S(1)}, bf16[304,128]{1,0:T(8,128)(2,1)S(1)}, u32[]{:S(2)}, u32[]{:S(2)}) collective-permute-start(bf16[304,128]{1,0:T(8,128)(2,1)S(1)} %get-tuple-element.126), channel_id=1, source_target_pairs={{0,2},{1,3},{2,0},{3,1},{4,6},{5,7},{6,4},{7,5},{8,10},{9,11},{10,... | collective-permute-start | bytes 233480 | tf_op jit(solution)/shard_map/ppermute | solution.py:367
  7.0 3.1 %src_inner.1 = (f32[4,1,128,128]{3,2,1,0:T(8,128)S(1)}, f32[4,1,128,128]{3,2,1,0:T(8,128)S(1)}) custom-call(s32[1]{0:T(128)S(6)} %copy.27.limit, bf16[4,1,128,128]{3,2,1,0:T(8,128)(2,1)S(1)} %copy-done.1, bf16[4,1,128,128]{3,2,1,0:T(8,128)(2,1)S(1)} %copy-done, s32[1,128,128]{2,1,0:T(8,128)S(1)} %copy-done.2), custom_call_target="tpu_custom_call" | custom-call | flops 21725184 | bytes 1048576 | tf_op jit(solution)/shard_map/src_inner/pallas_call | solution.py:349
  10.1 0.7 %rcv_inner.4 = (f32[4,1,32,128]{3,2,1,0:T(8,128)S(1)}, f32[4,1,32,128]{3,2,1,0:T(8,128)S(1)}) custom-call(s32[1]{0:T(128)S(6)} %copy.27.limit, bf16[4,1,128,128]{3,2,1,0:T(8,128)(2,1)S(1)} %copy-done, bf16[4,1,128,128]{3,2,1,0:T(8,128)(2,1)S(1)} %copy-done.1, s32[1,128,128]{2,1,0:T(8,128)S(1)} %copy-done.2), custom_call_target="tpu_custom_call" | custom-call | flops 5431296 | bytes 1048576 | tf_op jit(solution)/shard_map/rcv_inner/pallas_call | solution.py:349
  10.8 0.0 collective-permute-done.1.odd_in.odd_marks
  10.9 1.6 %src_outer.1 = (f32[4,1,128,128]{3,2,1,0:T(8,128)S(1)}, f32[4,1,128,128]{3,2,1,0:T(8,128)S(1)}, f32[2,128]{1,0:T(2,128)S(1)}) custom-call(s32[1]{0:T(128)S(6)} %copy.27.limit, bf16[4,1,128,128]{3,2,1,0:T(8,128)(2,1)S(1)} %copy-done.1, s32[1,128,128]{2,1,0:T(8,128)S(1)} %copy-done.2, ...), custom_call_target="tpu_custom_call", output_to_operand_aliasing={{0}: (5, {}), {1}: (6, {})} | custom-call | flops 6389760 | bytes 1048576 | tf_op jit(solution)/shard_map/src_outer/pallas_call | solution.py:349
  12.5 0.1 collective-permute-start.2
  12.6 0.6 %collective-permute-start.6 = (bf16[256,128]{1,0:T(8,128)(2,1)S(1)}, bf16[256,128]{1,0:T(8,128)(2,1)S(1)}, u32[]{:S(2)}, u32[]{:S(2)}) collective-permute-start(bf16[256,128]{1,0:T(8,128)(2,1)S(1)} %bitcast.14), channel_id=1, source_target_pairs={{0,1},{1,0},{2,4},{3,5},{4,2},{5,3},{6,8},{7,9},{8,6},{9,7},{10,12... | collective-permute-start | bytes 196616 | tf_op jit(solution)/shard_map/ppermute | solution.py:403
  13.1 2.5 %collective-permute-start.7 = (bf16[256,128]{1,0:T(8,128)(2,1)S(1)}, bf16[256,128]{1,0:T(8,128)(2,1)S(1)}, u32[]{:S(2)}, u32[]{:S(2)}) collective-permute-start(bf16[256,128]{1,0:T(8,128)(2,1)S(1)} %bitcast.13), channel_id=1, source_target_pairs={{0,2},{1,3},{2,0},{3,1},{4,6},{5,7},{6,4},{7,5},{8,10},{9,11},{10,... | collective-permute-start | bytes 196616 | tf_op jit(solution)/shard_map/ppermute | solution.py:404
  15.6 1.0 %collective-permute-start.5 = (f32[2,128]{1,0:T(2,128)S(1)}, f32[2,128]{1,0:T(2,128)S(1)}, u32[]{:S(2)}, u32[]{:S(2)}) collective-permute-start(f32[2,128]{1,0:T(2,128)S(1)} %add.31), channel_id=1, source_target_pairs={{0,7},{1,6},{2,5},{3,4},{4,3},{5,2},{6,1},{7,0},{8,15},{9,14},{10,... | collective-permute-start | bytes 3080 | tf_op jit(solution)/shard_map/ppermute | solution.py:424
  16.7 0.2 collective-permute-start.4
  16.9 1.5 %collective-permute-start.3 = (f32[2,128]{1,0:T(2,128)S(1)}, f32[2,128]{1,0:T(2,128)S(1)}, u32[]{:S(2)}, u32[]{:S(2)}) collective-permute-start(f32[2,128]{1,0:T(2,128)S(1)} %add.31), channel_id=1, source_target_pairs={{0,3},{1,2},{2,1},{3,0},{4,7},{5,6},{6,5},{7,4},{8,11},{9,10},{10,... | collective-permute-start | bytes 3080 | tf_op jit(solution)/shard_map/ppermute | solution.py:424
  18.4 0.7 %rcv_inner.7 = (f32[4,1,32,128]{3,2,1,0:T(8,128)S(1)}, f32[4,1,32,128]{3,2,1,0:T(8,128)S(1)}) custom-call(s32[1]{0:T(128)S(6)} %copy.27.limit, bf16[4,1,128,128]{3,2,1,0:T(8,128)(2,1)S(1)} %copy-done, bf16[4,1,128,128]{3,2,1,0:T(8,128)(2,1)S(1)} %copy-done.1, s32[1,128,128]{2,1,0:T(8,128)S(1)} %copy-done.2), custom_call_target="tpu_custom_call" | custom-call | flops 5431296 | bytes 1048576 | tf_op jit(solution)/shard_map/rcv_inner/pallas_call | solution.py:349
  19.1 0.9 %rcv_inner.6 = (f32[4,1,32,128]{3,2,1,0:T(8,128)S(1)}, f32[4,1,32,128]{3,2,1,0:T(8,128)S(1)}) custom-call(s32[1]{0:T(128)S(6)} %copy.27.limit, bf16[4,1,128,128]{3,2,1,0:T(8,128)(2,1)S(1)} %copy-done, bf16[4,1,128,128]{3,2,1,0:T(8,128)(2,1)S(1)} %copy-done.1, s32[1,128,128]{2,1,0:T(8,128)S(1)} %copy-done.2), custom_call_target="tpu_custom_call" | custom-call | flops 5431296 | bytes 1048576 | tf_op jit(solution)/shard_map/rcv_inner/pallas_call | solution.py:349
  20.1 0.9 %rcv_inner.5 = (f32[4,1,32,128]{3,2,1,0:T(8,128)S(1)}, f32[4,1,32,128]{3,2,1,0:T(8,128)S(1)}) custom-call(s32[1]{0:T(128)S(6)} %copy.27.limit, bf16[4,1,128,128]{3,2,1,0:T(8,128)(2,1)S(1)} %copy-done, bf16[4,1,128,128]{3,2,1,0:T(8,128)(2,1)S(1)} %copy-done.1, s32[1,128,128]{2,1,0:T(8,128)S(1)} %copy-done.2), custom_call_target="tpu_custom_call" | custom-call | flops 5431296 | bytes 1048576 | tf_op jit(solution)/shard_map/rcv_inner/pallas_call | solution.py:349
  21.0 0.0 collective-permute-done.5
  21.0 3.5 %collective-permute-start.10 = (f32[2,128]{1,0:T(2,128)S(1)}, f32[2,128]{1,0:T(2,128)S(1)}, u32[]{:S(2)}, u32[]{:S(2)}) collective-permute-start(f32[2,128]{1,0:T(2,128)S(1)} %add_add_fusion.1), channel_id=1, source_target_pairs={{0,25},{1,24},{2,27},{3,26},{4,29},{5,28},{6,31},{7,30},{8,17},{9,... | collective-permute-start | bytes 3080 | tf_op jit(solution)/shard_map/ppermute | solution.py:424
  24.6 0.8 %collective-permute-start.8 = (f32[2,128]{1,0:T(2,128)S(1)}, f32[2,128]{1,0:T(2,128)S(1)}, u32[]{:S(2)}, u32[]{:S(2)}) collective-permute-start(f32[2,128]{1,0:T(2,128)S(1)} %add_add_fusion.1), channel_id=1, source_target_pairs={{0,9},{1,8},{2,11},{3,10},{4,13},{5,12},{6,15},{7,14},{8,1},{9,0},... | collective-permute-start | bytes 3080 | tf_op jit(solution)/shard_map/ppermute | solution.py:424
  25.4 1.4 %rcv_outer.1 = (f32[4,1,32,128]{3,2,1,0:T(8,128)S(1)}, f32[4,1,32,128]{3,2,1,0:T(8,128)S(1)}, f32[4,1,32,128]{3,2,1,0:T(8,128)S(1)}, f32[4,1,32,128]{3,2,1,0:T(8...) custom-call(s32[1]{0:T(128)S(6)} %copy.27.limit, ...), custom_call_target="tpu_custom_call", output_to_operand_aliasing={{0}: (7, {}), {1}: (8, {}), {2}: (9, {}), {3}: (10, {}), {4... | custom-call | flops 6389760 | bytes 1048576 | tf_op jit(solution)/shard_map/rcv_outer/pallas_call | solution.py:349
  26.7 1.7 %collective-permute-done.9 = f32[2,128]{1,0:T(2,128)S(1)} collective-permute-done((f32[2,128]{1,0:T(2,128)S(1)}, f32[2,128]{1,0:T(2,128)S(1)}, u32[]{:S(2)}, u32[]{:S(2)}) %collective-permute-start.9) | collective-permute-done | bytes 1056 | tf_op jit(solution)/shard_map/ppermute | solution.py:424
  28.5 0.8 %combine.1 = (bf16[4,1,128,128]{3,2,1,0:T(8,128)(2,1)}, bf16[4,1,128,128]{3,2,1,0:T(8,128)(2,1)}, f32[1,128]{1,0:T(1,128)}) custom-call(f32[2,128]{1,0:T(2,128)S(1)} %add_add_fusion.sums, f32[4,1,128,128]{3,2,1,0:T(8,128)S(1)} %get-tuple-element.106.src_heavy, f32[4,1,128,128]{3,2,1,0:T(8,128)S(1)} %get-tuple-element.107.src_plain, ...), custom_call_target="tpu_custom_call" | custom-call | bytes 1048576 | tf_op jit(solution)/shard_map/combine/pallas_call | solution.py:349
  (22 shorter events, 0.1 us)
Async XLA Ops:
  1.3 0.9 %copy-start.2 = (s32[1,128,128]{2,1,0:T(8,128)S(1)}, s32[1,128,128]{2,1,0:T(8,128)}, u32[]{:S(2)}) copy-start(s32[1,128,128]{2,1,0:T(8,128)} %sat.13) | copy-start | bytes 196612
  2.4 4.6 %copy-start = (bf16[4,1,128,128]{3,2,1,0:T(8,128)(2,1)S(1)}, bf16[4,1,128,128]{3,2,1,0:T(8,128)(2,1)}, u32[]{:S(2)}) copy-start(bf16[4,1,128,128]{3,2,1,0:T(8,128)(2,1)} %rcv.1) | copy-start | bytes 393220
  2.4 4.6 %copy-start.1 = (bf16[4,1,128,128]{3,2,1,0:T(8,128)(2,1)S(1)}, bf16[4,1,128,128]{3,2,1,0:T(8,128)(2,1)}, u32[]{:S(2)}) copy-start(bf16[4,1,128,128]{3,2,1,0:T(8,128)(2,1)} %field.6) | copy-start | bytes 393220
  2.5 8.4 %collective-permute-start.1 = (bf16[304,128]{1,0:T(8,128)(2,1)S(1)}, bf16[304,128]{1,0:T(8,128)(2,1)S(1)}, u32[]{:S(2)}, u32[]{:S(2)}) collective-permute-start(bf16[304,128]{1,0:T(8,128)(2,1)S(1)} %get-tuple-element.125), channel_id=1, source_target_pairs={{0,1},{1,0},{2,4},{3,5},{4,2},{5,3},{6,8},{7,9},{8,6},{9,7},{10,12... | collective-permute-start | bytes 233480 | tf_op jit(solution)/shard_map/ppermute | solution.py:366
  3.0 7.9 %collective-permute-start = (bf16[304,128]{1,0:T(8,128)(2,1)S(1)}, bf16[304,128]{1,0:T(8,128)(2,1)S(1)}, u32[]{:S(2)}, u32[]{:S(2)}) collective-permute-start(bf16[304,128]{1,0:T(8,128)(2,1)S(1)} %get-tuple-element.126), channel_id=1, source_target_pairs={{0,2},{1,3},{2,0},{3,1},{4,6},{5,7},{6,4},{7,5},{8,10},{9,11},{10,... | collective-permute-start | bytes 233480 | tf_op jit(solution)/shard_map/ppermute | solution.py:367
  12.5 3.2 %collective-permute-start.2 = (f32[2,128]{1,0:T(2,128)S(1)}, f32[2,128]{1,0:T(2,128)S(1)}, u32[]{:S(2)}, u32[]{:S(2)}) collective-permute-start(f32[2,128]{1,0:T(2,128)S(1)} %get-tuple-element.74), channel_id=1, source_target_pairs={{0,1},{1,0},{2,3},{3,2},{4,5},{5,4},{6,7},{7,6},{8,9},{9,8},{10,11... | collective-permute-start | bytes 3080 | tf_op jit(solution)/shard_map/ppermute | solution.py:424
  12.6 8.5 %collective-permute-start.6 = (bf16[256,128]{1,0:T(8,128)(2,1)S(1)}, bf16[256,128]{1,0:T(8,128)(2,1)S(1)}, u32[]{:S(2)}, u32[]{:S(2)}) collective-permute-start(bf16[256,128]{1,0:T(8,128)(2,1)S(1)} %bitcast.14), channel_id=1, source_target_pairs={{0,1},{1,0},{2,4},{3,5},{4,2},{5,3},{6,8},{7,9},{8,6},{9,7},{10,12... | collective-permute-start | bytes 196616 | tf_op jit(solution)/shard_map/ppermute | solution.py:403
  13.1 7.9 %collective-permute-start.7 = (bf16[256,128]{1,0:T(8,128)(2,1)S(1)}, bf16[256,128]{1,0:T(8,128)(2,1)S(1)}, u32[]{:S(2)}, u32[]{:S(2)}) collective-permute-start(bf16[256,128]{1,0:T(8,128)(2,1)S(1)} %bitcast.13), channel_id=1, source_target_pairs={{0,2},{1,3},{2,0},{3,1},{4,6},{5,7},{6,4},{7,5},{8,10},{9,11},{10,... | collective-permute-start | bytes 196616 | tf_op jit(solution)/shard_map/ppermute | solution.py:404
  15.6 5.4 %collective-permute-start.5 = (f32[2,128]{1,0:T(2,128)S(1)}, f32[2,128]{1,0:T(2,128)S(1)}, u32[]{:S(2)}, u32[]{:S(2)}) collective-permute-start(f32[2,128]{1,0:T(2,128)S(1)} %add.31), channel_id=1, source_target_pairs={{0,7},{1,6},{2,5},{3,4},{4,3},{5,2},{6,1},{7,0},{8,15},{9,14},{10,... | collective-permute-start | bytes 3080 | tf_op jit(solution)/shard_map/ppermute | solution.py:424
  16.7 4.3 %collective-permute-start.4 = (f32[2,128]{1,0:T(2,128)S(1)}, f32[2,128]{1,0:T(2,128)S(1)}, u32[]{:S(2)}, u32[]{:S(2)}) collective-permute-start(f32[2,128]{1,0:T(2,128)S(1)} %add.31), channel_id=1, source_target_pairs={{0,5},{1,4},{2,7},{3,6},{4,1},{5,0},{6,3},{7,2},{8,13},{9,12},{10,... | collective-permute-start | bytes 3080 | tf_op jit(solution)/shard_map/ppermute | solution.py:424
  16.9 4.1 %collective-permute-start.3 = (f32[2,128]{1,0:T(2,128)S(1)}, f32[2,128]{1,0:T(2,128)S(1)}, u32[]{:S(2)}, u32[]{:S(2)}) collective-permute-start(f32[2,128]{1,0:T(2,128)S(1)} %add.31), channel_id=1, source_target_pairs={{0,3},{1,2},{2,1},{3,0},{4,7},{5,6},{6,5},{7,4},{8,11},{9,10},{10,... | collective-permute-start | bytes 3080 | tf_op jit(solution)/shard_map/ppermute | solution.py:424
  21.0 5.7 %collective-permute-start.10 = (f32[2,128]{1,0:T(2,128)S(1)}, f32[2,128]{1,0:T(2,128)S(1)}, u32[]{:S(2)}, u32[]{:S(2)}) collective-permute-start(f32[2,128]{1,0:T(2,128)S(1)} %add_add_fusion.1), channel_id=1, source_target_pairs={{0,25},{1,24},{2,27},{3,26},{4,29},{5,28},{6,31},{7,30},{8,17},{9,... | collective-permute-start | bytes 3080 | tf_op jit(solution)/shard_map/ppermute | solution.py:424
  24.6 3.9 %collective-permute-start.9 = (f32[2,128]{1,0:T(2,128)S(1)}, f32[2,128]{1,0:T(2,128)S(1)}, u32[]{:S(2)}, u32[]{:S(2)}) collective-permute-start(f32[2,128]{1,0:T(2,128)S(1)} %add_add_fusion.1), channel_id=1, source_target_pairs={{0,17},{1,16},{2,19},{3,18},{4,21},{5,20},{6,23},{7,22},{8,25},{9,... | collective-permute-start | bytes 3080 | tf_op jit(solution)/shard_map/ppermute | solution.py:424
  24.6 3.9 %collective-permute-start.8 = (f32[2,128]{1,0:T(2,128)S(1)}, f32[2,128]{1,0:T(2,128)S(1)}, u32[]{:S(2)}, u32[]{:S(2)}) collective-permute-start(f32[2,128]{1,0:T(2,128)S(1)} %add_add_fusion.1), channel_id=1, source_target_pairs={{0,9},{1,8},{2,11},{3,10},{4,13},{5,12},{6,15},{7,14},{8,1},{9,0},... | collective-permute-start | bytes 3080 | tf_op jit(solution)/shard_map/ppermute | solution.py:424
where the time goes:
time: 29.4 us; the launch traced here: 29.2 us
  starting transfers between devices  14.7 us (50%)
  Pallas kernels  10.1 us (34%)
  waiting for transfers between devices  1.75 us (6%)
  between operations  1.49 us (5%)
  other arithmetic  1.08 us (4%)
    pallas_call x8, Pallas kernels, call(): pl.pallas_call(kernel, out_shape=out_shape, in_specs=[SMEM if operand is...  10.1 us
    ppermute x7, starting transfers between devices, local(): arrived = [lax.ppermute(sums, DEVICES, route) for route in routes]  7.17 us
    ppermute x1, starting transfers between devices, local(): even = lax.ppermute(even, DEVICES, even_route)  3.98 us
    ppermute x1, starting transfers between devices, late_rows(): lax.ppermute(for_even(*low_high), DEVICES, even_route)  2.49 us
    ppermute x7, waiting for transfers between devices, local(): arrived = [lax.ppermute(sums, DEVICES, route) for route in routes]  1.74 us
    select_n x3, other arithmetic, for_even(): return jnp.where(lax.axis_index('inline') % 2 == 0, high, low)  0.95 us
  transfers between devices with their start and end apart: 11, of which 1 were waited for; matrix products, arithmetic and copies ran while one was open for 0% of the time, Pallas kernels for 27%

commit v1 on v0

--- a/solution.py
+++ b/solution.py
@@ -72,9 +72,9 @@
     *rows, sat = lax.optimization_barrier((*rows, sat))
     masks = edges((sat != 0).astype(jnp.bfloat16), 1, H)
     limits = jnp.full((LIMIT_ROWS, depth), limit[0]).astype(jnp.bfloat16)
-    return [
-        jnp.concatenate([part, choose(*masks), limits], axis=0) for part, choose in zip(rows, (for_even, for_odd))
-    ]
+    even = jnp.concatenate([rows[0], for_even(*masks), limits], axis=0)
+    even, odd_rows = lax.optimization_barrier((even, rows[1]))
+    return even, jnp.concatenate([odd_rows, for_odd(*masks), limits], axis=0)
 
 
 def unpack_marks(times, limit, sat, even_in, odd_in, masks, limits):
@@ -184,16 +184,20 @@
                         lambda h: masks[y, pl.ds(at + H + h, ROWS), :],
                     )
 
-                sums = add(paired(SHARED), ([zero] * times, [zero] * times))
-                for low in range(SHARED + 1, H + 1, GROUP):
-                    sizes = range(low, min(low + GROUP, H + 1))
-                    reaches = (
-                        first + base + PAIR - 1 - 2 * low >= 0,
-                        first + base + 2 * low < cells,
-                    )
-                    for sign, reach in zip((-1, 1), reaches):
-                        offsets = [sign * size for size in sizes]
-                        sums = lax.cond(reach, functools.partial(add, offsets), lambda kept: kept, sums)
+                sums = add(paired(ALWAYS), ([zero] * times, [zero] * times))
+                for low in range(ALWAYS + 1, H + 1, GROUP):
+                    high = min(low + GROUP - 1, H)
+                    if high <= SHARED:
+                        parts = [(paired(high, low), limit[0] >= low)]
+                    else:
+                        below = first + base + PAIR - 1 - 2 * low >= 0
+                        above = first + base + 2 * low < cells
+                        parts = [
+                            ([sign * size for size in range(low, high + 1)], jnp.logical_and(reach, limit[0] >= low))
+                            for sign, reach in ((-1, below), (1, above))
+                        ]
+                    for offsets, needed in parts:
+                        sums = lax.cond(needed, functools.partial(add, offsets), lambda kept: kept, sums)
                 heavy, plain = sums
                 rows = pl.ds(base + half * ROWS, ROWS)
                 for t in range(times):
@@ -216,6 +220,10 @@
 def add_outer(middle, heavy, plain, low, high, masks, limits):
     times, lines, cells, depth = middle.shape
     count = heavy[0].shape[2]
+    widest = [
+        jnp.max(jnp.maximum(limits[pl.ds(H if side else 0, ROWS), :], limits[pl.ds(H + cells * side, ROWS), :]))
+        for side in range(2)
+    ]
 
     for group in range(REACH // PAIR):
 
@@ -233,18 +241,32 @@
                             rows = pl.ds(base + half * ROWS, ROWS)
                             at = number * count + base + half * ROWS
                             rank = 2 * group + (1 - half if side else half)
-                            sizes = range(ROWS // 2 * rank + 1, H + 1)
-                            new_heavy, new_plain = accumulate(
-                                center,
-                                (
-                                    [heavy[number][t, y, rows, :] for t in range(times)],
-                                    [plain[number][t, y, rows, :] for t in range(times)],
-                                ),
-                                [size if side else -size for size in sizes],
-                                lambda h: [shifted[t, y, pl.ds(at + origin + 2 * h, ROWS), :] for t in range(times)],
-                                within(limits, at),
-                                lambda h: masks[y, pl.ds(at + H + h, ROWS), :],
+                            nearest = ROWS // 2 * rank + 1
+
+                            def add(offsets, sums):
+                                return accumulate(
+                                    center,
+                                    sums,
+                                    offsets,
+                                    lambda h: [shifted[t, y, pl.ds(at + origin + 2 * h, ROWS), :] for t in range(times)],
+                                    within(limits, at),
+                                    lambda h: masks[y, pl.ds(at + H + h, ROWS), :],
+                                )
+
+                            sums = (
+                                [heavy[number][t, y, rows, :] for t in range(times)],
+                                [plain[number][t, y, rows, :] for t in range(times)],
                             )
+                            for low in range(1, H + 1, GROUP):
+                                sizes = range(max(low, nearest), min(low + GROUP, H + 1))
+                                if sizes:
+                                    sums = lax.cond(
+                                        widest[side] >= float(sizes[0]),
+                                        functools.partial(add, [size if side else -size for size in sizes]),
+                                        lambda kept: kept,
+                                        sums,
+                                    )
+                            new_heavy, new_plain = sums
                             for t in range(times):
                                 heavy[number][t, y, rows, :] = new_heavy[t]
                                 plain[number][t, y, rows, :] = new_plain[t]
@@ -302,6 +324,25 @@
     for heavy, plain in zip(pieces[::2], pieces[1::2]):
         put(rcv_out, start, heavy, plain)
         start += heavy.shape[2]
+
+
+def ride_kernel(rows_in, sums, rows):
+    count = sums.shape[0]
+    parts, rest = [], sums[...]
+    for _ in range(3):
+        parts.append(rest.astype(jnp.bfloat16).astype(jnp.float32))
+        rest = rest - parts[-1]
+    parts.append(jnp.zeros((LIMIT_ROWS - 3 * count, sums.shape[1]), jnp.float32))
+    below = pl.ds(rows.shape[0] - LIMIT_ROWS, LIMIT_ROWS)
+    rows[below, :] = jnp.concatenate(parts, axis=0).astype(jnp.bfloat16)
+
+
+def sums_below(rows, count):
+    at = rows.shape[0] - LIMIT_ROWS
+    first, second, third = (
+        lax.slice_in_dim(rows, at + i * count, at + (i + 1) * count).astype(jnp.float32) for i in range(3)
+    )
+    return first + second + third
 
 
 def exchanges(size, lines):
@@ -327,8 +368,8 @@
     groups = [[1]]
     for at in range(0, len(bits), 2):
         low, *high = bits[at : at + 2]
-        groups.append([low | high[0], high[0], low] if high else [low])
-    return [[[(i, i ^ (mask | 1)) for i in range(count)] for mask in group] for group in groups]
+        groups.append([low, high[0], low | high[0]] if high else [low])
+    return groups
 
 
 def local(source_field, receiver_field, sat_mask, offset_range):
@@ -363,8 +404,8 @@
     src, rcv, sat = source_field, receiver_field, sat_mask
     even, odd = payloads(rcv, sat, offset_range)
     even_route, odd_route = exchanges(size, lax.axis_size("xline"))
+    even = lax.ppermute(even, DEVICES, even_route)
     odd = lax.ppermute(odd, DEVICES, odd_route)
-    even = lax.ppermute(even, DEVICES, even_route)
     heavy, plain = call(
         functools.partial(inner_kernel, 0),
         "src_inner",
@@ -397,13 +438,6 @@
         {5: 0, 6: 1},
     )
 
-    def late_rows(src):
-        low_high = edges(src, 2, REACH)
-        return (
-            lax.ppermute(for_odd(*low_high), DEVICES, odd_route),
-            lax.ppermute(for_even(*low_high), DEVICES, even_route),
-        )
-
     def finish(odd_late, even_late, *pieces):
         return call(
             rcv_outer_kernel,
@@ -415,30 +449,46 @@
             {7 + i: i for i in range(len(pieces))},
         )
 
-    steps = reduction_steps(size * lax.axis_size("xline"))
-    assert len(steps) >= 3
-    for number, routes in enumerate(steps):
-        if number == len(steps) - 1:
-            sums, late = lax.optimization_barrier((sums, late))
+    lines_all = lax.axis_size("xline")
+    steps = reduction_steps(size * lines_all)
+    assert len(steps) >= 3 and not any(lines_all in group for group in (steps[0], steps[-1]))
+    low_high = edges(src, 2, REACH)
+    ride = jnp.concatenate([for_even(*low_high), jnp.zeros((LIMIT_ROWS, depth), jnp.bfloat16)], axis=0)
+    for number, group in enumerate(steps):
+        last = number == len(steps) - 1
+        if last:
+            sums, *late = lax.optimization_barrier((sums, odd_late, even_late))
         sums, ahead = lax.optimization_barrier((sums, src))
-        arrived = [lax.ppermute(sums, DEVICES, route) for route in routes]
+        arrived = []
+        for changed in group:
+            if changed == lines_all:
+                ride = call(
+                    ride_kernel,
+                    "ride",
+                    shape(ride.shape, ride.dtype),
+                    (ride, sums),
+                    aliases={0: 0},
+                )
+                even_late = lax.ppermute(ride, DEVICES, even_route)
+                arrived.append(sums_below(even_late, sums.shape[0]))
+            else:
+                route = [(i, i ^ (changed | 1)) for i in range(size * lines_all)]
+                arrived.append(lax.ppermute(sums, DEVICES, route))
         if number == 0:
-            late = late_rows(ahead)
-            result = ()
-        elif number < len(steps) - 1:
-            share = range(1 + (PIECES - 1) * (number - 1) // (len(steps) - 2), 1 + (PIECES - 1) * number // (len(steps) - 2))
+            odd_late = lax.ppermute(for_odd(*edges(ahead, 2, REACH)), DEVICES, odd_route)
+        if not last:
+            share = range(1 + (PIECES - 1) * number // (len(steps) - 1), 1 + (PIECES - 1) * (number + 1) // (len(steps) - 1))
             result = [part for i in share for part in piece_at(i, ahead, rcv)]
             pieces += result
         else:
             result = pieces = list(finish(*late, *pieces))
         if len(arrived) == 3:
-            both, high, low = arrived
+            low, high, both = arrived
             sums = (sums + low) + (high + both)
         else:
             sums = sums + arrived[0]
-        if number:
-            sums, result = lax.optimization_barrier((sums, result))
-            pieces[len(pieces) - len(result) :] = result
+        sums, result = lax.optimization_barrier((sums, result))
+        pieces[len(pieces) - len(result) :] = result
 
     cell_count = float(lines * lax.axis_size("xline") * cells * size * depth * (2 * H + 1))
     src_adj, rcv_adj, semblance = call(

time: 29.4 us -> 29.7 us (1.010)
  waiting for transfers between devices: 1.75 us -> 3.17 us
  Pallas kernels: 10.1 us -> 8.79 us
    pallas_call x8 -> x9, Pallas kernels: 10.1 us -> 8.79 us  [call(): pl.pallas_call(kernel, out_shape=out_shape, in_specs=[SMEM if operand is...]
    ppermute x9 -> x8, waiting for transfers between devices: 1.74 us -> 2.85 us  [the longest x6 2.85 us: local(): arrived.append(lax.ppermute(sums, DEVICES, route))]
    ppermute x1, waiting for transfers between devices: 0.01 us -> 0.32 us  [local(): even = lax.ppermute(even, DEVICES, even_route)]
    ppermute x9 -> x8, starting transfers between devices: 10.2 us -> 10 us  [the longest x6 8.16 us: local(): arrived.append(lax.ppermute(sums, DEVICES, route))]
    select_n x3 -> x4, other arithmetic: 0.95 us -> 0.95 us  [for_even(): return jnp.where(lax.axis_index('inline') % 2 == 0, high, low)]
  transfers between devices with their start and end apart: 11 -> 10, of which waited for: 1 -> 4; matrix products, arithmetic and copies ran while one was open for 0% -> 0% of each run, Pallas kernels for 27% -> 23%
where the time goes in v1:
time: 29.7 us; the launch traced here: 29.3 us
  starting transfers between devices  14.5 us (49%)
  Pallas kernels  8.79 us (30%)
  waiting for transfers between devices  3.17 us (11%)
  between operations  1.48 us (5%)
  other arithmetic  1.19 us (4%)
    pallas_call x9, Pallas kernels, call(): pl.pallas_call(kernel, out_shape=out_shape, in_specs=[SMEM if operand is...  8.79 us
    ppermute x6, starting transfers between devices, local(): arrived.append(lax.ppermute(sums, DEVICES, route))  8.16 us
    ppermute x1, starting transfers between devices, local(): even = lax.ppermute(even, DEVICES, even_route)  3.98 us
    ppermute x6, waiting for transfers between devices, local(): arrived.append(lax.ppermute(sums, DEVICES, route))  2.85 us
    ppermute x1, starting transfers between devices, local(): even_late = lax.ppermute(ride, DEVICES, even_route)  1.81 us
    select_n x4, other arithmetic, for_even(): return jnp.where(lax.axis_index('inline') % 2 == 0, high, low)  0.95 us
  transfers between devices with their start and end apart: 10, of which 4 were waited for; matrix products, arithmetic and copies ran while one was open for 0% of the time, Pallas kernels for 23%

profile of v1, /device:TPU:0, one launch (start us, length us, event | category | flops | bytes accessed | tf_op | source)
XLA Modules:
  0.0 29.3 jit_solution(2016897298953837140)
XLA Ops:
  1.3 0.9 %broadcast_select_fusion = (bf16[4,1,64,128]{3,2,1,0:T(8,128)(2,1)S(1)}, bf16[4,1,64,128]{3,2,1,0:T(8,128)(2,1)S(1)}) fusion(pred[]{:T(512)S(6)} %eq.15, bf16[4,1,128,128]{3,2,1,0:T(8,128)(2,1)} %rcv.1), kind=kLoop, calls=%fused_computation.5 | loop fusion | flops 65536 | bytes 262145 | tf_op jit(solution)/shard_map/jit(_where)/select_n | solution.py:61
  2.3 0.1 pad.6.clone
  2.4 0.1 maximum_maximum_fusion
  2.5 0.1 maximum_maximum_fusion.1
  2.6 0.5 %collective-permute-start.1 = (bf16[304,128]{1,0:T(8,128)(2,1)S(1)}, bf16[304,128]{1,0:T(8,128)(2,1)S(1)}, u32[]{:S(2)}, u32[]{:S(2)}) collective-permute-start(bf16[304,128]{1,0:T(8,128)(2,1)S(1)} %maximum_maximum_fusion.1), channel_id=1, source_target_pairs={{0,1},{1,0},{2,4},{3,5},{4,2},{5,3},{6,8},{7,9},{8,6},{9,7},{10,12... | collective-permute-start | bytes 233480 | tf_op jit(solution)/shard_map/ppermute | solution.py:408
  3.1 4.0 %collective-permute-start = (bf16[304,128]{1,0:T(8,128)(2,1)S(1)}, bf16[304,128]{1,0:T(8,128)(2,1)S(1)}, u32[]{:S(2)}, u32[]{:S(2)}) collective-permute-start(bf16[304,128]{1,0:T(8,128)(2,1)S(1)} %maximum_maximum_fusion), channel_id=1, source_target_pairs={{0,2},{1,3},{2,0},{3,1},{4,6},{5,7},{6,4},{7,5},{8,10},{9,11},{10,... | collective-permute-start | bytes 233480 | tf_op jit(solution)/shard_map/ppermute | solution.py:407
  7.1 2.7 %src_inner.1 = (f32[4,1,128,128]{3,2,1,0:T(8,128)S(1)}, f32[4,1,128,128]{3,2,1,0:T(8,128)S(1)}) custom-call(s32[1]{0:T(128)S(6)} %copy.29.limit, bf16[4,1,128,128]{3,2,1,0:T(8,128)(2,1)S(1)} %copy-done, bf16[4,1,128,128]{3,2,1,0:T(8,128)(2,1)S(1)} %copy-done.1, s32[1,128,128]{2,1,0:T(8,128)S(1)} %copy-done.2), custom_call_target="tpu_custom_call" | custom-call | flops 21725184 | bytes 1048576 | tf_op jit(solution)/shard_map/src_inner/pallas_call | solution.py:390
  9.8 0.7 %rcv_inner.4 = (f32[4,1,32,128]{3,2,1,0:T(8,128)S(1)}, f32[4,1,32,128]{3,2,1,0:T(8,128)S(1)}) custom-call(s32[1]{0:T(128)S(6)} %copy.29.limit, bf16[4,1,128,128]{3,2,1,0:T(8,128)(2,1)S(1)} %copy-done.1, bf16[4,1,128,128]{3,2,1,0:T(8,128)(2,1)S(1)} %copy-done, s32[1,128,128]{2,1,0:T(8,128)S(1)} %copy-done.2), custom_call_target="tpu_custom_call" | custom-call | flops 5431296 | bytes 1048576 | tf_op jit(solution)/shard_map/rcv_inner/pallas_call | solution.py:390
  10.5 0.3 %collective-permute-done.even_in.even_marks = bf16[304,128]{1,0:T(8,128)(2,1)S(1)} collective-permute-done((bf16[304,128]{1,0:T(8,128)(2,1)S(1)}, bf16[304,128]{1,0:T(8,128)(2,1)S(1)}, u32[]{:S(2)}, u32[]{:S(2)}) %collective-permute-start) | collective-permute-done | bytes 77856 | tf_op jit(solution)/shard_map/ppermute | solution.py:407
  10.8 1.3 %src_outer.1 = (f32[4,1,128,128]{3,2,1,0:T(8,128)S(1)}, f32[4,1,128,128]{3,2,1,0:T(8,128)S(1)}, f32[2,128]{1,0:T(2,128)S(1)}) custom-call(s32[1]{0:T(128)S(6)} %copy.29.limit, bf16[4,1,128,128]{3,2,1,0:T(8,128)(2,1)S(1)} %copy-done, s32[1,128,128]{2,1,0:T(8,128)S(1)} %copy-done.2, ...), custom_call_target="tpu_custom_call", output_to_operand_aliasing={{0}: (5, {}), {1}: (6, {})} | custom-call | flops 6389760 | bytes 1048576 | tf_op jit(solution)/shard_map/src_outer/pallas_call | solution.py:390
  12.3 0.8 %rcv_inner.5 = (f32[4,1,32,128]{3,2,1,0:T(8,128)S(1)}, f32[4,1,32,128]{3,2,1,0:T(8,128)S(1)}) custom-call(s32[1]{0:T(128)S(6)} %copy.29.limit, bf16[4,1,128,128]{3,2,1,0:T(8,128)(2,1)S(1)} %copy-done.1, bf16[4,1,128,128]{3,2,1,0:T(8,128)(2,1)S(1)} %copy-done, s32[1,128,128]{2,1,0:T(8,128)S(1)} %copy-done.2), custom_call_target="tpu_custom_call" | custom-call | flops 5431296 | bytes 1048576 | tf_op jit(solution)/shard_map/rcv_inner/pallas_call | solution.py:390
  13.0 0.3 %collective-permute-done.2 = f32[2,128]{1,0:T(2,128)S(1)} collective-permute-done((f32[2,128]{1,0:T(2,128)S(1)}, f32[2,128]{1,0:T(2,128)S(1)}, u32[]{:S(2)}, u32[]{:S(2)}) %collective-permute-start.2) | collective-permute-done | bytes 1056 | tf_op jit(solution)/shard_map/ppermute | solution.py:476
  13.4 1.8 %collective-permute-start.3 = (bf16[272,128]{1,0:T(8,128)(2,1)S(1)}, bf16[272,128]{1,0:T(8,128)(2,1)S(1)}, u32[]{:S(2)}, u32[]{:S(2)}) collective-permute-start(bf16[272,128]{1,0:T(8,128)(2,1)S(1)} %ride.1), channel_id=1, source_target_pairs={{0,2},{1,3},{2,0},{3,1},{4,6},{5,7},{6,4},{7,5},{8,10},{9,11},{10,... | collective-permute-start | bytes 208904 | tf_op jit(solution)/shard_map/ppermute | solution.py:472
  15.2 0.1 collective-permute-start.6
  15.3 3.0 %collective-permute-start.5 = (f32[2,128]{1,0:T(2,128)S(1)}, f32[2,128]{1,0:T(2,128)S(1)}, u32[]{:S(2)}, u32[]{:S(2)}) collective-permute-start(f32[2,128]{1,0:T(2,128)S(1)} %add.39.sums), channel_id=1, source_target_pairs={{0,7},{1,6},{2,5},{3,4},{4,3},{5,2},{6,1},{7,0},{8,15},{9,14},{10,... | collective-permute-start | bytes 3080 | tf_op jit(solution)/shard_map/ppermute | solution.py:476
  18.3 0.4 %collective-permute-start.4 = (f32[2,128]{1,0:T(2,128)S(1)}, f32[2,128]{1,0:T(2,128)S(1)}, u32[]{:S(2)}, u32[]{:S(2)}) collective-permute-start(f32[2,128]{1,0:T(2,128)S(1)} %add.39.sums), channel_id=1, source_target_pairs={{0,5},{1,4},{2,7},{3,6},{4,1},{5,0},{6,3},{7,2},{8,13},{9,12},{10,... | collective-permute-start | bytes 3080 | tf_op jit(solution)/shard_map/ppermute | solution.py:476
  18.7 0.7 %rcv_inner.7 = (f32[4,1,32,128]{3,2,1,0:T(8,128)S(1)}, f32[4,1,32,128]{3,2,1,0:T(8,128)S(1)}) custom-call(s32[1]{0:T(128)S(6)} %copy.29.limit, bf16[4,1,128,128]{3,2,1,0:T(8,128)(2,1)S(1)} %copy-done.1, bf16[4,1,128,128]{3,2,1,0:T(8,128)(2,1)S(1)} %copy-done, s32[1,128,128]{2,1,0:T(8,128)S(1)} %copy-done.2), custom_call_target="tpu_custom_call" | custom-call | flops 5431296 | bytes 1048576 | tf_op jit(solution)/shard_map/rcv_inner/pallas_call | solution.py:390
  19.4 0.8 %rcv_inner.6 = (f32[4,1,32,128]{3,2,1,0:T(8,128)S(1)}, f32[4,1,32,128]{3,2,1,0:T(8,128)S(1)}) custom-call(s32[1]{0:T(128)S(6)} %copy.29.limit, bf16[4,1,128,128]{3,2,1,0:T(8,128)(2,1)S(1)} %copy-done.1, bf16[4,1,128,128]{3,2,1,0:T(8,128)(2,1)S(1)} %copy-done, s32[1,128,128]{2,1,0:T(8,128)S(1)} %copy-done.2), custom_call_target="tpu_custom_call" | custom-call | flops 5431296 | bytes 1048576 | tf_op jit(solution)/shard_map/rcv_inner/pallas_call | solution.py:390
  20.2 1.1 %collective-permute-done.4 = f32[2,128]{1,0:T(2,128)S(1)} collective-permute-done((f32[2,128]{1,0:T(2,128)S(1)}, f32[2,128]{1,0:T(2,128)S(1)}, u32[]{:S(2)}, u32[]{:S(2)}) %collective-permute-start.4) | collective-permute-done | bytes 1056 | tf_op jit(solution)/shard_map/ppermute | solution.py:476
  21.3 3.3 %collective-permute-start.9 = (f32[2,128]{1,0:T(2,128)S(1)}, f32[2,128]{1,0:T(2,128)S(1)}, u32[]{:S(2)}, u32[]{:S(2)}) collective-permute-start(f32[2,128]{1,0:T(2,128)S(1)} %add_add_fusion.1), channel_id=1, source_target_pairs={{0,25},{1,24},{2,27},{3,26},{4,29},{5,28},{6,31},{7,30},{8,17},{9,... | collective-permute-start | bytes 3080 | tf_op jit(solution)/shard_map/ppermute | solution.py:476
  24.6 1.3 %collective-permute-start.7 = (f32[2,128]{1,0:T(2,128)S(1)}, f32[2,128]{1,0:T(2,128)S(1)}, u32[]{:S(2)}, u32[]{:S(2)}) collective-permute-start(f32[2,128]{1,0:T(2,128)S(1)} %add_add_fusion.1), channel_id=1, source_target_pairs={{0,9},{1,8},{2,11},{3,10},{4,13},{5,12},{6,15},{7,14},{8,1},{9,0},... | collective-permute-start | bytes 3080 | tf_op jit(solution)/shard_map/ppermute | solution.py:476
  25.9 1.1 %rcv_outer.1 = (f32[4,1,32,128]{3,2,1,0:T(8,128)S(1)}, f32[4,1,32,128]{3,2,1,0:T(8,128)S(1)}, f32[4,1,32,128]{3,2,1,0:T(8,128)S(1)}, f32[4,1,32,128]{3,2,1,0:T(8...) custom-call(s32[1]{0:T(128)S(6)} %copy.29.limit, ...), custom_call_target="tpu_custom_call", output_to_operand_aliasing={{0}: (7, {}), {1}: (8, {}), {2}: (9, {}), {3}: (10, {}), {4... | custom-call | flops 6389760 | bytes 1048576 | tf_op jit(solution)/shard_map/rcv_outer/pallas_call | solution.py:390
  27.0 1.5 %collective-permute-done.8 = f32[2,128]{1,0:T(2,128)S(1)} collective-permute-done((f32[2,128]{1,0:T(2,128)S(1)}, f32[2,128]{1,0:T(2,128)S(1)}, u32[]{:S(2)}, u32[]{:S(2)}) %collective-permute-start.8) | collective-permute-done | bytes 1056 | tf_op jit(solution)/shard_map/ppermute | solution.py:476
  28.5 0.8 %combine.1 = (bf16[4,1,128,128]{3,2,1,0:T(8,128)(2,1)}, bf16[4,1,128,128]{3,2,1,0:T(8,128)(2,1)}, f32[1,128]{1,0:T(1,128)}) custom-call(f32[2,128]{1,0:T(2,128)S(1)} %add_add_fusion.sums, f32[4,1,128,128]{3,2,1,0:T(8,128)S(1)} %get-tuple-element.112.src_heavy, f32[4,1,128,128]{3,2,1,0:T(8,128)S(1)} %get-tuple-element.113.src_plain, ...), custom_call_target="tpu_custom_call" | custom-call | bytes 1048576 | tf_op jit(solution)/shard_map/combine/pallas_call | solution.py:390
  (24 shorter events, 0.2 us)
Async XLA Ops:
  1.3 0.9 %copy-start.2 = (s32[1,128,128]{2,1,0:T(8,128)S(1)}, s32[1,128,128]{2,1,0:T(8,128)}, u32[]{:S(2)}) copy-start(s32[1,128,128]{2,1,0:T(8,128)} %sat.13) | copy-start | bytes 196612
  2.4 4.7 %copy-start = (bf16[4,1,128,128]{3,2,1,0:T(8,128)(2,1)S(1)}, bf16[4,1,128,128]{3,2,1,0:T(8,128)(2,1)}, u32[]{:S(2)}) copy-start(bf16[4,1,128,128]{3,2,1,0:T(8,128)(2,1)} %field.6) | copy-start | bytes 393220
  2.4 4.7 %copy-start.1 = (bf16[4,1,128,128]{3,2,1,0:T(8,128)(2,1)S(1)}, bf16[4,1,128,128]{3,2,1,0:T(8,128)(2,1)}, u32[]{:S(2)}) copy-start(bf16[4,1,128,128]{3,2,1,0:T(8,128)(2,1)} %rcv.1) | copy-start | bytes 393220
  2.6 7.9 %collective-permute-start.1 = (bf16[304,128]{1,0:T(8,128)(2,1)S(1)}, bf16[304,128]{1,0:T(8,128)(2,1)S(1)}, u32[]{:S(2)}, u32[]{:S(2)}) collective-permute-start(bf16[304,128]{1,0:T(8,128)(2,1)S(1)} %maximum_maximum_fusion.1), channel_id=1, source_target_pairs={{0,1},{1,0},{2,4},{3,5},{4,2},{5,3},{6,8},{7,9},{8,6},{9,7},{10,12... | collective-permute-start | bytes 233480 | tf_op jit(solution)/shard_map/ppermute | solution.py:408
  3.1 7.7 %collective-permute-start = (bf16[304,128]{1,0:T(8,128)(2,1)S(1)}, bf16[304,128]{1,0:T(8,128)(2,1)S(1)}, u32[]{:S(2)}, u32[]{:S(2)}) collective-permute-start(bf16[304,128]{1,0:T(8,128)(2,1)S(1)} %maximum_maximum_fusion), channel_id=1, source_target_pairs={{0,2},{1,3},{2,0},{3,1},{4,6},{5,7},{6,4},{7,5},{8,10},{9,11},{10,... | collective-permute-start | bytes 233480 | tf_op jit(solution)/shard_map/ppermute | solution.py:407
  12.1 1.2 %collective-permute-start.2 = (f32[2,128]{1,0:T(2,128)S(1)}, f32[2,128]{1,0:T(2,128)S(1)}, u32[]{:S(2)}, u32[]{:S(2)}) collective-permute-start(f32[2,128]{1,0:T(2,128)S(1)} %get-tuple-element.79), channel_id=1, source_target_pairs={{0,1},{1,0},{2,3},{3,2},{4,5},{5,4},{6,7},{7,6},{8,9},{9,8},{10,11... | collective-permute-start | bytes 3080 | tf_op jit(solution)/shard_map/ppermute | solution.py:476
  13.4 7.9 %collective-permute-start.3 = (bf16[272,128]{1,0:T(8,128)(2,1)S(1)}, bf16[272,128]{1,0:T(8,128)(2,1)S(1)}, u32[]{:S(2)}, u32[]{:S(2)}) collective-permute-start(bf16[272,128]{1,0:T(8,128)(2,1)S(1)} %ride.1), channel_id=1, source_target_pairs={{0,2},{1,3},{2,0},{3,1},{4,6},{5,7},{6,4},{7,5},{8,10},{9,11},{10,... | collective-permute-start | bytes 208904 | tf_op jit(solution)/shard_map/ppermute | solution.py:472
  15.2 6.1 %collective-permute-start.6 = (bf16[256,128]{1,0:T(8,128)(2,1)S(1)}, bf16[256,128]{1,0:T(8,128)(2,1)S(1)}, u32[]{:S(2)}, u32[]{:S(2)}) collective-permute-start(bf16[256,128]{1,0:T(8,128)(2,1)S(1)} %bitcast.14), channel_id=1, source_target_pairs={{0,1},{1,0},{2,4},{3,5},{4,2},{5,3},{6,8},{7,9},{8,6},{9,7},{10,12... | collective-permute-start | bytes 196616 | tf_op jit(solution)/shard_map/ppermute | solution.py:478
  15.3 4.9 %collective-permute-start.5 = (f32[2,128]{1,0:T(2,128)S(1)}, f32[2,128]{1,0:T(2,128)S(1)}, u32[]{:S(2)}, u32[]{:S(2)}) collective-permute-start(f32[2,128]{1,0:T(2,128)S(1)} %add.39.sums), channel_id=1, source_target_pairs={{0,7},{1,6},{2,5},{3,4},{4,3},{5,2},{6,1},{7,0},{8,15},{9,14},{10,... | collective-permute-start | bytes 3080 | tf_op jit(solution)/shard_map/ppermute | solution.py:476
  18.3 3.0 %collective-permute-start.4 = (f32[2,128]{1,0:T(2,128)S(1)}, f32[2,128]{1,0:T(2,128)S(1)}, u32[]{:S(2)}, u32[]{:S(2)}) collective-permute-start(f32[2,128]{1,0:T(2,128)S(1)} %add.39.sums), channel_id=1, source_target_pairs={{0,5},{1,4},{2,7},{3,6},{4,1},{5,0},{6,3},{7,2},{8,13},{9,12},{10,... | collective-permute-start | bytes 3080 | tf_op jit(solution)/shard_map/ppermute | solution.py:476
  21.3 5.8 %collective-permute-start.9 = (f32[2,128]{1,0:T(2,128)S(1)}, f32[2,128]{1,0:T(2,128)S(1)}, u32[]{:S(2)}, u32[]{:S(2)}) collective-permute-start(f32[2,128]{1,0:T(2,128)S(1)} %add_add_fusion.1), channel_id=1, source_target_pairs={{0,25},{1,24},{2,27},{3,26},{4,29},{5,28},{6,31},{7,30},{8,17},{9,... | collective-permute-start | bytes 3080 | tf_op jit(solution)/shard_map/ppermute | solution.py:476
  24.6 3.9 %collective-permute-start.8 = (f32[2,128]{1,0:T(2,128)S(1)}, f32[2,128]{1,0:T(2,128)S(1)}, u32[]{:S(2)}, u32[]{:S(2)}) collective-permute-start(f32[2,128]{1,0:T(2,128)S(1)} %add_add_fusion.1), channel_id=1, source_target_pairs={{0,17},{1,16},{2,19},{3,18},{4,21},{5,20},{6,23},{7,22},{8,25},{9,... | collective-permute-start | bytes 3080 | tf_op jit(solution)/shard_map/ppermute | solution.py:476
  24.6 3.9 %collective-permute-start.7 = (f32[2,128]{1,0:T(2,128)S(1)}, f32[2,128]{1,0:T(2,128)S(1)}, u32[]{:S(2)}, u32[]{:S(2)}) collective-permute-start(f32[2,128]{1,0:T(2,128)S(1)} %add_add_fusion.1), channel_id=1, source_target_pairs={{0,9},{1,8},{2,11},{3,10},{4,13},{5,12},{6,15},{7,14},{8,1},{9,0},... | collective-permute-start | bytes 3080 | tf_op jit(solution)/shard_map/ppermute | solution.py:476

commit v2 on v1

--- a/solution.py
+++ b/solution.py
@@ -73,8 +73,7 @@
     masks = edges((sat != 0).astype(jnp.bfloat16), 1, H)
     limits = jnp.full((LIMIT_ROWS, depth), limit[0]).astype(jnp.bfloat16)
     even = jnp.concatenate([rows[0], for_even(*masks), limits], axis=0)
-    even, odd_rows = lax.optimization_barrier((even, rows[1]))
-    return even, jnp.concatenate([odd_rows, for_odd(*masks), limits], axis=0)
+    return even, jnp.concatenate([rows[1], for_odd(*masks), limits], axis=0)
 
 
 def unpack_marks(times, limit, sat, even_in, odd_in, masks, limits):
@@ -220,11 +219,6 @@
 def add_outer(middle, heavy, plain, low, high, masks, limits):
     times, lines, cells, depth = middle.shape
     count = heavy[0].shape[2]
-    widest = [
-        jnp.max(jnp.maximum(limits[pl.ds(H if side else 0, ROWS), :], limits[pl.ds(H + cells * side, ROWS), :]))
-        for side in range(2)
-    ]
-
     for group in range(REACH // PAIR):
 
         def tile(index, carry, group=group):
@@ -241,32 +235,18 @@
                             rows = pl.ds(base + half * ROWS, ROWS)
                             at = number * count + base + half * ROWS
                             rank = 2 * group + (1 - half if side else half)
-                            nearest = ROWS // 2 * rank + 1
-
-                            def add(offsets, sums):
-                                return accumulate(
-                                    center,
-                                    sums,
-                                    offsets,
-                                    lambda h: [shifted[t, y, pl.ds(at + origin + 2 * h, ROWS), :] for t in range(times)],
-                                    within(limits, at),
-                                    lambda h: masks[y, pl.ds(at + H + h, ROWS), :],
-                                )
-
-                            sums = (
-                                [heavy[number][t, y, rows, :] for t in range(times)],
-                                [plain[number][t, y, rows, :] for t in range(times)],
+                            sizes = range(ROWS // 2 * rank + 1, H + 1)
+                            new_heavy, new_plain = accumulate(
+                                center,
+                                (
+                                    [heavy[number][t, y, rows, :] for t in range(times)],
+                                    [plain[number][t, y, rows, :] for t in range(times)],
+                                ),
+                                [size if side else -size for size in sizes],
+                                lambda h: [shifted[t, y, pl.ds(at + origin + 2 * h, ROWS), :] for t in range(times)],
+                                within(limits, at),
+                                lambda h: masks[y, pl.ds(at + H + h, ROWS), :],
                             )
-                            for low in range(1, H + 1, GROUP):
-                                sizes = range(max(low, nearest), min(low + GROUP, H + 1))
-                                if sizes:
-                                    sums = lax.cond(
-                                        widest[side] >= float(sizes[0]),
-                                        functools.partial(add, [size if side else -size for size in sizes]),
-                                        lambda kept: kept,
-                                        sums,
-                                    )
-                            new_heavy, new_plain = sums
                             for t in range(times):
                                 heavy[number][t, y, rows, :] = new_heavy[t]
                                 plain[number][t, y, rows, :] = new_plain[t]
@@ -294,8 +274,8 @@
         return energy, weighted
 
     energy, weighted = lax.fori_loop(0, cells // PAIR, add, (zero, zero))
-    sums[0:1, :] = jnp.full((1, depth), jnp.sum(energy), jnp.float32)
-    sums[1:2, :] = jnp.full((1, depth), jnp.sum(weighted), jnp.float32)
+    sums[0:1, :] = jnp.sum(energy, axis=0, keepdims=True)
+    sums[1:2, :] = jnp.sum(weighted, axis=0, keepdims=True)
 
 
 def rcv_outer_kernel(limit, rcv, sat, even_marks, odd_marks, even_in, odd_in, *refs):
@@ -307,7 +287,8 @@
 
 def combine_kernel(cell_count, sums, src_heavy, src_plain, *refs):
     pieces, (src_out, rcv_out, semblance_out) = refs[:-3], refs[-3:]
-    energy, weighted = sums[0:1, :], sums[1:2, :]
+    total = jnp.broadcast_to(jnp.sum(sums[...], axis=1, keepdims=True), sums.shape)
+    energy, weighted = total[0:1], total[1:2]
     semblance = weighted / energy
     inverse_rms = 1.0 / jnp.sqrt(energy / cell_count + EPSILON)
     semblance_out[...] = semblance
@@ -406,6 +387,7 @@
     even_route, odd_route = exchanges(size, lax.axis_size("xline"))
     even = lax.ppermute(even, DEVICES, even_route)
     odd = lax.ppermute(odd, DEVICES, odd_route)
+    odd_late = lax.ppermute(for_odd(*edges(src, 2, REACH)), DEVICES, odd_route)
     heavy, plain = call(
         functools.partial(inner_kernel, 0),
         "src_inner",
@@ -424,10 +406,6 @@
             0.85 / PIECES,
         )
 
-    (heavy, plain), ahead = lax.optimization_barrier(((heavy, plain), rcv))
-    pieces = list(piece_at(0, src, ahead))
-    (heavy, plain), pieces = lax.optimization_barrier(((heavy, plain), pieces))
-    pieces = list(pieces)
     heavy, plain, sums = call(
         src_outer_kernel,
         "src_outer",
@@ -452,12 +430,15 @@
     lines_all = lax.axis_size("xline")
     steps = reduction_steps(size * lines_all)
     assert len(steps) >= 3 and not any(lines_all in group for group in (steps[0], steps[-1]))
-    low_high = edges(src, 2, REACH)
-    ride = jnp.concatenate([for_even(*low_high), jnp.zeros((LIMIT_ROWS, depth), jnp.bfloat16)], axis=0)
+    sums, ahead = lax.optimization_barrier((sums, src))
+    ride = jnp.concatenate([for_even(*edges(ahead, 2, REACH)), jnp.zeros((LIMIT_ROWS, depth), jnp.bfloat16)], axis=0)
+    pieces = []
     for number, group in enumerate(steps):
         last = number == len(steps) - 1
+        if number == 1:
+            sums, odd_late = lax.optimization_barrier((sums, odd_late))
         if last:
-            sums, *late = lax.optimization_barrier((sums, odd_late, even_late))
+            sums, even_late = lax.optimization_barrier((sums, even_late))
         sums, ahead = lax.optimization_barrier((sums, src))
         arrived = []
         for changed in group:
@@ -474,14 +455,14 @@
             else:
                 route = [(i, i ^ (changed | 1)) for i in range(size * lines_all)]
                 arrived.append(lax.ppermute(sums, DEVICES, route))
-        if number == 0:
-            odd_late = lax.ppermute(for_odd(*edges(ahead, 2, REACH)), DEVICES, odd_route)
         if not last:
-            share = range(1 + (PIECES - 1) * number // (len(steps) - 1), 1 + (PIECES - 1) * (number + 1) // (len(steps) - 1))
+            share = range(1) if number == 0 else range(
+                1 + (PIECES - 1) * (number - 1) // (len(steps) - 2), 1 + (PIECES - 1) * number // (len(steps) - 2)
+            )
             result = [part for i in share for part in piece_at(i, ahead, rcv)]
             pieces += result
         else:
-            result = pieces = list(finish(*late, *pieces))
+            result = pieces = list(finish(odd_late, even_late, *pieces))
         if len(arrived) == 3:
             low, high, both = arrived
             sums = (sums + low) + (high + both)

time: 29.7 us -> 28.8 us (0.970)
  waiting for transfers between devices: 3.17 us -> 6.99 us
  Pallas kernels: 8.79 us -> 6.4 us
  starting transfers between devices: 14.5 us -> 12.4 us
    ppermute x6, starting transfers between devices: 8.16 us -> 5.36 us  [local(): arrived.append(lax.ppermute(sums, DEVICES, route))]
    ppermute x1, waiting for transfers between devices: 0.32 us -> 3.02 us  [local(): even = lax.ppermute(even, DEVICES, even_route)]
    pallas_call x9, Pallas kernels: 8.79 us -> 6.4 us  [call(): pl.pallas_call(kernel, out_shape=out_shape, in_specs=[SMEM if operand is...]
    ppermute x6, waiting for transfers between devices: 2.85 us -> 3.97 us  [local(): arrived.append(lax.ppermute(sums, DEVICES, route))]
    ppermute x1, starting transfers between devices: 1.81 us -> 2.51 us  [local(): even_late = lax.ppermute(ride, DEVICES, even_route)]
  transfers between devices with their start and end apart: 10 -> 10, of which waited for: 4 -> 4; matrix products, arithmetic and copies ran while one was open for 0% -> 0% of each run, Pallas kernels for 23% -> 19%
where the time goes in v2:
time: 28.8 us; the launch traced here: 28.5 us
  starting transfers between devices  12.4 us (43%)
  waiting for transfers between devices  6.99 us (24%)
  Pallas kernels  6.4 us (22%)
  between operations  1.48 us (5%)
  other arithmetic  1.09 us (4%)
    pallas_call x9, Pallas kernels, call(): pl.pallas_call(kernel, out_shape=out_shape, in_specs=[SMEM if operand is...  6.4 us
    ppermute x6, starting transfers between devices, local(): arrived.append(lax.ppermute(sums, DEVICES, route))  5.36 us
    ppermute x1, starting transfers between devices, local(): even = lax.ppermute(even, DEVICES, even_route)  3.98 us
    ppermute x6, waiting for transfers between devices, local(): arrived.append(lax.ppermute(sums, DEVICES, route))  3.97 us
    ppermute x1, waiting for transfers between devices, local(): even = lax.ppermute(even, DEVICES, even_route)  3.02 us
    ppermute x1, starting transfers between devices, local(): even_late = lax.ppermute(ride, DEVICES, even_route)  2.51 us
    select_n x4, other arithmetic, for_even(): return jnp.where(lax.axis_index('inline') % 2 == 0, high, low)  0.95 us
  transfers between devices with their start and end apart: 10, of which 4 were waited for; matrix products, arithmetic and copies ran while one was open for 0% of the time, Pallas kernels for 19%

profile of v2, /device:TPU:0, one launch (start us, length us, event | category | flops | bytes accessed | tf_op | source)
XLA Modules:
  0.0 28.5 jit_solution(13974441722394960014)
XLA Ops:
  1.3 0.9 %broadcast_select_fusion = (bf16[4,1,64,128]{3,2,1,0:T(8,128)(2,1)S(1)}, bf16[4,1,64,128]{3,2,1,0:T(8,128)(2,1)S(1)}) fusion(pred[]{:T(512)S(6)} %eq.15, bf16[4,1,128,128]{3,2,1,0:T(8,128)(2,1)} %rcv.1), kind=kLoop, calls=%fused_computation.5 | loop fusion | flops 65536 | bytes 262145 | tf_op jit(solution)/shard_map/jit(_where)/select_n | solution.py:61
  2.3 0.1 pad.6.clone
  2.4 0.1 maximum_maximum_fusion.1
  2.5 0.0 copy-start.1
  2.5 0.5 %collective-permute-start.1 = (bf16[304,128]{1,0:T(8,128)(2,1)S(1)}, bf16[304,128]{1,0:T(8,128)(2,1)S(1)}, u32[]{:S(2)}, u32[]{:S(2)}) collective-permute-start(bf16[304,128]{1,0:T(8,128)(2,1)S(1)} %get-tuple-element.121), channel_id=1, source_target_pairs={{0,1},{1,0},{2,4},{3,5},{4,2},{5,3},{6,8},{7,9},{8,6},{9,7},{10,12... | collective-permute-start | bytes 233480 | tf_op jit(solution)/shard_map/ppermute | solution.py:389
  3.0 4.0 %collective-permute-start = (bf16[304,128]{1,0:T(8,128)(2,1)S(1)}, bf16[304,128]{1,0:T(8,128)(2,1)S(1)}, u32[]{:S(2)}, u32[]{:S(2)}) collective-permute-start(bf16[304,128]{1,0:T(8,128)(2,1)S(1)} %get-tuple-element.122), channel_id=1, source_target_pairs={{0,2},{1,3},{2,0},{3,1},{4,6},{5,7},{6,4},{7,5},{8,10},{9,11},{10,... | collective-permute-start | bytes 233480 | tf_op jit(solution)/shard_map/ppermute | solution.py:388
  7.0 0.1 collective-permute-start.3
  7.1 1.3 %src_inner.1 = (f32[4,1,128,128]{3,2,1,0:T(8,128)S(1)}, f32[4,1,128,128]{3,2,1,0:T(8,128)S(1)}) custom-call(s32[1]{0:T(128)S(6)} %copy.29.limit, bf16[4,1,128,128]{3,2,1,0:T(8,128)(2,1)S(1)} %copy-done, bf16[4,1,128,128]{3,2,1,0:T(8,128)(2,1)S(1)} %copy-done.1, s32[1,128,128]{2,1,0:T(8,128)S(1)} %copy-done.2), custom_call_target="tpu_custom_call" | custom-call | flops 21725184 | bytes 1048576 | tf_op jit(solution)/shard_map/src_inner/pallas_call | solution.py:371
  8.4 3.0 %collective-permute-done.even_in.even_marks = bf16[304,128]{1,0:T(8,128)(2,1)S(1)} collective-permute-done((bf16[304,128]{1,0:T(8,128)(2,1)S(1)}, bf16[304,128]{1,0:T(8,128)(2,1)S(1)}, u32[]{:S(2)}, u32[]{:S(2)}) %collective-permute-start) | collective-permute-done | bytes 77856 | tf_op jit(solution)/shard_map/ppermute | solution.py:388
  11.4 1.5 %src_outer.1 = (f32[4,1,128,128]{3,2,1,0:T(8,128)S(1)}, f32[4,1,128,128]{3,2,1,0:T(8,128)S(1)}, f32[2,128]{1,0:T(2,128)S(1)}) custom-call(s32[1]{0:T(128)S(6)} %copy.29.limit, bf16[4,1,128,128]{3,2,1,0:T(8,128)(2,1)S(1)} %copy-done, s32[1,128,128]{2,1,0:T(8,128)S(1)} %copy-done.2, ...), custom_call_target="tpu_custom_call", output_to_operand_aliasing={{0}: (5, {}), {1}: (6, {})} | custom-call | flops 6389760 | bytes 1048576 | tf_op jit(solution)/shard_map/src_outer/pallas_call | solution.py:371
  12.9 0.1 collective-permute-start.2
  13.0 0.4 %rcv_inner.4 = (f32[4,1,32,128]{3,2,1,0:T(8,128)S(1)}, f32[4,1,32,128]{3,2,1,0:T(8,128)S(1)}) custom-call(s32[1]{0:T(128)S(6)} %copy.29.limit, bf16[4,1,128,128]{3,2,1,0:T(8,128)(2,1)S(1)} %copy-done.1, bf16[4,1,128,128]{3,2,1,0:T(8,128)(2,1)S(1)} %copy-done, s32[1,128,128]{2,1,0:T(8,128)S(1)} %copy-done.2), custom_call_target="tpu_custom_call" | custom-call | flops 5431296 | bytes 1048576 | tf_op jit(solution)/shard_map/rcv_inner/pallas_call | solution.py:371
  13.4 0.7 %collective-permute-done.2 = f32[2,128]{1,0:T(2,128)S(1)} collective-permute-done((f32[2,128]{1,0:T(2,128)S(1)}, f32[2,128]{1,0:T(2,128)S(1)}, u32[]{:S(2)}, u32[]{:S(2)}) %collective-permute-start.2) | collective-permute-done | bytes 1056 | tf_op jit(solution)/shard_map/ppermute | solution.py:457
  14.1 2.5 %collective-permute-start.4 = (bf16[272,128]{1,0:T(8,128)(2,1)S(1)}, bf16[272,128]{1,0:T(8,128)(2,1)S(1)}, u32[]{:S(2)}, u32[]{:S(2)}) collective-permute-start(bf16[272,128]{1,0:T(8,128)(2,1)S(1)} %ride.1), channel_id=1, source_target_pairs={{0,2},{1,3},{2,0},{3,1},{4,6},{5,7},{6,4},{7,5},{8,10},{9,11},{10,... | collective-permute-start | bytes 208904 | tf_op jit(solution)/shard_map/ppermute | solution.py:453
  16.6 1.3 %collective-permute-start.5 = (f32[2,128]{1,0:T(2,128)S(1)}, f32[2,128]{1,0:T(2,128)S(1)}, u32[]{:S(2)}, u32[]{:S(2)}) collective-permute-start(f32[2,128]{1,0:T(2,128)S(1)} %add.39.sums), channel_id=1, source_target_pairs={{0,5},{1,4},{2,7},{3,6},{4,1},{5,0},{6,3},{7,2},{8,13},{9,12},{10,... | collective-permute-start | bytes 3080 | tf_op jit(solution)/shard_map/ppermute | solution.py:457
  17.9 0.4 %rcv_inner.7 = (f32[4,1,32,128]{3,2,1,0:T(8,128)S(1)}, f32[4,1,32,128]{3,2,1,0:T(8,128)S(1)}) custom-call(s32[1]{0:T(128)S(6)} %copy.29.limit, bf16[4,1,128,128]{3,2,1,0:T(8,128)(2,1)S(1)} %copy-done.1, bf16[4,1,128,128]{3,2,1,0:T(8,128)(2,1)S(1)} %copy-done, s32[1,128,128]{2,1,0:T(8,128)S(1)} %copy-done.2), custom_call_target="tpu_custom_call" | custom-call | flops 5431296 | bytes 1048576 | tf_op jit(solution)/shard_map/rcv_inner/pallas_call | solution.py:371
  18.3 0.4 %rcv_inner.6 = (f32[4,1,32,128]{3,2,1,0:T(8,128)S(1)}, f32[4,1,32,128]{3,2,1,0:T(8,128)S(1)}) custom-call(s32[1]{0:T(128)S(6)} %copy.29.limit, bf16[4,1,128,128]{3,2,1,0:T(8,128)(2,1)S(1)} %copy-done.1, bf16[4,1,128,128]{3,2,1,0:T(8,128)(2,1)S(1)} %copy-done, s32[1,128,128]{2,1,0:T(8,128)S(1)} %copy-done.2), custom_call_target="tpu_custom_call" | custom-call | flops 5431296 | bytes 1048576 | tf_op jit(solution)/shard_map/rcv_inner/pallas_call | solution.py:371
  18.6 0.4 %rcv_inner.5 = (f32[4,1,32,128]{3,2,1,0:T(8,128)S(1)}, f32[4,1,32,128]{3,2,1,0:T(8,128)S(1)}) custom-call(s32[1]{0:T(128)S(6)} %copy.29.limit, bf16[4,1,128,128]{3,2,1,0:T(8,128)(2,1)S(1)} %copy-done.1, bf16[4,1,128,128]{3,2,1,0:T(8,128)(2,1)S(1)} %copy-done, s32[1,128,128]{2,1,0:T(8,128)S(1)} %copy-done.2), custom_call_target="tpu_custom_call" | custom-call | flops 5431296 | bytes 1048576 | tf_op jit(solution)/shard_map/rcv_inner/pallas_call | solution.py:371
  19.0 1.5 %collective-permute-done.6 = f32[2,128]{1,0:T(2,128)S(1)} collective-permute-done((f32[2,128]{1,0:T(2,128)S(1)}, f32[2,128]{1,0:T(2,128)S(1)}, u32[]{:S(2)}, u32[]{:S(2)}) %collective-permute-start.6) | collective-permute-done | bytes 1056 | tf_op jit(solution)/shard_map/ppermute | solution.py:457
  20.5 3.2 %collective-permute-start.9 = (f32[2,128]{1,0:T(2,128)S(1)}, f32[2,128]{1,0:T(2,128)S(1)}, u32[]{:S(2)}, u32[]{:S(2)}) collective-permute-start(f32[2,128]{1,0:T(2,128)S(1)} %add_add_fusion.1), channel_id=1, source_target_pairs={{0,25},{1,24},{2,27},{3,26},{4,29},{5,28},{6,31},{7,30},{8,17},{9,... | collective-permute-start | bytes 3080 | tf_op jit(solution)/shard_map/ppermute | solution.py:457
  23.8 0.8 %collective-permute-start.7 = (f32[2,128]{1,0:T(2,128)S(1)}, f32[2,128]{1,0:T(2,128)S(1)}, u32[]{:S(2)}, u32[]{:S(2)}) collective-permute-start(f32[2,128]{1,0:T(2,128)S(1)} %add_add_fusion.1), channel_id=1, source_target_pairs={{0,9},{1,8},{2,11},{3,10},{4,13},{5,12},{6,15},{7,14},{8,1},{9,0},... | collective-permute-start | bytes 3080 | tf_op jit(solution)/shard_map/ppermute | solution.py:457
  24.6 1.4 %rcv_outer.1 = (f32[4,1,32,128]{3,2,1,0:T(8,128)S(1)}, f32[4,1,32,128]{3,2,1,0:T(8,128)S(1)}, f32[4,1,32,128]{3,2,1,0:T(8,128)S(1)}, f32[4,1,32,128]{3,2,1,0:T(8...) custom-call(s32[1]{0:T(128)S(6)} %copy.29.limit, ...), custom_call_target="tpu_custom_call", output_to_operand_aliasing={{0}: (7, {}), {1}: (8, {}), {2}: (9, {}), {3}: (10, {}), {4... | custom-call | flops 6389760 | bytes 1048576 | tf_op jit(solution)/shard_map/rcv_outer/pallas_call | solution.py:371
  25.9 1.7 %collective-permute-done.8 = f32[2,128]{1,0:T(2,128)S(1)} collective-permute-done((f32[2,128]{1,0:T(2,128)S(1)}, f32[2,128]{1,0:T(2,128)S(1)}, u32[]{:S(2)}, u32[]{:S(2)}) %collective-permute-start.8) | collective-permute-done | bytes 1056 | tf_op jit(solution)/shard_map/ppermute | solution.py:457
  27.7 0.8 %combine.1 = (bf16[4,1,128,128]{3,2,1,0:T(8,128)(2,1)}, bf16[4,1,128,128]{3,2,1,0:T(8,128)(2,1)}, f32[1,128]{1,0:T(1,128)}) custom-call(f32[2,128]{1,0:T(2,128)S(1)} %add_add_fusion.sums, f32[4,1,128,128]{3,2,1,0:T(8,128)S(1)} %get-tuple-element.104.src_heavy, f32[4,1,128,128]{3,2,1,0:T(8,128)S(1)} %get-tuple-element.105.src_plain, ...), custom_call_target="tpu_custom_call" | custom-call | bytes 1048576 | tf_op jit(solution)/shard_map/combine/pallas_call | solution.py:371
  (23 shorter events, 0.1 us)
Async XLA Ops:
  1.3 0.9 %copy-start.2 = (s32[1,128,128]{2,1,0:T(8,128)S(1)}, s32[1,128,128]{2,1,0:T(8,128)}, u32[]{:S(2)}) copy-start(s32[1,128,128]{2,1,0:T(8,128)} %sat.13) | copy-start | bytes 196612
  2.4 4.6 %copy-start = (bf16[4,1,128,128]{3,2,1,0:T(8,128)(2,1)S(1)}, bf16[4,1,128,128]{3,2,1,0:T(8,128)(2,1)}, u32[]{:S(2)}) copy-start(bf16[4,1,128,128]{3,2,1,0:T(8,128)(2,1)} %field.5) | copy-start | bytes 393220
  2.5 4.6 %copy-start.1 = (bf16[4,1,128,128]{3,2,1,0:T(8,128)(2,1)S(1)}, bf16[4,1,128,128]{3,2,1,0:T(8,128)(2,1)}, u32[]{:S(2)}) copy-start(bf16[4,1,128,128]{3,2,1,0:T(8,128)(2,1)} %rcv.1) | copy-start | bytes 393220
  2.5 5.9 %collective-permute-start.1 = (bf16[304,128]{1,0:T(8,128)(2,1)S(1)}, bf16[304,128]{1,0:T(8,128)(2,1)S(1)}, u32[]{:S(2)}, u32[]{:S(2)}) collective-permute-start(bf16[304,128]{1,0:T(8,128)(2,1)S(1)} %get-tuple-element.121), channel_id=1, source_target_pairs={{0,1},{1,0},{2,4},{3,5},{4,2},{5,3},{6,8},{7,9},{8,6},{9,7},{10,12... | collective-permute-start | bytes 233480 | tf_op jit(solution)/shard_map/ppermute | solution.py:389
  3.0 8.4 %collective-permute-start = (bf16[304,128]{1,0:T(8,128)(2,1)S(1)}, bf16[304,128]{1,0:T(8,128)(2,1)S(1)}, u32[]{:S(2)}, u32[]{:S(2)}) collective-permute-start(bf16[304,128]{1,0:T(8,128)(2,1)S(1)} %get-tuple-element.122), channel_id=1, source_target_pairs={{0,2},{1,3},{2,0},{3,1},{4,6},{5,7},{6,4},{7,5},{8,10},{9,11},{10,... | collective-permute-start | bytes 233480 | tf_op jit(solution)/shard_map/ppermute | solution.py:388
  7.0 7.1 %collective-permute-start.3 = (bf16[256,128]{1,0:T(8,128)(2,1)S(1)}, bf16[256,128]{1,0:T(8,128)(2,1)S(1)}, u32[]{:S(2)}, u32[]{:S(2)}) collective-permute-start(bf16[256,128]{1,0:T(8,128)(2,1)S(1)} %bitcast.14), channel_id=1, source_target_pairs={{0,1},{1,0},{2,4},{3,5},{4,2},{5,3},{6,8},{7,9},{8,6},{9,7},{10,12... | collective-permute-start | bytes 196616 | tf_op jit(solution)/shard_map/ppermute | solution.py:390
  12.9 1.2 %collective-permute-start.2 = (f32[2,128]{1,0:T(2,128)S(1)}, f32[2,128]{1,0:T(2,128)S(1)}, u32[]{:S(2)}, u32[]{:S(2)}) collective-permute-start(f32[2,128]{1,0:T(2,128)S(1)} %get-tuple-element.67), channel_id=1, source_target_pairs={{0,1},{1,0},{2,3},{3,2},{4,5},{5,4},{6,7},{7,6},{8,9},{9,8},{10,11... | collective-permute-start | bytes 3080 | tf_op jit(solution)/shard_map/ppermute | solution.py:457
  14.1 6.4 %collective-permute-start.4 = (bf16[272,128]{1,0:T(8,128)(2,1)S(1)}, bf16[272,128]{1,0:T(8,128)(2,1)S(1)}, u32[]{:S(2)}, u32[]{:S(2)}) collective-permute-start(bf16[272,128]{1,0:T(8,128)(2,1)S(1)} %ride.1), channel_id=1, source_target_pairs={{0,2},{1,3},{2,0},{3,1},{4,6},{5,7},{6,4},{7,5},{8,10},{9,11},{10,... | collective-permute-start | bytes 208904 | tf_op jit(solution)/shard_map/ppermute | solution.py:453
  16.6 3.9 %collective-permute-start.6 = (f32[2,128]{1,0:T(2,128)S(1)}, f32[2,128]{1,0:T(2,128)S(1)}, u32[]{:S(2)}, u32[]{:S(2)}) collective-permute-start(f32[2,128]{1,0:T(2,128)S(1)} %add.39.sums), channel_id=1, source_target_pairs={{0,7},{1,6},{2,5},{3,4},{4,3},{5,2},{6,1},{7,0},{8,15},{9,14},{10,... | collective-permute-start | bytes 3080 | tf_op jit(solution)/shard_map/ppermute | solution.py:457
  16.6 3.9 %collective-permute-start.5 = (f32[2,128]{1,0:T(2,128)S(1)}, f32[2,128]{1,0:T(2,128)S(1)}, u32[]{:S(2)}, u32[]{:S(2)}) collective-permute-start(f32[2,128]{1,0:T(2,128)S(1)} %add.39.sums), channel_id=1, source_target_pairs={{0,5},{1,4},{2,7},{3,6},{4,1},{5,0},{6,3},{7,2},{8,13},{9,12},{10,... | collective-permute-start | bytes 3080 | tf_op jit(solution)/shard_map/ppermute | solution.py:457
  20.5 5.4 %collective-permute-start.9 = (f32[2,128]{1,0:T(2,128)S(1)}, f32[2,128]{1,0:T(2,128)S(1)}, u32[]{:S(2)}, u32[]{:S(2)}) collective-permute-start(f32[2,128]{1,0:T(2,128)S(1)} %add_add_fusion.1), channel_id=1, source_target_pairs={{0,25},{1,24},{2,27},{3,26},{4,29},{5,28},{6,31},{7,30},{8,17},{9,... | collective-permute-start | bytes 3080 | tf_op jit(solution)/shard_map/ppermute | solution.py:457
  23.8 3.9 %collective-permute-start.8 = (f32[2,128]{1,0:T(2,128)S(1)}, f32[2,128]{1,0:T(2,128)S(1)}, u32[]{:S(2)}, u32[]{:S(2)}) collective-permute-start(f32[2,128]{1,0:T(2,128)S(1)} %add_add_fusion.1), channel_id=1, source_target_pairs={{0,17},{1,16},{2,19},{3,18},{4,21},{5,20},{6,23},{7,22},{8,25},{9,... | collective-permute-start | bytes 3080 | tf_op jit(solution)/shard_map/ppermute | solution.py:457
  23.8 3.9 %collective-permute-start.7 = (f32[2,128]{1,0:T(2,128)S(1)}, f32[2,128]{1,0:T(2,128)S(1)}, u32[]{:S(2)}, u32[]{:S(2)}) collective-permute-start(f32[2,128]{1,0:T(2,128)S(1)} %add_add_fusion.1), channel_id=1, source_target_pairs={{0,9},{1,8},{2,11},{3,10},{4,13},{5,12},{6,15},{7,14},{8,1},{9,0},... | collective-permute-start | bytes 3080 | tf_op jit(solution)/shard_map/ppermute | solution.py:457

commit v3 on v2

--- a/solution.py
+++ b/solution.py
@@ -387,7 +387,9 @@
     even_route, odd_route = exchanges(size, lax.axis_size("xline"))
     even = lax.ppermute(even, DEVICES, even_route)
     odd = lax.ppermute(odd, DEVICES, odd_route)
-    odd_late = lax.ppermute(for_odd(*edges(src, 2, REACH)), DEVICES, odd_route)
+    low_high = edges(src, 2, REACH)
+    odd_late = lax.ppermute(for_odd(*low_high), DEVICES, odd_route)
+    even_late = lax.ppermute(for_even(*low_high), DEVICES, even_route)
     heavy, plain = call(
         functools.partial(inner_kernel, 0),
         "src_inner",
@@ -428,48 +430,13 @@
         )
 
     lines_all = lax.axis_size("xline")
-    steps = reduction_steps(size * lines_all)
-    assert len(steps) >= 3 and not any(lines_all in group for group in (steps[0], steps[-1]))
+    count = size * lines_all
+    spread = jnp.broadcast_to(sums[None], (count, *sums.shape))
+    gathered = lax.all_to_all(spread, DEVICES, 0, 0, tiled=True)
     sums, ahead = lax.optimization_barrier((sums, src))
-    ride = jnp.concatenate([for_even(*edges(ahead, 2, REACH)), jnp.zeros((LIMIT_ROWS, depth), jnp.bfloat16)], axis=0)
-    pieces = []
-    for number, group in enumerate(steps):
-        last = number == len(steps) - 1
-        if number == 1:
-            sums, odd_late = lax.optimization_barrier((sums, odd_late))
-        if last:
-            sums, even_late = lax.optimization_barrier((sums, even_late))
-        sums, ahead = lax.optimization_barrier((sums, src))
-        arrived = []
-        for changed in group:
-            if changed == lines_all:
-                ride = call(
-                    ride_kernel,
-                    "ride",
-                    shape(ride.shape, ride.dtype),
-                    (ride, sums),
-                    aliases={0: 0},
-                )
-                even_late = lax.ppermute(ride, DEVICES, even_route)
-                arrived.append(sums_below(even_late, sums.shape[0]))
-            else:
-                route = [(i, i ^ (changed | 1)) for i in range(size * lines_all)]
-                arrived.append(lax.ppermute(sums, DEVICES, route))
-        if not last:
-            share = range(1) if number == 0 else range(
-                1 + (PIECES - 1) * (number - 1) // (len(steps) - 2), 1 + (PIECES - 1) * number // (len(steps) - 2)
-            )
-            result = [part for i in share for part in piece_at(i, ahead, rcv)]
-            pieces += result
-        else:
-            result = pieces = list(finish(odd_late, even_late, *pieces))
-        if len(arrived) == 3:
-            low, high, both = arrived
-            sums = (sums + low) + (high + both)
-        else:
-            sums = sums + arrived[0]
-        sums, result = lax.optimization_barrier((sums, result))
-        pieces[len(pieces) - len(result) :] = result
+    pieces = [part for i in range(PIECES) for part in piece_at(i, ahead, rcv)]
+    pieces = finish(odd_late, even_late, *pieces)
+    sums = jnp.sum(gathered, axis=0)
 
     cell_count = float(lines * lax.axis_size("xline") * cells * size * depth * (2 * H + 1))
     src_adj, rcv_adj, semblance = call(

time: 28.8 us -> 28.2 us (0.979); the launches traced: 28.5 us -> 28.4 us
  Pallas kernels: 6.4 us -> 9.29 us
  waiting for transfers between devices: 6.99 us -> 4.85 us
  starting transfers between devices: 12.4 us -> 10.9 us
  local copies, waits for them, and re-layouts: 0.1 us -> 0.72 us
    ppermute x8 -> x2, starting transfers between devices: 7.94 us -> 0.14 us  [the longest x1 0.07 us: local(): even_late = lax.ppermute(for_even(*low_high), DEVICES, even_route)]
    all_to_all x0 -> x1, starting transfers between devices: none -> 6.31 us  [local(): gathered = lax.all_to_all(spread, DEVICES, 0, 0, tiled=True)]
    ppermute x8 -> x2, waiting for transfers between devices: 3.97 us -> 0.01 us  [the longest x1 0.01 us: local(): even_late = lax.ppermute(for_even(*low_high), DEVICES, even_route)]
    all_to_all x0 -> x1, waiting for transfers between devices: none -> 2.91 us  [local(): gathered = lax.all_to_all(spread, DEVICES, 0, 0, tiled=True)]
    pallas_call x9 -> x8, Pallas kernels: 6.4 us -> 9.29 us  [call(): pl.pallas_call(kernel, out_shape=out_shape, in_specs=[SMEM if operand is...]
    ppermute x1, waiting for transfers between devices: 3.02 us -> 1.94 us  [local(): even = lax.ppermute(even, DEVICES, even_route)]
    broadcast_in_dim x0 -> x1, local copies, waits for them, and re-layouts: none -> 0.62 us  [local(): spread = jnp.broadcast_to(sums[None], (count, *sums.shape))]
    select_n x4 -> x3, other arithmetic: 0.95 us -> 0.94 us  [for_even(): return jnp.where(lax.axis_index('inline') % 2 == 0, high, low)]
  transfers between devices with their start and end apart: 10 -> 5, of which waited for: 4 -> 2; matrix products, arithmetic and copies ran while one was open for 0% -> 2% of each run, Pallas kernels for 19% -> 30%
where the time goes in v3:
time: 28.2 us; the launch traced here: 28.4 us
  starting transfers between devices  10.9 us (39%)
  Pallas kernels  9.29 us (33%)
  waiting for transfers between devices  4.85 us (17%)
  between operations  1.46 us (5%)
  other arithmetic  1.11 us (4%)
  local copies, waits for them, and re-layouts  0.72 us (3%)
    pallas_call x8, Pallas kernels, call(): pl.pallas_call(kernel, out_shape=out_shape, in_specs=[SMEM if operand is...  9.29 us
    all_to_all x1, starting transfers between devices, local(): gathered = lax.all_to_all(spread, DEVICES, 0, 0, tiled=True)  6.31 us
    ppermute x1, starting transfers between devices, local(): even = lax.ppermute(even, DEVICES, even_route)  3.98 us
    all_to_all x1, waiting for transfers between devices, local(): gathered = lax.all_to_all(spread, DEVICES, 0, 0, tiled=True)  2.91 us
    ppermute x1, waiting for transfers between devices, local(): even = lax.ppermute(even, DEVICES, even_route)  1.94 us
    select_n x3, other arithmetic, for_even(): return jnp.where(lax.axis_index('inline') % 2 == 0, high, low)  0.94 us
    broadcast_in_dim x1, local copies, waits for them, and re-layouts, local(): spread = jnp.broadcast_to(sums[None], (count, *sums.shape))  0.62 us
  transfers between devices with their start and end apart: 5, of which 2 were waited for; matrix products, arithmetic and copies ran while one was open for 2% of the time, Pallas kernels for 30%

profile of v3, /device:TPU:0, one launch (start us, length us, event | category | flops | bytes accessed | tf_op | source)
XLA Modules:
  0.0 28.4 jit_solution(10335980856417783195)
XLA Ops:
  1.3 0.0 copy-start.2
  1.3 0.9 %broadcast_select_fusion.2 = (bf16[4,1,64,128]{3,2,1,0:T(8,128)(2,1)S(1)}, bf16[4,1,64,128]{3,2,1,0:T(8,128)(2,1)S(1)}) fusion(pred[]{:T(512)S(6)} %eq.15, bf16[4,1,128,128]{3,2,1,0:T(8,128)(2,1)} %rcv.1), kind=kLoop, calls=%fused_computation.5 | loop fusion | flops 65536 | bytes 262145 | tf_op jit(solution)/shard_map/jit(_where)/select_n | solution.py:61
  2.2 0.0 copy-done.2
  2.3 0.1 pad.5.clone
  2.4 0.1 maximum_maximum_fusion.1
  2.5 0.5 %collective-permute-start.1 = (bf16[304,128]{1,0:T(8,128)(2,1)S(1)}, bf16[304,128]{1,0:T(8,128)(2,1)S(1)}, u32[]{:S(2)}, u32[]{:S(2)}) collective-permute-start(bf16[304,128]{1,0:T(8,128)(2,1)S(1)} %get-tuple-element.65), channel_id=1, source_target_pairs={{0,1},{1,0},{2,4},{3,5},{4,2},{5,3},{6,8},{7,9},{8,6},{9,7},{10,12... | collective-permute-start | bytes 233480 | tf_op jit(solution)/shard_map/ppermute | solution.py:389
  3.0 4.0 %collective-permute-start = (bf16[304,128]{1,0:T(8,128)(2,1)S(1)}, bf16[304,128]{1,0:T(8,128)(2,1)S(1)}, u32[]{:S(2)}, u32[]{:S(2)}) collective-permute-start(bf16[304,128]{1,0:T(8,128)(2,1)S(1)} %get-tuple-element.66), channel_id=1, source_target_pairs={{0,2},{1,3},{2,0},{3,1},{4,6},{5,7},{6,4},{7,5},{8,10},{9,11},{10,... | collective-permute-start | bytes 233480 | tf_op jit(solution)/shard_map/ppermute | solution.py:388
  7.0 0.1 collective-permute-start.2
  7.1 0.1 collective-permute-start.3
  7.2 2.7 %src_inner.1 = (f32[4,1,128,128]{3,2,1,0:T(8,128)S(1)}, f32[4,1,128,128]{3,2,1,0:T(8,128)S(1)}) custom-call(s32[1]{0:T(128)S(6)} %copy.29.limit, bf16[4,1,128,128]{3,2,1,0:T(8,128)(2,1)S(1)} %copy-done.1, bf16[4,1,128,128]{3,2,1,0:T(8,128)(2,1)S(1)} %copy-done, s32[1,128,128]{2,1,0:T(8,128)S(1)} %copy-done.2), custom_call_target="tpu_custom_call" | custom-call | flops 21725184 | bytes 1048576 | tf_op jit(solution)/shard_map/src_inner/pallas_call | solution.py:371
  9.9 0.0 collective-permute-done.1.odd_in.odd_marks
  9.9 1.9 %collective-permute-done.even_in.even_marks = bf16[304,128]{1,0:T(8,128)(2,1)S(1)} collective-permute-done((bf16[304,128]{1,0:T(8,128)(2,1)S(1)}, bf16[304,128]{1,0:T(8,128)(2,1)S(1)}, u32[]{:S(2)}, u32[]{:S(2)}) %collective-permute-start) | collective-permute-done | bytes 77856 | tf_op jit(solution)/shard_map/ppermute | solution.py:388
  11.9 1.4 %src_outer.1 = (f32[4,1,128,128]{3,2,1,0:T(8,128)S(1)}, f32[4,1,128,128]{3,2,1,0:T(8,128)S(1)}, f32[2,128]{1,0:T(2,128)S(1)}) custom-call(s32[1]{0:T(128)S(6)} %copy.29.limit, bf16[4,1,128,128]{3,2,1,0:T(8,128)(2,1)S(1)} %copy-done.1, s32[1,128,128]{2,1,0:T(8,128)S(1)} %copy-done.2, ...), custom_call_target="tpu_custom_call", output_to_operand_aliasing={{0}: (5, {}), {1}: (6, {})} | custom-call | flops 6389760 | bytes 1048576 | tf_op jit(solution)/shard_map/src_outer/pallas_call | solution.py:371
  13.3 0.6 %broadcast_in_dim.10 = f32[32,2,128]{2,1,0:T(2,128)} broadcast(f32[2,128]{1,0:T(2,128)S(1)} %get-tuple-element.36), dimensions={1,2} | broadcast | bytes 33792 | tf_op jit(solution)/shard_map/broadcast_in_dim | solution.py:434
  13.9 6.3 %all-to-all-start = ((f32[32,2,128]{2,1,0:T(2,128)}), f32[32,2,128]{2,1,0:T(2,128)S(1)}, u32[]{:S(2)}, u32[]{:S(2)}) async-start(f32[32,2,128]{2,1,0:T(2,128)} %broadcast_in_dim.10), calls=%async_computation | async-start | bytes 65536 | tf_op jit(solution)/shard_map/all_to_all | solution.py:435
  20.3 0.7 %rcv_inner.7 = (f32[4,1,32,128]{3,2,1,0:T(8,128)S(1)}, f32[4,1,32,128]{3,2,1,0:T(8,128)S(1)}) custom-call(s32[1]{0:T(128)S(6)} %copy.29.limit, bf16[4,1,128,128]{3,2,1,0:T(8,128)(2,1)S(1)} %copy-done, bf16[4,1,128,128]{3,2,1,0:T(8,128)(2,1)S(1)} %copy-done.1, s32[1,128,128]{2,1,0:T(8,128)S(1)} %copy-done.2), custom_call_target="tpu_custom_call" | custom-call | flops 5431296 | bytes 1048576 | tf_op jit(solution)/shard_map/rcv_inner/pallas_call | solution.py:371
  20.9 0.8 %rcv_inner.6 = (f32[4,1,32,128]{3,2,1,0:T(8,128)S(1)}, f32[4,1,32,128]{3,2,1,0:T(8,128)S(1)}) custom-call(s32[1]{0:T(128)S(6)} %copy.29.limit, bf16[4,1,128,128]{3,2,1,0:T(8,128)(2,1)S(1)} %copy-done, bf16[4,1,128,128]{3,2,1,0:T(8,128)(2,1)S(1)} %copy-done.1, s32[1,128,128]{2,1,0:T(8,128)S(1)} %copy-done.2), custom_call_target="tpu_custom_call" | custom-call | flops 5431296 | bytes 1048576 | tf_op jit(solution)/shard_map/rcv_inner/pallas_call | solution.py:371
  21.7 0.8 %rcv_inner.5 = (f32[4,1,32,128]{3,2,1,0:T(8,128)S(1)}, f32[4,1,32,128]{3,2,1,0:T(8,128)S(1)}) custom-call(s32[1]{0:T(128)S(6)} %copy.29.limit, bf16[4,1,128,128]{3,2,1,0:T(8,128)(2,1)S(1)} %copy-done, bf16[4,1,128,128]{3,2,1,0:T(8,128)(2,1)S(1)} %copy-done.1, s32[1,128,128]{2,1,0:T(8,128)S(1)} %copy-done.2), custom_call_target="tpu_custom_call" | custom-call | flops 5431296 | bytes 1048576 | tf_op jit(solution)/shard_map/rcv_inner/pallas_call | solution.py:371
  22.5 0.7 %rcv_inner.4 = (f32[4,1,32,128]{3,2,1,0:T(8,128)S(1)}, f32[4,1,32,128]{3,2,1,0:T(8,128)S(1)}) custom-call(s32[1]{0:T(128)S(6)} %copy.29.limit, bf16[4,1,128,128]{3,2,1,0:T(8,128)(2,1)S(1)} %copy-done, bf16[4,1,128,128]{3,2,1,0:T(8,128)(2,1)S(1)} %copy-done.1, s32[1,128,128]{2,1,0:T(8,128)S(1)} %copy-done.2), custom_call_target="tpu_custom_call" | custom-call | flops 5431296 | bytes 1048576 | tf_op jit(solution)/shard_map/rcv_inner/pallas_call | solution.py:371
  23.2 0.0 collective-permute-done.2.even_in
  23.2 0.0 collective-permute-done.3.odd_in
  23.2 1.4 %rcv_outer.1 = (f32[4,1,32,128]{3,2,1,0:T(8,128)S(1)}, f32[4,1,32,128]{3,2,1,0:T(8,128)S(1)}, f32[4,1,32,128]{3,2,1,0:T(8,128)S(1)}, f32[4,1,32,128]{3,2,1,0:T(8...) custom-call(s32[1]{0:T(128)S(6)} %copy.29.limit, ...), custom_call_target="tpu_custom_call", output_to_operand_aliasing={{0}: (7, {}), {1}: (8, {}), {2}: (9, {}), {3}: (10, {}), {4... | custom-call | flops 6389760 | bytes 1048576 | tf_op jit(solution)/shard_map/rcv_outer/pallas_call | solution.py:371
  24.6 2.9 %all-to-all-done = f32[32,2,128]{2,1,0:T(2,128)S(1)} async-done(((f32[32,2,128]{2,1,0:T(2,128)}), f32[32,2,128]{2,1,0:T(2,128)S(1)}, u32[]{:S(2)}, u32[]{:S(2)}) %all-to-all-start) | async-done | bytes 32800 | tf_op jit(solution)/shard_map/all_to_all | solution.py:435
  27.5 0.8 %combine.1 = (bf16[4,1,128,128]{3,2,1,0:T(8,128)(2,1)}, bf16[4,1,128,128]{3,2,1,0:T(8,128)(2,1)}, f32[1,128]{1,0:T(1,128)}) custom-call(f32[2,128]{1,0:T(2,128)S(1)} %reduce_sum.9.sums, f32[4,1,128,128]{3,2,1,0:T(8,128)S(1)} %get-tuple-element.37.src_heavy, f32[4,1,128,128]{3,2,1,0:T(8,128)S(1)} %get-tuple-element.38.src_plain, ...), custom_call_target="tpu_custom_call" | custom-call | bytes 1048576 | tf_op jit(solution)/shard_map/combine/pallas_call | solution.py:371
  (9 shorter events, 0.1 us)
Async XLA Ops:
  1.3 0.9 %copy-start.2 = (s32[1,128,128]{2,1,0:T(8,128)S(1)}, s32[1,128,128]{2,1,0:T(8,128)}, u32[]{:S(2)}) copy-start(s32[1,128,128]{2,1,0:T(8,128)} %sat.13) | copy-start | bytes 196612
  2.4 4.6 %copy-start.1 = (bf16[4,1,128,128]{3,2,1,0:T(8,128)(2,1)S(1)}, bf16[4,1,128,128]{3,2,1,0:T(8,128)(2,1)}, u32[]{:S(2)}) copy-start(bf16[4,1,128,128]{3,2,1,0:T(8,128)(2,1)} %field.5) | copy-start | bytes 393220
  2.5 7.4 %collective-permute-start.1 = (bf16[304,128]{1,0:T(8,128)(2,1)S(1)}, bf16[304,128]{1,0:T(8,128)(2,1)S(1)}, u32[]{:S(2)}, u32[]{:S(2)}) collective-permute-start(bf16[304,128]{1,0:T(8,128)(2,1)S(1)} %get-tuple-element.65), channel_id=1, source_target_pairs={{0,1},{1,0},{2,4},{3,5},{4,2},{5,3},{6,8},{7,9},{8,6},{9,7},{10,12... | collective-permute-start | bytes 233480 | tf_op jit(solution)/shard_map/ppermute | solution.py:389
  3.0 4.2 %copy-start = (bf16[4,1,128,128]{3,2,1,0:T(8,128)(2,1)S(1)}, bf16[4,1,128,128]{3,2,1,0:T(8,128)(2,1)}, u32[]{:S(2)}) copy-start(bf16[4,1,128,128]{3,2,1,0:T(8,128)(2,1)} %rcv.1) | copy-start | bytes 393220
  3.0 8.9 %collective-permute-start = (bf16[304,128]{1,0:T(8,128)(2,1)S(1)}, bf16[304,128]{1,0:T(8,128)(2,1)S(1)}, u32[]{:S(2)}, u32[]{:S(2)}) collective-permute-start(bf16[304,128]{1,0:T(8,128)(2,1)S(1)} %get-tuple-element.66), channel_id=1, source_target_pairs={{0,2},{1,3},{2,0},{3,1},{4,6},{5,7},{6,4},{7,5},{8,10},{9,11},{10,... | collective-permute-start | bytes 233480 | tf_op jit(solution)/shard_map/ppermute | solution.py:388
  7.0 16.2 %collective-permute-start.2 = (bf16[256,128]{1,0:T(8,128)(2,1)S(1)}, bf16[256,128]{1,0:T(8,128)(2,1)S(1)}, u32[]{:S(2)}, u32[]{:S(2)}) collective-permute-start(bf16[256,128]{1,0:T(8,128)(2,1)S(1)} %bitcast.14), channel_id=1, source_target_pairs={{0,2},{1,3},{2,0},{3,1},{4,6},{5,7},{6,4},{7,5},{8,10},{9,11},{10,... | collective-permute-start | bytes 196616 | tf_op jit(solution)/shard_map/ppermute | solution.py:392
  7.1 16.1 %collective-permute-start.3 = (bf16[256,128]{1,0:T(8,128)(2,1)S(1)}, bf16[256,128]{1,0:T(8,128)(2,1)S(1)}, u32[]{:S(2)}, u32[]{:S(2)}) collective-permute-start(bf16[256,128]{1,0:T(8,128)(2,1)S(1)} %bitcast.13), channel_id=1, source_target_pairs={{0,1},{1,0},{2,4},{3,5},{4,2},{5,3},{6,8},{7,9},{8,6},{9,7},{10,12... | collective-permute-start | bytes 196616 | tf_op jit(solution)/shard_map/ppermute | solution.py:391
  13.9 13.6 %all-to-all-start = ((f32[32,2,128]{2,1,0:T(2,128)}), f32[32,2,128]{2,1,0:T(2,128)S(1)}, u32[]{:S(2)}, u32[]{:S(2)}) async-start(f32[32,2,128]{2,1,0:T(2,128)} %broadcast_in_dim.10), calls=%async_computation | async-start | bytes 65536 | tf_op jit(solution)/shard_map/all_to_all | solution.py:435

commit v4 on v3

--- a/solution.py
+++ b/solution.py
@@ -16,7 +16,6 @@
 ROWS = 8
 PAIR = 2 * ROWS
 LIMIT_ROWS = 16
-PIECES = 4
 DEVICES = ("inline", "xline")
 GROUP = 8
 GRANT = 12 << 20
@@ -29,6 +28,10 @@
     return relative * relative
 
 
+def cap_of(mask):
+    return jnp.where(mask != 0, SATURATION * SATURATION, 2.0)
+
+
 def payload_layout(times, lines):
     mask_at = times * lines * REACH
     return mask_at, mask_at + lines * H
@@ -69,28 +72,28 @@
     depth = rcv.shape[-1]
     rows = edges(rcv, 2, REACH)
     rows = for_even(*rows), for_odd(*rows)
-    *rows, sat = lax.optimization_barrier((*rows, sat))
+    *rows, sat, limit = lax.optimization_barrier((*rows, sat, limit))
     masks = edges((sat != 0).astype(jnp.bfloat16), 1, H)
     limits = jnp.full((LIMIT_ROWS, depth), limit[0]).astype(jnp.bfloat16)
     even = jnp.concatenate([rows[0], for_even(*masks), limits], axis=0)
-    return even, jnp.concatenate([rows[1], for_odd(*masks), limits], axis=0)
-
-
-def unpack_marks(times, limit, sat, even_in, odd_in, masks, limits):
+    return limit, even, jnp.concatenate([rows[1], for_odd(*masks), limits], axis=0)
+
+
+def unpack_marks(times, limit, sat, even_in, odd_in, caps, limits):
     lines, cells, depth = sat.shape
     mask_at, limit_at = payload_layout(times, lines)
 
     def halo(arrived, low, there):
         row_at = 0 if low else H + cells
         for y in range(lines):
-            masks[y, pl.ds(row_at, H), :] = arrived[pl.ds(mask_at + y * H, H), :].astype(jnp.float32)
+            caps[y, pl.ds(row_at, H), :] = cap_of(arrived[pl.ds(mask_at + y * H, H), :].astype(jnp.float32))
         value = arrived[pl.ds(limit_at, LIMIT_ROWS), :].astype(jnp.float32)
         for part in range(H // LIMIT_ROWS):
             limits[pl.ds(row_at + part * LIMIT_ROWS, LIMIT_ROWS), :] = value
 
     by_parity(even_in, odd_in, halo)
     for y in range(lines):
-        masks[y, pl.ds(H, cells), :] = (sat[y] != 0).astype(jnp.float32)
+        caps[y, pl.ds(H, cells), :] = cap_of(sat[y])
     limits[pl.ds(H, cells), :] = jnp.full((cells, depth), limit[0], jnp.int32).astype(jnp.float32)
 
 
@@ -116,7 +119,7 @@
     return image
 
 
-def accumulate(center, sums, offsets, far_at, masked, mask_at):
+def accumulate(center, sums, offsets, far_at, masked, cap_at):
     heavy, plain = sums
     times = range(len(center))
     near = {}
@@ -136,7 +139,7 @@
                     heavy = [heavy[t] + terms[t] * square for t in times]
         else:
             square = square_weight(offset)
-            weighed = image * jnp.where(mask_at(offset) != 0.0, SATURATION * SATURATION, square)
+            weighed = image * jnp.minimum(cap_at(offset), square)
             plain = [plain[t] + image * far[t] for t in times]
             heavy = [heavy[t] + weighed * far[t] for t in times]
     return heavy, plain
@@ -152,7 +155,7 @@
     return [[rows[half * ROWS : (half + 1) * ROWS] for rows in both] for half in range(2)]
 
 
-def inner_kernel(first, limit, middle, field, sat, heavy_out, plain_out, shifted, masks):
+def inner_kernel(limit, middle, field, sat, heavy_out, plain_out, shifted, caps):
     times, lines, cells, depth = field.shape
     zero = jnp.zeros((ROWS, depth), jnp.float32)
     blank = jnp.zeros((REACH, depth), jnp.float32)
@@ -162,41 +165,51 @@
             shifted[t, y, pl.ds(REACH, cells), :] = field[t, y].astype(jnp.float32)
             shifted[t, y, pl.ds(REACH + cells, REACH), :] = blank
     for y in range(lines):
-        masks[y, pl.ds(0, H), :] = blank[:H]
-        masks[y, pl.ds(H, cells), :] = (sat[y] != 0).astype(jnp.float32)
-        masks[y, pl.ds(H + cells, H), :] = blank[:H]
+        caps[y, pl.ds(0, H), :] = blank[:H]
+        caps[y, pl.ds(H, cells), :] = cap_of(sat[y])
+        caps[y, pl.ds(H + cells, H), :] = blank[:H]
     inside = [(size <= limit[0]).astype(jnp.float32) for size in range(H + 1)]
 
     def tile(index, carry):
         base = pl.multiple_of(index * PAIR, PAIR)
         for y in range(lines):
-            for half, center in enumerate(tiles_of(middle, y, first + base)):
-                at = first + base + half * ROWS
-
-                def add(offsets, sums):
+            for half, center in enumerate(tiles_of(middle, y, base)):
+                at = base + half * ROWS
+
+                def add(offsets, masked, sums):
                     return accumulate(
                         center,
                         sums,
                         offsets,
                         lambda h: [shifted[t, y, pl.ds(at + REACH + 2 * h, ROWS), :] for t in range(times)],
-                        lambda image, h: image * inside[abs(h)] if abs(h) > ALWAYS else image,
-                        lambda h: masks[y, pl.ds(at + H + h, ROWS), :],
+                        lambda image, h: image * inside[abs(h)] if masked else image,
+                        lambda h: caps[y, pl.ds(at + H + h, ROWS), :],
                     )
 
-                sums = add(paired(ALWAYS), ([zero] * times, [zero] * times))
+                sums = add(paired(ALWAYS), False, ([zero] * times, [zero] * times))
                 for low in range(ALWAYS + 1, H + 1, GROUP):
                     high = min(low + GROUP - 1, H)
                     if high <= SHARED:
                         parts = [(paired(high, low), limit[0] >= low)]
                     else:
-                        below = first + base + PAIR - 1 - 2 * low >= 0
-                        above = first + base + 2 * low < cells
+                        below = base + PAIR - 1 - 2 * low >= 0
+                        above = base + 2 * low < cells
                         parts = [
                             ([sign * size for size in range(low, high + 1)], jnp.logical_and(reach, limit[0] >= low))
                             for sign, reach in ((-1, below), (1, above))
                         ]
                     for offsets, needed in parts:
-                        sums = lax.cond(needed, functools.partial(add, offsets), lambda kept: kept, sums)
+                        sums = lax.cond(
+                            needed,
+                            lambda sums: lax.cond(
+                                limit[0] >= high,
+                                functools.partial(add, offsets, False),
+                                functools.partial(add, offsets, True),
+                                sums,
+                            ),
+                            lambda kept: kept,
+                            sums,
+                        )
                 heavy, plain = sums
                 rows = pl.ds(base + half * ROWS, ROWS)
                 for t in range(times):
@@ -216,7 +229,7 @@
     return masked
 
 
-def add_outer(middle, heavy, plain, low, high, masks, limits):
+def add_outer(middle, heavy, plain, low, high, caps, limits):
     times, lines, cells, depth = middle.shape
     count = heavy[0].shape[2]
     for group in range(REACH // PAIR):
@@ -245,7 +258,7 @@
                                 [size if side else -size for size in sizes],
                                 lambda h: [shifted[t, y, pl.ds(at + origin + 2 * h, ROWS), :] for t in range(times)],
                                 within(limits, at),
-                                lambda h: masks[y, pl.ds(at + H + h, ROWS), :],
+                                lambda h: caps[y, pl.ds(at + H + h, ROWS), :],
                             )
                             for t in range(times):
                                 heavy[number][t, y, rows, :] = new_heavy[t]
@@ -256,11 +269,11 @@
         lax.fori_loop(0, 2, tile, 0)
 
 
-def src_outer_kernel(limit, src, sat, even_in, odd_in, heavy_in, plain_in, heavy, plain, sums, low, high, masks, limits):
+def src_outer_kernel(limit, src, sat, even_in, odd_in, heavy_in, plain_in, heavy, plain, sums, low, high, caps, limits):
     times, lines, cells, depth = src.shape
-    unpack_marks(times, limit, sat, even_in, odd_in, masks, limits)
+    unpack_marks(times, limit, sat, even_in, odd_in, caps, limits)
     unpack_halo(even_in, odd_in, low, high)
-    add_outer(src, [heavy], [plain], low, high, masks, limits)
+    add_outer(src, [heavy], [plain], low, high, caps, limits)
     zero = jnp.zeros((ROWS, depth), jnp.float32)
 
     def add(index, totals):
@@ -274,20 +287,22 @@
         return energy, weighted
 
     energy, weighted = lax.fori_loop(0, cells // PAIR, add, (zero, zero))
-    sums[0:1, :] = jnp.sum(energy, axis=0, keepdims=True)
-    sums[1:2, :] = jnp.sum(weighted, axis=0, keepdims=True)
+    sums[...] = jnp.broadcast_to(
+        jnp.concatenate([jnp.sum(part, axis=0, keepdims=True) for part in (energy, weighted)], axis=0)[None], sums.shape
+    )
 
 
 def rcv_outer_kernel(limit, rcv, sat, even_marks, odd_marks, even_in, odd_in, *refs):
-    parts, (low, high, masks, limits) = refs[len(refs) // 2 - 2 : -4], refs[-4:]
-    unpack_marks(rcv.shape[0], limit, sat, even_marks, odd_marks, masks, limits)
+    parts, (low, high, caps, limits) = refs[len(refs) // 2 - 2 : -4], refs[-4:]
+    unpack_marks(rcv.shape[0], limit, sat, even_marks, odd_marks, caps, limits)
     unpack_halo(even_in, odd_in, low, high)
-    add_outer(rcv, parts[::2], parts[1::2], low, high, masks, limits)
+    add_outer(rcv, parts[::2], parts[1::2], low, high, caps, limits)
 
 
 def combine_kernel(cell_count, sums, src_heavy, src_plain, *refs):
     pieces, (src_out, rcv_out, semblance_out) = refs[:-3], refs[-3:]
-    total = jnp.broadcast_to(jnp.sum(sums[...], axis=1, keepdims=True), sums.shape)
+    total = jnp.sum(sums[...], axis=0)
+    total = jnp.broadcast_to(jnp.sum(total, axis=1, keepdims=True), total.shape)
     energy, weighted = total[0:1], total[1:2]
     semblance = weighted / energy
     inverse_rms = 1.0 / jnp.sqrt(energy / cell_count + EPSILON)
@@ -305,25 +320,6 @@
     for heavy, plain in zip(pieces[::2], pieces[1::2]):
         put(rcv_out, start, heavy, plain)
         start += heavy.shape[2]
-
-
-def ride_kernel(rows_in, sums, rows):
-    count = sums.shape[0]
-    parts, rest = [], sums[...]
-    for _ in range(3):
-        parts.append(rest.astype(jnp.bfloat16).astype(jnp.float32))
-        rest = rest - parts[-1]
-    parts.append(jnp.zeros((LIMIT_ROWS - 3 * count, sums.shape[1]), jnp.float32))
-    below = pl.ds(rows.shape[0] - LIMIT_ROWS, LIMIT_ROWS)
-    rows[below, :] = jnp.concatenate(parts, axis=0).astype(jnp.bfloat16)
-
-
-def sums_below(rows, count):
-    at = rows.shape[0] - LIMIT_ROWS
-    first, second, third = (
-        lax.slice_in_dim(rows, at + i * count, at + (i + 1) * count).astype(jnp.float32) for i in range(3)
-    )
-    return first + second + third
 
 
 def exchanges(size, lines):
@@ -343,16 +339,6 @@
     return routes
 
 
-def reduction_steps(count):
-    assert count & (count - 1) == 0
-    bits = [1 << bit for bit in range(1, count.bit_length() - 1)]
-    groups = [[1]]
-    for at in range(0, len(bits), 2):
-        low, *high = bits[at : at + 2]
-        groups.append([low, high[0], low | high[0]] if high else [low])
-    return groups
-
-
 def local(source_field, receiver_field, sat_mask, offset_range):
     times, lines, cells, depth = source_field.shape
     size = lax.axis_size("inline")
@@ -360,11 +346,10 @@
     image_cells = lines * cells * depth * (2 * H + 1)
     shape = jax.ShapeDtypeStruct
     total = shape((times, lines, cells, depth), jnp.float32)
-    piece = shape((times, lines, cells // PIECES, depth), jnp.float32)
     field_out = shape(source_field.shape, jnp.bfloat16)
     extended = pltpu.VMEM((times, lines, cells + 2 * REACH, depth), jnp.float32)
     edge = pltpu.VMEM((times, lines, ROWS + REACH, depth), jnp.float32)
-    masks = pltpu.VMEM((lines, cells + 2 * H, depth), jnp.float32)
+    caps = pltpu.VMEM((lines, cells + 2 * H, depth), jnp.float32)
     limits = pltpu.VMEM((cells + 2 * H, depth), jnp.float32)
 
     def call(kernel, name, out_shape, operands, scratch=(), share=0.0, aliases={}):
@@ -383,37 +368,27 @@
         )(*operands)
 
     src, rcv, sat = source_field, receiver_field, sat_mask
-    even, odd = payloads(rcv, sat, offset_range)
+    offset_range, even, odd = payloads(rcv, sat, offset_range)
     even_route, odd_route = exchanges(size, lax.axis_size("xline"))
     even = lax.ppermute(even, DEVICES, even_route)
     odd = lax.ppermute(odd, DEVICES, odd_route)
-    low_high = edges(src, 2, REACH)
-    odd_late = lax.ppermute(for_odd(*low_high), DEVICES, odd_route)
-    even_late = lax.ppermute(for_even(*low_high), DEVICES, even_route)
+    odd_late = lax.ppermute(for_odd(*edges(src, 2, REACH)), DEVICES, odd_route)
+
     heavy, plain = call(
-        functools.partial(inner_kernel, 0),
+        inner_kernel,
         "src_inner",
         (total, total),
         (offset_range, src, rcv, sat),
-        [extended, masks],
+        [extended, caps],
         0.85,
     )
-    def piece_at(number, src, rcv):
-        return call(
-            functools.partial(inner_kernel, number * (cells // PIECES)),
-            "rcv_inner",
-            (piece, piece),
-            (offset_range, rcv, src, sat),
-            [extended, masks],
-            0.85 / PIECES,
-        )
-
+    count = size * lax.axis_size("xline")
     heavy, plain, sums = call(
         src_outer_kernel,
         "src_outer",
-        (total, total, shape((2, depth), jnp.float32)),
+        (total, total, shape((count, 2, depth), jnp.float32)),
         (offset_range, src, sat, even, odd, heavy, plain),
-        [edge, edge, masks, limits],
+        [edge, edge, caps, limits],
         0.25,
         {5: 0, 6: 1},
     )
@@ -424,26 +399,38 @@
             "rcv_outer",
             [piece] * len(pieces),
             (offset_range, rcv, sat, even, odd, even_late, odd_late, *pieces),
-            [edge, edge, masks, limits],
+            [edge, edge, caps, limits],
             0.25,
             {7 + i: i for i in range(len(pieces))},
         )
 
-    lines_all = lax.axis_size("xline")
-    count = size * lines_all
-    spread = jnp.broadcast_to(sums[None], (count, *sums.shape))
-    gathered = lax.all_to_all(spread, DEVICES, 0, 0, tiled=True)
+    gathered = lax.all_to_all(sums, DEVICES, 0, 0, tiled=True)
     sums, ahead = lax.optimization_barrier((sums, src))
-    pieces = [part for i in range(PIECES) for part in piece_at(i, ahead, rcv)]
-    pieces = finish(odd_late, even_late, *pieces)
-    sums = jnp.sum(gathered, axis=0)
+    even_late = lax.ppermute(for_even(*edges(ahead, 2, REACH)), DEVICES, even_route)
+    pieces = call(
+        inner_kernel,
+        "rcv_inner",
+        (total, total),
+        (offset_range, rcv, ahead, sat),
+        [extended, caps],
+        0.85,
+    )
+    pieces = call(
+        rcv_outer_kernel,
+        "rcv_outer",
+        (total, total),
+        (offset_range, rcv, sat, even, odd, even_late, odd_late, *pieces),
+        [edge, edge, caps, limits],
+        0.25,
+        {7: 0, 8: 1},
+    )
 
     cell_count = float(lines * lax.axis_size("xline") * cells * size * depth * (2 * H + 1))
     src_adj, rcv_adj, semblance = call(
         functools.partial(combine_kernel, cell_count),
         "combine",
         (field_out, field_out, shape((1, depth), jnp.float32)),
-        (sums, heavy, plain, *pieces),
+        (gathered, heavy, plain, *pieces),
     )
     return src_adj, rcv_adj, semblance[0, 0]
 

time: 28.2 us -> 29 us (1.028); the launches traced: 28.4 us -> 28.8 us
  Pallas kernels: 9.29 us -> 11.6 us
  waiting for transfers between devices: 4.85 us -> 2.79 us
  starting transfers between devices: 10.9 us -> 11.7 us
  local copies, waits for them, and re-layouts: 0.72 us -> 0.09 us
    ppermute x2, starting transfers between devices: 0.14 us -> 2.58 us  [the longest x1 2.51 us: local(): lax.ppermute(for_even(*edges(ahead, 2, REACH)), DEVICES, even_route)]
    pallas_call x8 -> x5, Pallas kernels: 9.29 us -> 11.6 us  [call(): pl.pallas_call(kernel, out_shape=out_shape, in_specs=[SMEM if operand is...]
    all_to_all x1, starting transfers between devices: 6.31 us -> 4.67 us  [local(): gathered = lax.all_to_all(sums, DEVICES, 0, 0, tiled=True)]
    ppermute x1, waiting for transfers between devices: 1.94 us -> 0.6 us  [local(): even = lax.ppermute(even, DEVICES, even_route)]
    all_to_all x1, waiting for transfers between devices: 2.91 us -> 2.19 us  [local(): gathered = lax.all_to_all(sums, DEVICES, 0, 0, tiled=True)]
    broadcast_in_dim x1 -> x0, local copies, waits for them, and re-layouts: 0.62 us -> none  [local(): spread = jnp.broadcast_to(sums[None], (count, *sums.shape))]
    select_n x3 -> x4, other arithmetic: 0.94 us -> 0.95 us  [for_even(): return jnp.where(lax.axis_index('inline') % 2 == 0, high, low)]
  transfers between devices with their start and end apart: 5 -> 5, of which waited for: 2 -> 2; matrix products, arithmetic and copies ran while one was open for 2% -> 0% of each run, Pallas kernels for 30% -> 37%
where the time goes in v4:
time: 29 us; the launch traced here: 28.8 us
  starting transfers between devices  11.7 us (40%)
  Pallas kernels  11.6 us (40%)
  waiting for transfers between devices  2.79 us (10%)
  between operations  1.43 us (5%)
  other arithmetic  1.07 us (4%)
    pallas_call x5, Pallas kernels, call(): pl.pallas_call(kernel, out_shape=out_shape, in_specs=[SMEM if operand is...  11.6 us
    all_to_all x1, starting transfers between devices, local(): gathered = lax.all_to_all(sums, DEVICES, 0, 0, tiled=True)  4.67 us
    ppermute x1, starting transfers between devices, local(): even = lax.ppermute(even, DEVICES, even_route)  3.98 us
    ppermute x1, starting transfers between devices, local(): lax.ppermute(for_even(*edges(ahead, 2, REACH)), DEVICES, even_route)  2.51 us
    all_to_all x1, waiting for transfers between devices, local(): gathered = lax.all_to_all(sums, DEVICES, 0, 0, tiled=True)  2.19 us
    select_n x4, other arithmetic, for_even(): return jnp.where(lax.axis_index('inline') % 2 == 0, high, low)  0.95 us
    ppermute x1, waiting for transfers between devices, local(): even = lax.ppermute(even, DEVICES, even_route)  0.6 us
  transfers between devices with their start and end apart: 5, of which 2 were waited for; matrix products, arithmetic and copies ran while one was open for 0% of the time, Pallas kernels for 37%

profile of v4, /device:TPU:0, one launch (start us, length us, event | category | flops | bytes accessed | tf_op | source)
XLA Modules:
  0.0 28.8 jit_solution(1710986817797828282)
XLA Ops:
  1.3 0.0 copy-start.2
  1.3 0.9 %broadcast_select_fusion = (bf16[4,1,64,128]{3,2,1,0:T(8,128)(2,1)S(1)}, bf16[4,1,64,128]{3,2,1,0:T(8,128)(2,1)S(1)}) fusion(pred[]{:T(512)S(6)} %eq.15, bf16[4,1,128,128]{3,2,1,0:T(8,128)(2,1)} %rcv.1), kind=kLoop, calls=%fused_computation.5 | loop fusion | flops 65536 | bytes 262145 | tf_op jit(solution)/shard_map/jit(_where)/select_n | solution.py:64
  2.2 0.0 copy-done.2
  2.3 0.1 pad.5.clone
  2.4 0.0 copy-start
  2.4 0.1 maximum_maximum_fusion.1
  2.5 0.0 copy-start.1
  2.5 0.5 %collective-permute-start.1 = (bf16[304,128]{1,0:T(8,128)(2,1)S(1)}, bf16[304,128]{1,0:T(8,128)(2,1)S(1)}, u32[]{:S(2)}, u32[]{:S(2)}) collective-permute-start(bf16[304,128]{1,0:T(8,128)(2,1)S(1)} %get-tuple-element.41), channel_id=1, source_target_pairs={{0,1},{1,0},{2,4},{3,5},{4,2},{5,3},{6,8},{7,9},{8,6},{9,7},{10,12... | collective-permute-start | bytes 233480 | tf_op jit(solution)/shard_map/ppermute | solution.py:374
  3.0 4.0 %collective-permute-start = (bf16[304,128]{1,0:T(8,128)(2,1)S(1)}, bf16[304,128]{1,0:T(8,128)(2,1)S(1)}, u32[]{:S(2)}, u32[]{:S(2)}) collective-permute-start(bf16[304,128]{1,0:T(8,128)(2,1)S(1)} %get-tuple-element.42), channel_id=1, source_target_pairs={{0,2},{1,3},{2,0},{3,1},{4,6},{5,7},{6,4},{7,5},{8,10},{9,11},{10,... | collective-permute-start | bytes 233480 | tf_op jit(solution)/shard_map/ppermute | solution.py:373
  7.0 0.0 copy-done
  7.0 0.1 collective-permute-start.3
  7.1 0.0 copy-done.1
  7.1 3.7 %src_inner.1 = (f32[4,1,128,128]{3,2,1,0:T(8,128)S(1)}, f32[4,1,128,128]{3,2,1,0:T(8,128)S(1)}) custom-call(s32[1]{0:T(128)S(6)} %copy.15.limit, bf16[4,1,128,128]{3,2,1,0:T(8,128)(2,1)S(1)} %copy-done, bf16[4,1,128,128]{3,2,1,0:T(8,128)(2,1)S(1)} %copy-done.1, s32[1,128,128]{2,1,0:T(8,128)S(1)} %copy-done.2), custom_call_target="tpu_custom_call" | custom-call | flops 21725184 | bytes 1048576 | tf_op jit(solution)/shard_map/src_inner/pallas_call | solution.py:356
  10.8 0.0 collective-permute-done.1.odd_in.odd_marks
  10.8 0.6 %collective-permute-done.even_in.even_marks = bf16[304,128]{1,0:T(8,128)(2,1)S(1)} collective-permute-done((bf16[304,128]{1,0:T(8,128)(2,1)S(1)}, bf16[304,128]{1,0:T(8,128)(2,1)S(1)}, u32[]{:S(2)}, u32[]{:S(2)}) %collective-permute-start) | collective-permute-done | bytes 77856 | tf_op jit(solution)/shard_map/ppermute | solution.py:373
  11.4 2.0 %src_outer.1 = (f32[4,1,128,128]{3,2,1,0:T(8,128)S(1)}, f32[4,1,128,128]{3,2,1,0:T(8,128)S(1)}, f32[32,2,128]{2,1,0:T(2,128)}) custom-call(s32[1]{0:T(128)S(6)} %copy.15.limit, bf16[4,1,128,128]{3,2,1,0:T(8,128)(2,1)S(1)} %copy-done, s32[1,128,128]{2,1,0:T(8,128)S(1)} %copy-done.2, ...), custom_call_target="tpu_custom_call", output_to_operand_aliasing={{0}: (5, {}), {1}: (6, {})} | custom-call | flops 6389760 | bytes 1048576 | tf_op jit(solution)/shard_map/src_outer/pallas_call | solution.py:356
  13.5 2.5 %collective-permute-start.2 = (bf16[256,128]{1,0:T(8,128)(2,1)S(1)}, bf16[256,128]{1,0:T(8,128)(2,1)S(1)}, u32[]{:S(2)}, u32[]{:S(2)}) collective-permute-start(bf16[256,128]{1,0:T(8,128)(2,1)S(1)} %bitcast.14), channel_id=1, source_target_pairs={{0,2},{1,3},{2,0},{3,1},{4,6},{5,7},{6,4},{7,5},{8,10},{9,11},{10,... | collective-permute-start | bytes 196616 | tf_op jit(solution)/shard_map/ppermute | solution.py:409
  16.0 4.7 %all-to-all-start = ((f32[32,2,128]{2,1,0:T(2,128)}), f32[32,2,128]{2,1,0:T(2,128)S(1)}, u32[]{:S(2)}, u32[]{:S(2)}) async-start(f32[32,2,128]{2,1,0:T(2,128)} %get-tuple-element.26), calls=%async_computation | async-start | bytes 65536 | tf_op jit(solution)/shard_map/all_to_all | solution.py:407
  20.7 3.7 %rcv_inner.1 = (f32[4,1,128,128]{3,2,1,0:T(8,128)S(1)}, f32[4,1,128,128]{3,2,1,0:T(8,128)S(1)}) custom-call(s32[1]{0:T(128)S(6)} %copy.15.limit, bf16[4,1,128,128]{3,2,1,0:T(8,128)(2,1)S(1)} %copy-done.1, bf16[4,1,128,128]{3,2,1,0:T(8,128)(2,1)S(1)} %copy-done, s32[1,128,128]{2,1,0:T(8,128)S(1)} %copy-done.2), custom_call_target="tpu_custom_call" | custom-call | flops 21725184 | bytes 1048576 | tf_op jit(solution)/shard_map/rcv_inner/pallas_call | solution.py:356
  24.4 0.0 collective-permute-done.3.odd_in
  24.4 0.0 collective-permute-done.2.even_in
  24.4 1.3 %rcv_outer.1 = (f32[4,1,128,128]{3,2,1,0:T(8,128)S(1)}, f32[4,1,128,128]{3,2,1,0:T(8,128)S(1)}) custom-call(s32[1]{0:T(128)S(6)} %copy.15.limit, bf16[4,1,128,128]{3,2,1,0:T(8,128)(2,1)S(1)} %copy-done.1, s32[1,128,128]{2,1,0:T(8,128)S(1)} %copy-done.2, ...), custom_call_target="tpu_custom_call", output_to_operand_aliasing={{0}: (7, {}), {1}: (8, {})} | custom-call | flops 6389760 | bytes 1048576 | tf_op jit(solution)/shard_map/rcv_outer/pallas_call | solution.py:356
  25.7 2.2 %all-to-all-done.sums = f32[32,2,128]{2,1,0:T(2,128)S(1)} async-done(((f32[32,2,128]{2,1,0:T(2,128)}), f32[32,2,128]{2,1,0:T(2,128)S(1)}, u32[]{:S(2)}, u32[]{:S(2)}) %all-to-all-start) | async-done | bytes 32800 | tf_op jit(solution)/shard_map/all_to_all | solution.py:407
  27.9 0.9 %combine.1 = (bf16[4,1,128,128]{3,2,1,0:T(8,128)(2,1)}, bf16[4,1,128,128]{3,2,1,0:T(8,128)(2,1)}, f32[1,128]{1,0:T(1,128)}) custom-call(f32[32,2,128]{2,1,0:T(2,128)S(1)} %all-to-all-done.sums, f32[4,1,128,128]{3,2,1,0:T(8,128)S(1)} %get-tuple-element.27.src_heavy, f32[4,1,128,128]{3,2,1,0:T(8,128)S(1)} %get-tuple-element.28.src_plain, ...), custom_call_target="tpu_custom_call" | custom-call | bytes 1048576 | tf_op jit(solution)/shard_map/combine/pallas_call | solution.py:356
  (5 shorter events, 0.0 us)
Async XLA Ops:
  1.3 0.9 %copy-start.2 = (s32[1,128,128]{2,1,0:T(8,128)S(1)}, s32[1,128,128]{2,1,0:T(8,128)}, u32[]{:S(2)}) copy-start(s32[1,128,128]{2,1,0:T(8,128)} %sat.7) | copy-start | bytes 196612
  2.4 4.6 %copy-start = (bf16[4,1,128,128]{3,2,1,0:T(8,128)(2,1)S(1)}, bf16[4,1,128,128]{3,2,1,0:T(8,128)(2,1)}, u32[]{:S(2)}) copy-start(bf16[4,1,128,128]{3,2,1,0:T(8,128)(2,1)} %field.2) | copy-start | bytes 393220
  2.5 4.6 %copy-start.1 = (bf16[4,1,128,128]{3,2,1,0:T(8,128)(2,1)S(1)}, bf16[4,1,128,128]{3,2,1,0:T(8,128)(2,1)}, u32[]{:S(2)}) copy-start(bf16[4,1,128,128]{3,2,1,0:T(8,128)(2,1)} %rcv.1) | copy-start | bytes 393220
  2.5 8.3 %collective-permute-start.1 = (bf16[304,128]{1,0:T(8,128)(2,1)S(1)}, bf16[304,128]{1,0:T(8,128)(2,1)S(1)}, u32[]{:S(2)}, u32[]{:S(2)}) collective-permute-start(bf16[304,128]{1,0:T(8,128)(2,1)S(1)} %get-tuple-element.41), channel_id=1, source_target_pairs={{0,1},{1,0},{2,4},{3,5},{4,2},{5,3},{6,8},{7,9},{8,6},{9,7},{10,12... | collective-permute-start | bytes 233480 | tf_op jit(solution)/shard_map/ppermute | solution.py:374
  3.0 8.4 %collective-permute-start = (bf16[304,128]{1,0:T(8,128)(2,1)S(1)}, bf16[304,128]{1,0:T(8,128)(2,1)S(1)}, u32[]{:S(2)}, u32[]{:S(2)}) collective-permute-start(bf16[304,128]{1,0:T(8,128)(2,1)S(1)} %get-tuple-element.42), channel_id=1, source_target_pairs={{0,2},{1,3},{2,0},{3,1},{4,6},{5,7},{6,4},{7,5},{8,10},{9,11},{10,... | collective-permute-start | bytes 233480 | tf_op jit(solution)/shard_map/ppermute | solution.py:373
  7.0 17.4 %collective-permute-start.3 = (bf16[256,128]{1,0:T(8,128)(2,1)S(1)}, bf16[256,128]{1,0:T(8,128)(2,1)S(1)}, u32[]{:S(2)}, u32[]{:S(2)}) collective-permute-start(bf16[256,128]{1,0:T(8,128)(2,1)S(1)} %bitcast.13), channel_id=1, source_target_pairs={{0,1},{1,0},{2,4},{3,5},{4,2},{5,3},{6,8},{7,9},{8,6},{9,7},{10,12... | collective-permute-start | bytes 196616 | tf_op jit(solution)/shard_map/ppermute | solution.py:375
  13.5 10.9 %collective-permute-start.2 = (bf16[256,128]{1,0:T(8,128)(2,1)S(1)}, bf16[256,128]{1,0:T(8,128)(2,1)S(1)}, u32[]{:S(2)}, u32[]{:S(2)}) collective-permute-start(bf16[256,128]{1,0:T(8,128)(2,1)S(1)} %bitcast.14), channel_id=1, source_target_pairs={{0,2},{1,3},{2,0},{3,1},{4,6},{5,7},{6,4},{7,5},{8,10},{9,11},{10,... | collective-permute-start | bytes 196616 | tf_op jit(solution)/shard_map/ppermute | solution.py:409
  16.0 11.9 %all-to-all-start = ((f32[32,2,128]{2,1,0:T(2,128)}), f32[32,2,128]{2,1,0:T(2,128)S(1)}, u32[]{:S(2)}, u32[]{:S(2)}) async-start(f32[32,2,128]{2,1,0:T(2,128)} %get-tuple-element.26), calls=%async_computation | async-start | bytes 65536 | tf_op jit(solution)/shard_map/all_to_all | solution.py:407

commit v5 on v4

--- a/solution.py
+++ b/solution.py
@@ -176,40 +176,24 @@
             for half, center in enumerate(tiles_of(middle, y, base)):
                 at = base + half * ROWS
 
-                def add(offsets, masked, sums):
+                def add(offsets, sums):
                     return accumulate(
                         center,
                         sums,
                         offsets,
                         lambda h: [shifted[t, y, pl.ds(at + REACH + 2 * h, ROWS), :] for t in range(times)],
-                        lambda image, h: image * inside[abs(h)] if masked else image,
+                        lambda image, h: image * inside[abs(h)] if abs(h) > ALWAYS else image,
                         lambda h: caps[y, pl.ds(at + H + h, ROWS), :],
                     )
 
-                sums = add(paired(ALWAYS), False, ([zero] * times, [zero] * times))
-                for low in range(ALWAYS + 1, H + 1, GROUP):
-                    high = min(low + GROUP - 1, H)
-                    if high <= SHARED:
-                        parts = [(paired(high, low), limit[0] >= low)]
-                    else:
-                        below = base + PAIR - 1 - 2 * low >= 0
-                        above = base + 2 * low < cells
-                        parts = [
-                            ([sign * size for size in range(low, high + 1)], jnp.logical_and(reach, limit[0] >= low))
-                            for sign, reach in ((-1, below), (1, above))
-                        ]
-                    for offsets, needed in parts:
-                        sums = lax.cond(
-                            needed,
-                            lambda sums: lax.cond(
-                                limit[0] >= high,
-                                functools.partial(add, offsets, False),
-                                functools.partial(add, offsets, True),
-                                sums,
-                            ),
-                            lambda kept: kept,
-                            sums,
-                        )
+                sums = add(paired(SHARED), ([zero] * times, [zero] * times))
+                for low in range(SHARED + 1, H + 1, GROUP):
+                    below = base + PAIR - 1 - 2 * low >= 0
+                    above = base + 2 * low < cells
+                    for sign, reach in ((-1, below), (1, above)):
+                        offsets = [sign * size for size in range(low, min(low + GROUP, H + 1))]
+                        needed = jnp.logical_and(reach, limit[0] >= low)
+                        sums = lax.cond(needed, functools.partial(add, offsets), lambda kept: kept, sums)
                 heavy, plain = sums
                 rows = pl.ds(base + half * ROWS, ROWS)
                 for t in range(times):
@@ -372,8 +356,6 @@
     even_route, odd_route = exchanges(size, lax.axis_size("xline"))
     even = lax.ppermute(even, DEVICES, even_route)
     odd = lax.ppermute(odd, DEVICES, odd_route)
-    odd_late = lax.ppermute(for_odd(*edges(src, 2, REACH)), DEVICES, odd_route)
-
     heavy, plain = call(
         inner_kernel,
         "src_inner",
@@ -382,6 +364,10 @@
         [extended, caps],
         0.85,
     )
+    (heavy, plain), ahead = lax.optimization_barrier(((heavy, plain), src))
+    low_high = edges(ahead, 2, REACH)
+    odd_late = lax.ppermute(for_odd(*low_high), DEVICES, odd_route)
+    even_late = lax.ppermute(for_even(*low_high), DEVICES, even_route)
     count = size * lax.axis_size("xline")
     heavy, plain, sums = call(
         src_outer_kernel,
@@ -405,8 +391,7 @@
         )
 
     gathered = lax.all_to_all(sums, DEVICES, 0, 0, tiled=True)
-    sums, ahead = lax.optimization_barrier((sums, src))
-    even_late = lax.ppermute(for_even(*edges(ahead, 2, REACH)), DEVICES, even_route)
+    sums, ahead, odd_late, even_late = lax.optimization_barrier((sums, src, odd_late, even_late))
     pieces = call(
         inner_kernel,
         "rcv_inner",

time: 29 us -> 27.7 us (0.955)
  Pallas kernels: 11.6 us -> 7.92 us
  waiting for transfers between devices: 2.79 us -> 4.05 us
  starting transfers between devices: 11.7 us -> 12.9 us
    pallas_call x5, Pallas kernels: 11.6 us -> 7.92 us  [call(): pl.pallas_call(kernel, out_shape=out_shape, in_specs=[SMEM if operand is...]
    all_to_all x1, waiting for transfers between devices: 2.19 us -> 4.04 us  [local(): gathered = lax.all_to_all(sums, DEVICES, 0, 0, tiled=True)]
    all_to_all x1, starting transfers between devices: 4.67 us -> 5.41 us  [local(): gathered = lax.all_to_all(sums, DEVICES, 0, 0, tiled=True)]
    ppermute x1, waiting for transfers between devices: 0.6 us -> 0.01 us  [local(): even = lax.ppermute(even, DEVICES, even_route)]
    ppermute x2, starting transfers between devices: 2.58 us -> 3.04 us  [the longest x1 2.97 us: local(): even_late = lax.ppermute(for_even(*low_high), DEVICES, even_route)]
    select_n x4 -> x3, other arithmetic: 0.95 us -> 0.95 us  [for_even(): return jnp.where(lax.axis_index('inline') % 2 == 0, high, low)]
  transfers between devices with their start and end apart: 5 -> 5, of which waited for: 2 -> 1; matrix products, arithmetic and copies ran while one was open for 0% -> 0% of each run, Pallas kernels for 37% -> 26%
where the time goes in v5:
time: 27.7 us; the launch traced here: 27.5 us
  starting transfers between devices  12.9 us (47%)
  Pallas kernels  7.92 us (29%)
  waiting for transfers between devices  4.05 us (15%)
  between operations  1.41 us (5%)
  other arithmetic  1.06 us (4%)
    pallas_call x5, Pallas kernels, call(): pl.pallas_call(kernel, out_shape=out_shape, in_specs=[SMEM if operand is...  7.92 us
    all_to_all x1, starting transfers between devices, local(): gathered = lax.all_to_all(sums, DEVICES, 0, 0, tiled=True)  5.41 us
    all_to_all x1, waiting for transfers between devices, local(): gathered = lax.all_to_all(sums, DEVICES, 0, 0, tiled=True)  4.04 us
    ppermute x1, starting transfers between devices, local(): even = lax.ppermute(even, DEVICES, even_route)  3.98 us
    ppermute x1, starting transfers between devices, local(): even_late = lax.ppermute(for_even(*low_high), DEVICES, even_route)  2.97 us
    select_n x3, other arithmetic, for_even(): return jnp.where(lax.axis_index('inline') % 2 == 0, high, low)  0.95 us
  transfers between devices with their start and end apart: 5, of which 1 were waited for; matrix products, arithmetic and copies ran while one was open for 0% of the time, Pallas kernels for 26%

profile of v5, /device:TPU:0, one launch (start us, length us, event | category | flops | bytes accessed | tf_op | source)
XLA Modules:
  0.0 27.5 jit_solution(9431951942181641291)
XLA Ops:
  1.3 0.0 copy-start.2
  1.3 0.9 %broadcast_select_fusion.2 = (bf16[4,1,64,128]{3,2,1,0:T(8,128)(2,1)S(1)}, bf16[4,1,64,128]{3,2,1,0:T(8,128)(2,1)S(1)}) fusion(pred[]{:T(512)S(6)} %eq.15, bf16[4,1,128,128]{3,2,1,0:T(8,128)(2,1)} %rcv.1), kind=kLoop, calls=%fused_computation.5 | loop fusion | flops 65536 | bytes 262145 | tf_op jit(solution)/shard_map/jit(_where)/select_n | solution.py:64
  2.2 0.0 copy-done.2
  2.3 0.1 pad.5.clone
  2.4 0.0 copy-start
  2.4 0.0 copy-start.1
  2.4 0.1 maximum_maximum_fusion.1
  2.5 0.5 %collective-permute-start.1 = (bf16[304,128]{1,0:T(8,128)(2,1)S(1)}, bf16[304,128]{1,0:T(8,128)(2,1)S(1)}, u32[]{:S(2)}, u32[]{:S(2)}) collective-permute-start(bf16[304,128]{1,0:T(8,128)(2,1)S(1)} %get-tuple-element.53), channel_id=1, source_target_pairs={{0,1},{1,0},{2,4},{3,5},{4,2},{5,3},{6,8},{7,9},{8,6},{9,7},{10,12... | collective-permute-start | bytes 233480 | tf_op jit(solution)/shard_map/ppermute | solution.py:358
  3.0 4.0 %collective-permute-start = (bf16[304,128]{1,0:T(8,128)(2,1)S(1)}, bf16[304,128]{1,0:T(8,128)(2,1)S(1)}, u32[]{:S(2)}, u32[]{:S(2)}) collective-permute-start(bf16[304,128]{1,0:T(8,128)(2,1)S(1)} %get-tuple-element.54), channel_id=1, source_target_pairs={{0,2},{1,3},{2,0},{3,1},{4,6},{5,7},{6,4},{7,5},{8,10},{9,11},{10,... | collective-permute-start | bytes 233480 | tf_op jit(solution)/shard_map/ppermute | solution.py:357
  7.0 0.0 copy-done
  7.0 0.0 copy-done.1
  7.0 1.9 %src_inner.1 = (f32[4,1,128,128]{3,2,1,0:T(8,128)S(1)}, f32[4,1,128,128]{3,2,1,0:T(8,128)S(1)}) custom-call(s32[1]{0:T(128)S(6)} %copy.15.limit, bf16[4,1,128,128]{3,2,1,0:T(8,128)(2,1)S(1)} %copy-done.1, bf16[4,1,128,128]{3,2,1,0:T(8,128)(2,1)S(1)} %copy-done, s32[1,128,128]{2,1,0:T(8,128)S(1)} %copy-done.2), custom_call_target="tpu_custom_call" | custom-call | flops 21725184 | bytes 1048576 | tf_op jit(solution)/shard_map/src_inner/pallas_call | solution.py:340
  8.9 0.1 collective-permute-start.2
  8.9 3.0 %collective-permute-start.3 = (bf16[256,128]{1,0:T(8,128)(2,1)S(1)}, bf16[256,128]{1,0:T(8,128)(2,1)S(1)}, u32[]{:S(2)}, u32[]{:S(2)}) collective-permute-start(bf16[256,128]{1,0:T(8,128)(2,1)S(1)} %bitcast.13), channel_id=1, source_target_pairs={{0,2},{1,3},{2,0},{3,1},{4,6},{5,7},{6,4},{7,5},{8,10},{9,11},{10,... | collective-permute-start | bytes 196616 | tf_op jit(solution)/shard_map/ppermute | solution.py:370
  11.9 0.0 collective-permute-done.1.odd_in.odd_marks
  11.9 0.0 collective-permute-done.even_in.even_marks
  11.9 2.0 %src_outer.1 = (f32[4,1,128,128]{3,2,1,0:T(8,128)S(1)}, f32[4,1,128,128]{3,2,1,0:T(8,128)S(1)}, f32[32,2,128]{2,1,0:T(2,128)}) custom-call(s32[1]{0:T(128)S(6)} %copy.15.limit, bf16[4,1,128,128]{3,2,1,0:T(8,128)(2,1)S(1)} %copy-done.1, s32[1,128,128]{2,1,0:T(8,128)S(1)} %copy-done.2, ...), custom_call_target="tpu_custom_call", output_to_operand_aliasing={{0}: (5, {}), {1}: (6, {})} | custom-call | flops 6389760 | bytes 1048576 | tf_op jit(solution)/shard_map/src_outer/pallas_call | solution.py:340
  14.0 5.4 %all-to-all-start = ((f32[32,2,128]{2,1,0:T(2,128)}), f32[32,2,128]{2,1,0:T(2,128)S(1)}, u32[]{:S(2)}, u32[]{:S(2)}) async-start(f32[32,2,128]{2,1,0:T(2,128)} %get-tuple-element.33), calls=%async_computation | async-start | bytes 65536 | tf_op jit(solution)/shard_map/all_to_all | solution.py:393
  19.4 0.0 collective-permute-done.2.odd_in
  19.4 0.0 collective-permute-done.3.even_in
  19.4 1.9 %rcv_inner.1 = (f32[4,1,128,128]{3,2,1,0:T(8,128)S(1)}, f32[4,1,128,128]{3,2,1,0:T(8,128)S(1)}) custom-call(s32[1]{0:T(128)S(6)} %copy.15.limit, bf16[4,1,128,128]{3,2,1,0:T(8,128)(2,1)S(1)} %copy-done, bf16[4,1,128,128]{3,2,1,0:T(8,128)(2,1)S(1)} %copy-done.1, s32[1,128,128]{2,1,0:T(8,128)S(1)} %copy-done.2), custom_call_target="tpu_custom_call" | custom-call | flops 21725184 | bytes 1048576 | tf_op jit(solution)/shard_map/rcv_inner/pallas_call | solution.py:340
  21.3 1.3 %rcv_outer.1 = (f32[4,1,128,128]{3,2,1,0:T(8,128)S(1)}, f32[4,1,128,128]{3,2,1,0:T(8,128)S(1)}) custom-call(s32[1]{0:T(128)S(6)} %copy.15.limit, bf16[4,1,128,128]{3,2,1,0:T(8,128)(2,1)S(1)} %copy-done, s32[1,128,128]{2,1,0:T(8,128)S(1)} %copy-done.2, ...), custom_call_target="tpu_custom_call", output_to_operand_aliasing={{0}: (7, {}), {1}: (8, {})} | custom-call | flops 6389760 | bytes 1048576 | tf_op jit(solution)/shard_map/rcv_outer/pallas_call | solution.py:340
  22.6 4.0 %all-to-all-done.sums = f32[32,2,128]{2,1,0:T(2,128)S(1)} async-done(((f32[32,2,128]{2,1,0:T(2,128)}), f32[32,2,128]{2,1,0:T(2,128)S(1)}, u32[]{:S(2)}, u32[]{:S(2)}) %all-to-all-start) | async-done | bytes 32800 | tf_op jit(solution)/shard_map/all_to_all | solution.py:393
  26.6 0.9 %combine.1 = (bf16[4,1,128,128]{3,2,1,0:T(8,128)(2,1)}, bf16[4,1,128,128]{3,2,1,0:T(8,128)(2,1)}, f32[1,128]{1,0:T(1,128)}) custom-call(f32[32,2,128]{2,1,0:T(2,128)S(1)} %all-to-all-done.sums, f32[4,1,128,128]{3,2,1,0:T(8,128)S(1)} %get-tuple-element.34.src_heavy, f32[4,1,128,128]{3,2,1,0:T(8,128)S(1)} %get-tuple-element.35.src_plain, ...), custom_call_target="tpu_custom_call" | custom-call | bytes 1048576 | tf_op jit(solution)/shard_map/combine/pallas_call | solution.py:340
  (4 shorter events, 0.0 us)
Async XLA Ops:
  1.3 0.9 %copy-start.2 = (s32[1,128,128]{2,1,0:T(8,128)S(1)}, s32[1,128,128]{2,1,0:T(8,128)}, u32[]{:S(2)}) copy-start(s32[1,128,128]{2,1,0:T(8,128)} %sat.7) | copy-start | bytes 196612
  2.4 4.6 %copy-start = (bf16[4,1,128,128]{3,2,1,0:T(8,128)(2,1)S(1)}, bf16[4,1,128,128]{3,2,1,0:T(8,128)(2,1)}, u32[]{:S(2)}) copy-start(bf16[4,1,128,128]{3,2,1,0:T(8,128)(2,1)} %rcv.1) | copy-start | bytes 393220
  2.4 4.6 %copy-start.1 = (bf16[4,1,128,128]{3,2,1,0:T(8,128)(2,1)S(1)}, bf16[4,1,128,128]{3,2,1,0:T(8,128)(2,1)}, u32[]{:S(2)}) copy-start(bf16[4,1,128,128]{3,2,1,0:T(8,128)(2,1)} %field.2) | copy-start | bytes 393220
  2.5 9.4 %collective-permute-start.1 = (bf16[304,128]{1,0:T(8,128)(2,1)S(1)}, bf16[304,128]{1,0:T(8,128)(2,1)S(1)}, u32[]{:S(2)}, u32[]{:S(2)}) collective-permute-start(bf16[304,128]{1,0:T(8,128)(2,1)S(1)} %get-tuple-element.53), channel_id=1, source_target_pairs={{0,1},{1,0},{2,4},{3,5},{4,2},{5,3},{6,8},{7,9},{8,6},{9,7},{10,12... | collective-permute-start | bytes 233480 | tf_op jit(solution)/shard_map/ppermute | solution.py:358
  3.0 8.9 %collective-permute-start = (bf16[304,128]{1,0:T(8,128)(2,1)S(1)}, bf16[304,128]{1,0:T(8,128)(2,1)S(1)}, u32[]{:S(2)}, u32[]{:S(2)}) collective-permute-start(bf16[304,128]{1,0:T(8,128)(2,1)S(1)} %get-tuple-element.54), channel_id=1, source_target_pairs={{0,2},{1,3},{2,0},{3,1},{4,6},{5,7},{6,4},{7,5},{8,10},{9,11},{10,... | collective-permute-start | bytes 233480 | tf_op jit(solution)/shard_map/ppermute | solution.py:357
  8.9 10.5 %collective-permute-start.2 = (bf16[256,128]{1,0:T(8,128)(2,1)S(1)}, bf16[256,128]{1,0:T(8,128)(2,1)S(1)}, u32[]{:S(2)}, u32[]{:S(2)}) collective-permute-start(bf16[256,128]{1,0:T(8,128)(2,1)S(1)} %bitcast.14), channel_id=1, source_target_pairs={{0,1},{1,0},{2,4},{3,5},{4,2},{5,3},{6,8},{7,9},{8,6},{9,7},{10,12... | collective-permute-start | bytes 196616 | tf_op jit(solution)/shard_map/ppermute | solution.py:369
  8.9 10.4 %collective-permute-start.3 = (bf16[256,128]{1,0:T(8,128)(2,1)S(1)}, bf16[256,128]{1,0:T(8,128)(2,1)S(1)}, u32[]{:S(2)}, u32[]{:S(2)}) collective-permute-start(bf16[256,128]{1,0:T(8,128)(2,1)S(1)} %bitcast.13), channel_id=1, source_target_pairs={{0,2},{1,3},{2,0},{3,1},{4,6},{5,7},{6,4},{7,5},{8,10},{9,11},{10,... | collective-permute-start | bytes 196616 | tf_op jit(solution)/shard_map/ppermute | solution.py:370
  14.0 12.7 %all-to-all-start = ((f32[32,2,128]{2,1,0:T(2,128)}), f32[32,2,128]{2,1,0:T(2,128)S(1)}, u32[]{:S(2)}, u32[]{:S(2)}) async-start(f32[32,2,128]{2,1,0:T(2,128)} %get-tuple-element.33), calls=%async_computation | async-start | bytes 65536 | tf_op jit(solution)/shard_map/all_to_all | solution.py:393

commit v6 on v5

--- a/solution.py
+++ b/solution.py
@@ -34,7 +34,8 @@
 
 def payload_layout(times, lines):
     mask_at = times * lines * REACH
-    return mask_at, mask_at + lines * H
+    limit_at = mask_at + lines * H
+    return mask_at, limit_at, limit_at + LIMIT_ROWS
 
 
 def by_parity(even, odd, work):
@@ -68,20 +69,20 @@
     return for_even(high, low)
 
 
-def payloads(rcv, sat, limit):
+def payloads(src, rcv, sat, limit):
     depth = rcv.shape[-1]
     rows = edges(rcv, 2, REACH)
     rows = for_even(*rows), for_odd(*rows)
-    *rows, sat, limit = lax.optimization_barrier((*rows, sat, limit))
+    *rows, sat, src, limit = lax.optimization_barrier((*rows, sat, src, limit))
     masks = edges((sat != 0).astype(jnp.bfloat16), 1, H)
     limits = jnp.full((LIMIT_ROWS, depth), limit[0]).astype(jnp.bfloat16)
-    even = jnp.concatenate([rows[0], for_even(*masks), limits], axis=0)
-    return limit, even, jnp.concatenate([rows[1], for_odd(*masks), limits], axis=0)
+    odd = jnp.concatenate([rows[1], for_odd(*masks), limits], axis=0)
+    return limit, jnp.concatenate([rows[0], for_even(*masks), limits, for_even(*edges(src, 2, REACH))], axis=0), odd
 
 
 def unpack_marks(times, limit, sat, even_in, odd_in, caps, limits):
     lines, cells, depth = sat.shape
-    mask_at, limit_at = payload_layout(times, lines)
+    mask_at, limit_at, _ = payload_layout(times, lines)
 
     def halo(arrived, low, there):
         row_at = 0 if low else H + cells
@@ -97,15 +98,16 @@
     limits[pl.ds(H, cells), :] = jnp.full((cells, depth), limit[0], jnp.int32).astype(jnp.float32)
 
 
-def unpack_halo(even_in, odd_in, low_out, high_out):
+def unpack_halo(even_in, even_at, odd_in, odd_at, low_out, high_out):
     times, lines, _, depth = low_out.shape
     blank = jnp.zeros((ROWS, depth), jnp.float32)
 
     def halo(arrived, low, there):
         out, field_at, blank_at = (low_out, 0, REACH) if low else (high_out, ROWS, 0)
+        start = even_at if arrived is even_in else odd_at
         for t in range(times):
             for y in range(lines):
-                at = (t * lines + y) * REACH
+                at = start + (t * lines + y) * REACH
                 out[t, y, pl.ds(field_at, REACH), :] = arrived[pl.ds(at, REACH), :].astype(jnp.float32) * there
                 out[t, y, pl.ds(blank_at, ROWS), :] = blank
 
@@ -256,7 +258,7 @@
 def src_outer_kernel(limit, src, sat, even_in, odd_in, heavy_in, plain_in, heavy, plain, sums, low, high, caps, limits):
     times, lines, cells, depth = src.shape
     unpack_marks(times, limit, sat, even_in, odd_in, caps, limits)
-    unpack_halo(even_in, odd_in, low, high)
+    unpack_halo(even_in, 0, odd_in, 0, low, high)
     add_outer(src, [heavy], [plain], low, high, caps, limits)
     zero = jnp.zeros((ROWS, depth), jnp.float32)
 
@@ -276,10 +278,10 @@
     )
 
 
-def rcv_outer_kernel(limit, rcv, sat, even_marks, odd_marks, even_in, odd_in, *refs):
+def rcv_outer_kernel(limit, rcv, sat, even_in, odd_marks, odd_in, *refs):
     parts, (low, high, caps, limits) = refs[len(refs) // 2 - 2 : -4], refs[-4:]
-    unpack_marks(rcv.shape[0], limit, sat, even_marks, odd_marks, caps, limits)
-    unpack_halo(even_in, odd_in, low, high)
+    unpack_marks(rcv.shape[0], limit, sat, even_in, odd_marks, caps, limits)
+    unpack_halo(even_in, payload_layout(*rcv.shape[:2])[2], odd_in, 0, low, high)
     add_outer(rcv, parts[::2], parts[1::2], low, high, caps, limits)
 
 
@@ -352,7 +354,7 @@
         )(*operands)
 
     src, rcv, sat = source_field, receiver_field, sat_mask
-    offset_range, even, odd = payloads(rcv, sat, offset_range)
+    offset_range, even, odd = payloads(src, rcv, sat, offset_range)
     even_route, odd_route = exchanges(size, lax.axis_size("xline"))
     even = lax.ppermute(even, DEVICES, even_route)
     odd = lax.ppermute(odd, DEVICES, odd_route)
@@ -365,9 +367,7 @@
         0.85,
     )
     (heavy, plain), ahead = lax.optimization_barrier(((heavy, plain), src))
-    low_high = edges(ahead, 2, REACH)
-    odd_late = lax.ppermute(for_odd(*low_high), DEVICES, odd_route)
-    even_late = lax.ppermute(for_even(*low_high), DEVICES, even_route)
+    odd_late = lax.ppermute(for_odd(*edges(ahead, 2, REACH)), DEVICES, odd_route)
     count = size * lax.axis_size("xline")
     heavy, plain, sums = call(
         src_outer_kernel,
@@ -384,14 +384,14 @@
             rcv_outer_kernel,
             "rcv_outer",
             [piece] * len(pieces),
-            (offset_range, rcv, sat, even, odd, even_late, odd_late, *pieces),
+            (offset_range, rcv, sat, even, odd, odd_late, *pieces),
             [edge, edge, caps, limits],
             0.25,
             {7 + i: i for i in range(len(pieces))},
         )
 
     gathered = lax.all_to_all(sums, DEVICES, 0, 0, tiled=True)
-    sums, ahead, odd_late, even_late = lax.optimization_barrier((sums, src, odd_late, even_late))
+    sums, ahead, odd_late = lax.optimization_barrier((sums, src, odd_late))
     pieces = call(
         inner_kernel,
         "rcv_inner",
@@ -404,10 +404,10 @@
         rcv_outer_kernel,
         "rcv_outer",
         (total, total),
-        (offset_range, rcv, sat, even, odd, even_late, odd_late, *pieces),
+        (offset_range, rcv, sat, even, odd, odd_late, *pieces),
         [edge, edge, caps, limits],
         0.25,
-        {7: 0, 8: 1},
+        {6: 0, 7: 1},
     )
 
     cell_count = float(lines * lax.axis_size("xline") * cells * size * depth * (2 * H + 1))

time: 27.7 us -> 27.5 us (level)
  starting transfers between devices: 12.9 us -> 9.25 us
  waiting for transfers between devices: 4.05 us -> 5.71 us
  Pallas kernels: 7.92 us -> 9.31 us
    ppermute x2 -> x1, starting transfers between devices: 3.04 us -> 0.07 us  [local(): lax.ppermute(for_odd(*edges(ahead, 2, REACH)), DEVICES, odd_route)]
    ppermute x1, waiting for transfers between devices: 0.01 us -> 2.36 us  [local(): even = lax.ppermute(even, DEVICES, even_route)]
    pallas_call x5, Pallas kernels: 7.92 us -> 9.31 us  [call(): pl.pallas_call(kernel, out_shape=out_shape, in_specs=[SMEM if operand is...]
    all_to_all x1, waiting for transfers between devices: 4.04 us -> 3.35 us  [local(): gathered = lax.all_to_all(sums, DEVICES, 0, 0, tiled=True)]
    all_to_all x1, starting transfers between devices: 5.41 us -> 4.94 us  [local(): gathered = lax.all_to_all(sums, DEVICES, 0, 0, tiled=True)]
    unnamed x6, local copies, waits for them, and re-layouts: 0.01 us -> 0.33 us
    select_n x3 -> x4, other arithmetic: 0.95 us -> 0.95 us  [for_even(): return jnp.where(lax.axis_index('inline') % 2 == 0, high, low)]
  transfers between devices with their start and end apart: 5 -> 4, of which waited for: 1 -> 2; matrix products, arithmetic and copies ran while one was open for 0% -> 0% of each run, Pallas kernels for 26% -> 31%
where the time goes in v6:
time: 27.5 us; the launch traced here: 27 us
  Pallas kernels  9.31 us (34%)
  starting transfers between devices  9.25 us (34%)
  waiting for transfers between devices  5.71 us (21%)
  between operations  1.44 us (5%)
  other arithmetic  0.98 us (4%)
  local copies, waits for them, and re-layouts  0.34 us (1%)
    pallas_call x5, Pallas kernels, call(): pl.pallas_call(kernel, out_shape=out_shape, in_specs=[SMEM if operand is...  9.31 us
    all_to_all x1, starting transfers between devices, local(): gathered = lax.all_to_all(sums, DEVICES, 0, 0, tiled=True)  4.94 us
    ppermute x1, starting transfers between devices, local(): even = lax.ppermute(even, DEVICES, even_route)  3.73 us
    all_to_all x1, waiting for transfers between devices, local(): gathered = lax.all_to_all(sums, DEVICES, 0, 0, tiled=True)  3.35 us
    ppermute x1, waiting for transfers between devices, local(): even = lax.ppermute(even, DEVICES, even_route)  2.36 us
    select_n x4, other arithmetic, for_even(): return jnp.where(lax.axis_index('inline') % 2 == 0, high, low)  0.95 us
  transfers between devices with their start and end apart: 4, of which 2 were waited for; matrix products, arithmetic and copies ran while one was open for 0% of the time, Pallas kernels for 31%

profile of v6, /device:TPU:0, one launch (start us, length us, event | category | flops | bytes accessed | tf_op | source)
XLA Modules:
  0.0 27.0 jit_solution(14751838618727423141)
XLA Ops:
  1.3 0.0 copy-start.2
  1.3 0.9 %broadcast_select_fusion = (bf16[4,1,64,128]{3,2,1,0:T(8,128)(2,1)S(1)}, bf16[4,1,64,128]{3,2,1,0:T(8,128)(2,1)S(1)}) fusion(pred[]{:T(512)S(6)} %eq.15, bf16[4,1,128,128]{3,2,1,0:T(8,128)(2,1)} %rcv.1), kind=kLoop, calls=%fused_computation.5 | loop fusion | flops 65536 | bytes 262145 | tf_op jit(solution)/shard_map/jit(_where)/select_n | solution.py:65
  2.2 0.0 copy-done.2
  2.2 0.0 copy-start
  2.3 0.5 %collective-permute-start.1 = (bf16[304,128]{1,0:T(8,128)(2,1)S(1)}, bf16[304,128]{1,0:T(8,128)(2,1)S(1)}, u32[]{:S(2)}, u32[]{:S(2)}) collective-permute-start(bf16[304,128]{1,0:T(8,128)(2,1)S(1)} %pad_maximum_fusion.1), channel_id=1, source_target_pairs={{0,1},{1,0},{2,4},{3,5},{4,2},{5,3},{6,8},{7,9},{8,6},{9,7},{10,12... | collective-permute-start | bytes 233480 | tf_op jit(solution)/shard_map/ppermute | solution.py:360
  2.8 0.3 %copy-done = bf16[4,1,128,128]{3,2,1,0:T(8,128)(2,1)S(1)} copy-done((bf16[4,1,128,128]{3,2,1,0:T(8,128)(2,1)S(1)}, bf16[4,1,128,128]{3,2,1,0:T(8,128)(2,1)}, u32[]{:S(2)}) %copy-start) | copy-done | bytes 131096
  3.2 0.0 copy-start.1
  3.2 3.7 %collective-permute-start = (bf16[560,128]{1,0:T(8,128)(2,1)S(1)}, bf16[560,128]{1,0:T(8,128)(2,1)S(1)}, u32[]{:S(2)}, u32[]{:S(2)}) collective-permute-start(bf16[560,128]{1,0:T(8,128)(2,1)S(1)} %pad_maximum_fusion), channel_id=1, source_target_pairs={{0,2},{1,3},{2,0},{3,1},{4,6},{5,7},{6,4},{7,5},{8,10},{9,11},{10,... | collective-permute-start | bytes 430088 | tf_op jit(solution)/shard_map/ppermute | solution.py:359
  6.9 0.0 copy-done.1
  6.9 2.6 %src_inner.1 = (f32[4,1,128,128]{3,2,1,0:T(8,128)S(1)}, f32[4,1,128,128]{3,2,1,0:T(8,128)S(1)}) custom-call(s32[1]{0:T(128)S(6)} %copy.15.limit, bf16[4,1,128,128]{3,2,1,0:T(8,128)(2,1)S(1)} %copy-done, bf16[4,1,128,128]{3,2,1,0:T(8,128)(2,1)S(1)} %copy-done.1, s32[1,128,128]{2,1,0:T(8,128)S(1)} %copy-done.2), custom_call_target="tpu_custom_call" | custom-call | flops 21725184 | bytes 1048576 | tf_op jit(solution)/shard_map/src_inner/pallas_call | solution.py:342
  9.5 0.1 collective-permute-start.2
  9.6 0.0 collective-permute-done.1.odd_in.odd_marks
  9.6 2.4 %collective-permute-done.even_in = bf16[560,128]{1,0:T(8,128)(2,1)S(1)} collective-permute-done((bf16[560,128]{1,0:T(8,128)(2,1)S(1)}, bf16[560,128]{1,0:T(8,128)(2,1)S(1)}, u32[]{:S(2)}, u32[]{:S(2)}) %collective-permute-start) | collective-permute-done | bytes 143392 | tf_op jit(solution)/shard_map/ppermute | solution.py:359
  11.9 2.0 %src_outer.1 = (f32[4,1,128,128]{3,2,1,0:T(8,128)S(1)}, f32[4,1,128,128]{3,2,1,0:T(8,128)S(1)}, f32[32,2,128]{2,1,0:T(2,128)}) custom-call(s32[1]{0:T(128)S(6)} %copy.15.limit, bf16[4,1,128,128]{3,2,1,0:T(8,128)(2,1)S(1)} %copy-done, s32[1,128,128]{2,1,0:T(8,128)S(1)} %copy-done.2, ...), custom_call_target="tpu_custom_call", output_to_operand_aliasing={{0}: (5, {}), {1}: (6, {})} | custom-call | flops 6389760 | bytes 1048576 | tf_op jit(solution)/shard_map/src_outer/pallas_call | solution.py:342
  14.0 4.9 %all-to-all-start = ((f32[32,2,128]{2,1,0:T(2,128)}), f32[32,2,128]{2,1,0:T(2,128)S(1)}, u32[]{:S(2)}, u32[]{:S(2)}) async-start(f32[32,2,128]{2,1,0:T(2,128)} %get-tuple-element.34), calls=%async_computation | async-start | bytes 65536 | tf_op jit(solution)/shard_map/all_to_all | solution.py:393
  18.9 0.0 collective-permute-done.2.odd_in
  18.9 2.6 %rcv_inner.1 = (f32[4,1,128,128]{3,2,1,0:T(8,128)S(1)}, f32[4,1,128,128]{3,2,1,0:T(8,128)S(1)}) custom-call(s32[1]{0:T(128)S(6)} %copy.15.limit, bf16[4,1,128,128]{3,2,1,0:T(8,128)(2,1)S(1)} %copy-done.1, bf16[4,1,128,128]{3,2,1,0:T(8,128)(2,1)S(1)} %copy-done, s32[1,128,128]{2,1,0:T(8,128)S(1)} %copy-done.2), custom_call_target="tpu_custom_call" | custom-call | flops 21725184 | bytes 1048576 | tf_op jit(solution)/shard_map/rcv_inner/pallas_call | solution.py:342
  21.5 1.3 %rcv_outer.1 = (f32[4,1,128,128]{3,2,1,0:T(8,128)S(1)}, f32[4,1,128,128]{3,2,1,0:T(8,128)S(1)}) custom-call(s32[1]{0:T(128)S(6)} %copy.15.limit, bf16[4,1,128,128]{3,2,1,0:T(8,128)(2,1)S(1)} %copy-done.1, s32[1,128,128]{2,1,0:T(8,128)S(1)} %copy-done.2, ...), custom_call_target="tpu_custom_call", output_to_operand_aliasing={{0}: (6, {}), {1}: (7, {})} | custom-call | flops 6389760 | bytes 1048576 | tf_op jit(solution)/shard_map/rcv_outer/pallas_call | solution.py:342
  22.8 3.4 %all-to-all-done.sums = f32[32,2,128]{2,1,0:T(2,128)S(1)} async-done(((f32[32,2,128]{2,1,0:T(2,128)}), f32[32,2,128]{2,1,0:T(2,128)S(1)}, u32[]{:S(2)}, u32[]{:S(2)}) %all-to-all-start) | async-done | bytes 32800 | tf_op jit(solution)/shard_map/all_to_all | solution.py:393
  26.2 0.9 %combine.1 = (bf16[4,1,128,128]{3,2,1,0:T(8,128)(2,1)}, bf16[4,1,128,128]{3,2,1,0:T(8,128)(2,1)}, f32[1,128]{1,0:T(1,128)}) custom-call(f32[32,2,128]{2,1,0:T(2,128)S(1)} %all-to-all-done.sums, f32[4,1,128,128]{3,2,1,0:T(8,128)S(1)} %get-tuple-element.35.src_heavy, f32[4,1,128,128]{3,2,1,0:T(8,128)S(1)} %get-tuple-element.36.src_plain, ...), custom_call_target="tpu_custom_call" | custom-call | bytes 1048576 | tf_op jit(solution)/shard_map/combine/pallas_call | solution.py:342
  (7 shorter events, 0.1 us)
Async XLA Ops:
  1.3 0.9 %copy-start.2 = (s32[1,128,128]{2,1,0:T(8,128)S(1)}, s32[1,128,128]{2,1,0:T(8,128)}, u32[]{:S(2)}) copy-start(s32[1,128,128]{2,1,0:T(8,128)} %sat.7) | copy-start | bytes 196612
  2.2 0.9 %copy-start = (bf16[4,1,128,128]{3,2,1,0:T(8,128)(2,1)S(1)}, bf16[4,1,128,128]{3,2,1,0:T(8,128)(2,1)}, u32[]{:S(2)}) copy-start(bf16[4,1,128,128]{3,2,1,0:T(8,128)(2,1)} %field.2) | copy-start | bytes 393220
  2.3 7.3 %collective-permute-start.1 = (bf16[304,128]{1,0:T(8,128)(2,1)S(1)}, bf16[304,128]{1,0:T(8,128)(2,1)S(1)}, u32[]{:S(2)}, u32[]{:S(2)}) collective-permute-start(bf16[304,128]{1,0:T(8,128)(2,1)S(1)} %pad_maximum_fusion.1), channel_id=1, source_target_pairs={{0,1},{1,0},{2,4},{3,5},{4,2},{5,3},{6,8},{7,9},{8,6},{9,7},{10,12... | collective-permute-start | bytes 233480 | tf_op jit(solution)/shard_map/ppermute | solution.py:360
  3.2 3.8 %copy-start.1 = (bf16[4,1,128,128]{3,2,1,0:T(8,128)(2,1)S(1)}, bf16[4,1,128,128]{3,2,1,0:T(8,128)(2,1)}, u32[]{:S(2)}) copy-start(bf16[4,1,128,128]{3,2,1,0:T(8,128)(2,1)} %rcv.1) | copy-start | bytes 393220
  3.2 8.8 %collective-permute-start = (bf16[560,128]{1,0:T(8,128)(2,1)S(1)}, bf16[560,128]{1,0:T(8,128)(2,1)S(1)}, u32[]{:S(2)}, u32[]{:S(2)}) collective-permute-start(bf16[560,128]{1,0:T(8,128)(2,1)S(1)} %pad_maximum_fusion), channel_id=1, source_target_pairs={{0,2},{1,3},{2,0},{3,1},{4,6},{5,7},{6,4},{7,5},{8,10},{9,11},{10,... | collective-permute-start | bytes 430088 | tf_op jit(solution)/shard_map/ppermute | solution.py:359
  9.5 9.4 %collective-permute-start.2 = (bf16[256,128]{1,0:T(8,128)(2,1)S(1)}, bf16[256,128]{1,0:T(8,128)(2,1)S(1)}, u32[]{:S(2)}, u32[]{:S(2)}) collective-permute-start(bf16[256,128]{1,0:T(8,128)(2,1)S(1)} %bitcast.14), channel_id=1, source_target_pairs={{0,1},{1,0},{2,4},{3,5},{4,2},{5,3},{6,8},{7,9},{8,6},{9,7},{10,12... | collective-permute-start | bytes 196616 | tf_op jit(solution)/shard_map/ppermute | solution.py:370
  14.0 12.2 %all-to-all-start = ((f32[32,2,128]{2,1,0:T(2,128)}), f32[32,2,128]{2,1,0:T(2,128)S(1)}, u32[]{:S(2)}, u32[]{:S(2)}) async-start(f32[32,2,128]{2,1,0:T(2,128)} %get-tuple-element.34), calls=%async_computation | async-start | bytes 65536 | tf_op jit(solution)/shard_map/all_to_all | solution.py:393

commit v7 on v5

--- a/solution.py
+++ b/solution.py
@@ -72,11 +72,12 @@
     depth = rcv.shape[-1]
     rows = edges(rcv, 2, REACH)
     rows = for_even(*rows), for_odd(*rows)
-    *rows, sat, limit = lax.optimization_barrier((*rows, sat, limit))
+    *rows, sat = lax.optimization_barrier((*rows, sat))
     masks = edges((sat != 0).astype(jnp.bfloat16), 1, H)
     limits = jnp.full((LIMIT_ROWS, depth), limit[0]).astype(jnp.bfloat16)
-    even = jnp.concatenate([rows[0], for_even(*masks), limits], axis=0)
-    return limit, even, jnp.concatenate([rows[1], for_odd(*masks), limits], axis=0)
+    return [
+        jnp.concatenate([part, choose(*masks), limits], axis=0) for part, choose in zip(rows, (for_even, for_odd))
+    ]
 
 
 def unpack_marks(times, limit, sat, even_in, odd_in, caps, limits):
@@ -155,7 +156,8 @@
     return [[rows[half * ROWS : (half + 1) * ROWS] for rows in both] for half in range(2)]
 
 
-def inner_kernel(limit, middle, field, sat, heavy_out, plain_out, shifted, caps):
+def inner_kernel(limit, middle, field, sat, heavy_out, plain_out, *refs):
+    *sums_out, shifted, caps = refs
     times, lines, cells, depth = field.shape
     zero = jnp.zeros((ROWS, depth), jnp.float32)
     blank = jnp.zeros((REACH, depth), jnp.float32)
@@ -170,7 +172,7 @@
         caps[y, pl.ds(H + cells, H), :] = blank[:H]
     inside = [(size <= limit[0]).astype(jnp.float32) for size in range(H + 1)]
 
-    def tile(index, carry):
+    def tile(index, totals):
         base = pl.multiple_of(index * PAIR, PAIR)
         for y in range(lines):
             for half, center in enumerate(tiles_of(middle, y, base)):
@@ -199,9 +201,13 @@
                 for t in range(times):
                     heavy_out[t, y, rows, :] = heavy[t]
                     plain_out[t, y, rows, :] = plain[t]
-        return carry
-
-    lax.fori_loop(0, heavy_out.shape[2] // PAIR, tile, 0)
+                if sums_out:
+                    totals = totals[0] + image_of(center, plain), totals[1] + image_of(center, heavy)
+        return totals
+
+    totals = lax.fori_loop(0, cells // PAIR, tile, (zero, zero) if sums_out else 0)
+    if sums_out:
+        sums_out[0][...] = jnp.concatenate(totals, axis=0)
 
 
 def within(limits, at):
@@ -213,9 +219,9 @@
     return masked
 
 
-def add_outer(middle, heavy, plain, low, high, caps, limits):
+def each_outer_tile(middle, low, high, visit):
     times, lines, cells, depth = middle.shape
-    count = heavy[0].shape[2]
+
     for group in range(REACH // PAIR):
 
         def tile(index, carry, group=group):
@@ -224,63 +230,68 @@
                 @pl.when(index == side)
                 def _():
                     first = cells - (group + 1) * PAIR if side else group * PAIR
-                    number = first // count
-                    base = pl.multiple_of(first - number * count + (index - side) * PAIR, PAIR)
+                    base = pl.multiple_of(first + (index - side) * PAIR, PAIR)
                     origin = ROWS - cells if side else REACH
                     for y in range(lines):
-                        for half, center in enumerate(tiles_of(middle, y, number * count + base)):
-                            rows = pl.ds(base + half * ROWS, ROWS)
-                            at = number * count + base + half * ROWS
+                        for half, center in enumerate(tiles_of(middle, y, base)):
+                            at = base + half * ROWS
                             rank = 2 * group + (1 - half if side else half)
                             sizes = range(ROWS // 2 * rank + 1, H + 1)
-                            new_heavy, new_plain = accumulate(
+                            visit(
+                                y,
+                                at,
                                 center,
-                                (
-                                    [heavy[number][t, y, rows, :] for t in range(times)],
-                                    [plain[number][t, y, rows, :] for t in range(times)],
-                                ),
                                 [size if side else -size for size in sizes],
                                 lambda h: [shifted[t, y, pl.ds(at + origin + 2 * h, ROWS), :] for t in range(times)],
-                                within(limits, at),
-                                lambda h: caps[y, pl.ds(at + H + h, ROWS), :],
                             )
-                            for t in range(times):
-                                heavy[number][t, y, rows, :] = new_heavy[t]
-                                plain[number][t, y, rows, :] = new_plain[t]
 
             return carry
 
         lax.fori_loop(0, 2, tile, 0)
 
 
-def src_outer_kernel(limit, src, sat, even_in, odd_in, heavy_in, plain_in, heavy, plain, sums, low, high, caps, limits):
+def energy_kernel(limit, src, sat, even_in, odd_in, inner, sums, total, low, high, caps, limits):
     times, lines, cells, depth = src.shape
     unpack_marks(times, limit, sat, even_in, odd_in, caps, limits)
     unpack_halo(even_in, odd_in, low, high)
-    add_outer(src, [heavy], [plain], low, high, caps, limits)
-    zero = jnp.zeros((ROWS, depth), jnp.float32)
-
-    def add(index, totals):
-        energy, weighted = totals
-        base = pl.multiple_of(index * PAIR, PAIR)
-        for y in range(lines):
-            for half, center in enumerate(tiles_of(src, y, base)):
-                rows = pl.ds(base + half * ROWS, ROWS)
-                energy = energy + image_of(center, [plain[t, y, rows, :] for t in range(times)])
-                weighted = weighted + image_of(center, [heavy[t, y, rows, :] for t in range(times)])
-        return energy, weighted
-
-    energy, weighted = lax.fori_loop(0, cells // PAIR, add, (zero, zero))
-    sums[...] = jnp.broadcast_to(
-        jnp.concatenate([jnp.sum(part, axis=0, keepdims=True) for part in (energy, weighted)], axis=0)[None], sums.shape
-    )
-
-
-def rcv_outer_kernel(limit, rcv, sat, even_marks, odd_marks, even_in, odd_in, *refs):
-    parts, (low, high, caps, limits) = refs[len(refs) // 2 - 2 : -4], refs[-4:]
-    unpack_marks(rcv.shape[0], limit, sat, even_marks, odd_marks, caps, limits)
+    total[...] = inner[...]
+
+    def visit(y, at, center, offsets, far_at):
+        energy, weighted = total[:ROWS, :], total[ROWS:, :]
+        masked = within(limits, at)
+        for offset in offsets:
+            image = masked(image_of(center, far_at(offset)), offset)
+            power = image * image
+            energy = energy + power
+            square = square_weight(offset)
+            if abs(offset) > SHARED:
+                square = jnp.minimum(caps[y, pl.ds(at + H + offset, ROWS), :], square)
+            weighted = weighted + power * square
+        total[:ROWS, :] = energy
+        total[ROWS:, :] = weighted
+
+    each_outer_tile(src, low, high, visit)
+    rows = [jnp.sum(total[pl.ds(part * ROWS, ROWS), :], axis=0, keepdims=True) for part in range(2)]
+    sums[...] = jnp.broadcast_to(jnp.concatenate(rows, axis=0)[None], sums.shape)
+
+
+def outer_kernel(limit, middle, sat, even_marks, odd_marks, even_in, odd_in, heavy_in, plain_in, heavy, plain, *scratch):
+    low, high, caps, limits = scratch
+    times, lines, cells, depth = middle.shape
+    unpack_marks(times, limit, sat, even_marks, odd_marks, caps, limits)
     unpack_halo(even_in, odd_in, low, high)
-    add_outer(rcv, parts[::2], parts[1::2], low, high, caps, limits)
+
+    def visit(y, at, center, offsets, far_at):
+        rows = pl.ds(at, ROWS)
+        sums = [heavy[t, y, rows, :] for t in range(times)], [plain[t, y, rows, :] for t in range(times)]
+        new_heavy, new_plain = accumulate(
+            center, sums, offsets, far_at, within(limits, at), lambda h: caps[y, pl.ds(at + H + h, ROWS), :]
+        )
+        for t in range(times):
+            heavy[t, y, rows, :] = new_heavy[t]
+            plain[t, y, rows, :] = new_plain[t]
+
+    each_outer_tile(middle, low, high, visit)
 
 
 def combine_kernel(cell_count, sums, src_heavy, src_plain, *refs):
@@ -352,46 +363,42 @@
         )(*operands)
 
     src, rcv, sat = source_field, receiver_field, sat_mask
-    offset_range, even, odd = payloads(rcv, sat, offset_range)
+    even, odd = payloads(rcv, sat, offset_range)
     even_route, odd_route = exchanges(size, lax.axis_size("xline"))
     even = lax.ppermute(even, DEVICES, even_route)
     odd = lax.ppermute(odd, DEVICES, odd_route)
-    heavy, plain = call(
+    even_late = lax.ppermute(for_even(*edges(src, 2, REACH)), DEVICES, even_route)
+
+    heavy, plain, inner = call(
         inner_kernel,
         "src_inner",
-        (total, total),
+        (total, total, shape((2 * ROWS, depth), jnp.float32)),
         (offset_range, src, rcv, sat),
         [extended, caps],
         0.85,
     )
-    (heavy, plain), ahead = lax.optimization_barrier(((heavy, plain), src))
-    low_high = edges(ahead, 2, REACH)
-    odd_late = lax.ppermute(for_odd(*low_high), DEVICES, odd_route)
-    even_late = lax.ppermute(for_even(*low_high), DEVICES, even_route)
-    count = size * lax.axis_size("xline")
-    heavy, plain, sums = call(
-        src_outer_kernel,
+    sums = call(
+        energy_kernel,
+        "energy",
+        shape((size * lax.axis_size("xline"), 2, depth), jnp.float32),
+        (offset_range, src, sat, even, odd, inner),
+        [pltpu.VMEM((2 * ROWS, depth), jnp.float32), edge, edge, caps, limits],
+        0.15,
+    )
+    gathered = lax.all_to_all(sums, DEVICES, 0, 0, tiled=True)
+
+    sums, heavy, plain, ahead = lax.optimization_barrier((sums, heavy, plain, src))
+    heavy, plain = call(
+        outer_kernel,
         "src_outer",
-        (total, total, shape((count, 2, depth), jnp.float32)),
-        (offset_range, src, sat, even, odd, heavy, plain),
+        (total, total),
+        (offset_range, ahead, sat, even, odd, even, odd, heavy, plain),
         [edge, edge, caps, limits],
         0.25,
-        {5: 0, 6: 1},
-    )
-
-    def finish(odd_late, even_late, *pieces):
-        return call(
-            rcv_outer_kernel,
-            "rcv_outer",
-            [piece] * len(pieces),
-            (offset_range, rcv, sat, even, odd, even_late, odd_late, *pieces),
-            [edge, edge, caps, limits],
-            0.25,
-            {7 + i: i for i in range(len(pieces))},
-        )
-
-    gathered = lax.all_to_all(sums, DEVICES, 0, 0, tiled=True)
-    sums, ahead, odd_late, even_late = lax.optimization_barrier((sums, src, odd_late, even_late))
+        {7: 0, 8: 1},
+    )
+    heavy, plain, ahead = lax.optimization_barrier((heavy, plain, ahead))
+    odd_late = lax.ppermute(for_odd(*edges(ahead, 2, REACH)), DEVICES, odd_route)
     pieces = call(
         inner_kernel,
         "rcv_inner",
@@ -401,7 +408,7 @@
         0.85,
     )
     pieces = call(
-        rcv_outer_kernel,
+        outer_kernel,
         "rcv_outer",
         (total, total),
         (offset_range, rcv, sat, even, odd, even_late, odd_late, *pieces),

time: 27.7 us -> 29.1 us (1.051)
  Pallas kernels: 7.92 us -> 9.98 us
  starting transfers between devices: 12.9 us -> 11.2 us
  waiting for transfers between devices: 4.05 us -> 5.05 us
    ppermute x2, starting transfers between devices: 3.04 us -> 0.14 us  [the longest x1 0.07 us: local(): lax.ppermute(for_odd(*edges(ahead, 2, REACH)), DEVICES, odd_route)]
    pallas_call x5 -> x6, Pallas kernels: 7.92 us -> 9.98 us  [call(): pl.pallas_call(kernel, out_shape=out_shape, in_specs=[SMEM if operand is...]
    ppermute x1, waiting for transfers between devices: 0.01 us -> 1.72 us  [local(): even = lax.ppermute(even, DEVICES, even_route)]
    all_to_all x1, starting transfers between devices: 5.41 us -> 6.58 us  [local(): gathered = lax.all_to_all(sums, DEVICES, 0, 0, tiled=True)]
    all_to_all x1, waiting for transfers between devices: 4.04 us -> 3.32 us  [local(): gathered = lax.all_to_all(sums, DEVICES, 0, 0, tiled=True)]
    select_n x3 -> x4, other arithmetic: 0.95 us -> 0.95 us  [for_even(): return jnp.where(lax.axis_index('inline') % 2 == 0, high, low)]
  transfers between devices with their start and end apart: 5 -> 5, of which waited for: 1 -> 2; matrix products, arithmetic and copies ran while one was open for 0% -> 0% of each run, Pallas kernels for 26% -> 32%
where the time goes in v7:
time: 29.1 us; the launch traced here: 28.9 us
  starting transfers between devices  11.2 us (38%)
  Pallas kernels  9.98 us (34%)
  waiting for transfers between devices  5.05 us (17%)
  between operations  1.45 us (5%)
  other arithmetic  1.07 us (4%)
    pallas_call x6, Pallas kernels, call(): pl.pallas_call(kernel, out_shape=out_shape, in_specs=[SMEM if operand is...  9.98 us
    all_to_all x1, starting transfers between devices, local(): gathered = lax.all_to_all(sums, DEVICES, 0, 0, tiled=True)  6.58 us
    ppermute x1, starting transfers between devices, local(): even = lax.ppermute(even, DEVICES, even_route)  3.98 us
    all_to_all x1, waiting for transfers between devices, local(): gathered = lax.all_to_all(sums, DEVICES, 0, 0, tiled=True)  3.32 us
    ppermute x1, waiting for transfers between devices, local(): even = lax.ppermute(even, DEVICES, even_route)  1.72 us
    select_n x4, other arithmetic, for_even(): return jnp.where(lax.axis_index('inline') % 2 == 0, high, low)  0.95 us
  transfers between devices with their start and end apart: 5, of which 2 were waited for; matrix products, arithmetic and copies ran while one was open for 0% of the time, Pallas kernels for 32%

profile of v7, /device:TPU:0, one launch (start us, length us, event | category | flops | bytes accessed | tf_op | source)
XLA Modules:
  0.0 28.9 jit_solution(8396012164739347711)
XLA Ops:
  1.3 0.0 copy-start.1
  1.3 0.9 %broadcast_select_fusion = (bf16[4,1,64,128]{3,2,1,0:T(8,128)(2,1)S(1)}, bf16[4,1,64,128]{3,2,1,0:T(8,128)(2,1)S(1)}) fusion(pred[]{:T(512)S(6)} %eq.15, bf16[4,1,128,128]{3,2,1,0:T(8,128)(2,1)} %middle.6), kind=kLoop, calls=%fused_computation.5 | loop fusion | flops 65536 | bytes 262145 | tf_op jit(solution)/shard_map/jit(_where)/select_n | solution.py:64
  2.2 0.0 copy-done.1
  2.3 0.1 pad.5.clone
  2.4 0.1 maximum_maximum_fusion.1
  2.5 0.0 copy-start.2
  2.5 0.5 %collective-permute-start.1 = (bf16[304,128]{1,0:T(8,128)(2,1)S(1)}, bf16[304,128]{1,0:T(8,128)(2,1)S(1)}, u32[]{:S(2)}, u32[]{:S(2)}) collective-permute-start(bf16[304,128]{1,0:T(8,128)(2,1)S(1)} %get-tuple-element.49), channel_id=1, source_target_pairs={{0,1},{1,0},{2,4},{3,5},{4,2},{5,3},{6,8},{7,9},{8,6},{9,7},{10,12... | collective-permute-start | bytes 233480 | tf_op jit(solution)/shard_map/ppermute | solution.py:369
  3.0 4.0 %collective-permute-start = (bf16[304,128]{1,0:T(8,128)(2,1)S(1)}, bf16[304,128]{1,0:T(8,128)(2,1)S(1)}, u32[]{:S(2)}, u32[]{:S(2)}) collective-permute-start(bf16[304,128]{1,0:T(8,128)(2,1)S(1)} %get-tuple-element.50), channel_id=1, source_target_pairs={{0,2},{1,3},{2,0},{3,1},{4,6},{5,7},{6,4},{7,5},{8,10},{9,11},{10,... | collective-permute-start | bytes 233480 | tf_op jit(solution)/shard_map/ppermute | solution.py:368
  7.0 0.0 copy-done
  7.0 0.1 collective-permute-start.2
  7.1 0.0 copy-done.2
  7.1 2.6 %src_inner.1 = (f32[4,1,128,128]{3,2,1,0:T(8,128)S(1)}, f32[4,1,128,128]{3,2,1,0:T(8,128)S(1)}, f32[16,128]{1,0:T(8,128)S(1)}) custom-call(s32[1]{0:T(128)S(6)} %copy.15.limit, bf16[4,1,128,128]{3,2,1,0:T(8,128)(2,1)S(1)} %copy-done, bf16[4,1,128,128]{3,2,1,0:T(8,128)(2,1)S(1)} %copy-done.2, s32[1,128,128]{2,1,0:T(8,128)S(1)} %copy-done.1), custom_call_target="tpu_custom_call" | custom-call | flops 21725184 | bytes 1048576 | tf_op jit(solution)/shard_map/src_inner/pallas_call | solution.py:351
  9.7 0.0 collective-permute-done.1.odd_in.odd_marks
  9.7 1.7 %collective-permute-done.even_in.even_marks = bf16[304,128]{1,0:T(8,128)(2,1)S(1)} collective-permute-done((bf16[304,128]{1,0:T(8,128)(2,1)S(1)}, bf16[304,128]{1,0:T(8,128)(2,1)S(1)}, u32[]{:S(2)}, u32[]{:S(2)}) %collective-permute-start) | collective-permute-done | bytes 77856 | tf_op jit(solution)/shard_map/ppermute | solution.py:368
  11.4 1.3 %energy.1 = f32[32,2,128]{2,1,0:T(2,128)} custom-call(s32[1]{0:T(128)S(6)} %copy.15.limit, bf16[4,1,128,128]{3,2,1,0:T(8,128)(2,1)S(1)} %copy-done, s32[1,128,128]{2,1,0:T(8,128)S(1)} %copy-done.1, bf16[304,128]{1,0:T(8,128)(2,1)S(1)} %collective-permute-done.even_in.even_marks, bf16[304,128]{1,0:T(8,128)(2,1)S(1)} %collective-permute-done.1.odd_in.odd_marks, ...), custom_call_target="tpu_custom_call" | custom-call | flops 3833856 | bytes 1048576 | tf_op jit(solution)/shard_map/energy/pallas_call | solution.py:351
  12.8 1.3 %src_outer.1 = (f32[4,1,128,128]{3,2,1,0:T(8,128)S(1)}, f32[4,1,128,128]{3,2,1,0:T(8,128)S(1)}) custom-call(s32[1]{0:T(128)S(6)} %copy.15.limit, bf16[4,1,128,128]{3,2,1,0:T(8,128)(2,1)S(1)} %copy-done, s32[1,128,128]{2,1,0:T(8,128)S(1)} %copy-done.1, ...), custom_call_target="tpu_custom_call", output_to_operand_aliasing={{0}: (7, {}), {1}: (8, {})} | custom-call | flops 6389760 | bytes 1048576 | tf_op jit(solution)/shard_map/src_outer/pallas_call | solution.py:351
  14.1 0.1 collective-permute-start.3
  14.2 6.6 %all-to-all-start = ((f32[32,2,128]{2,1,0:T(2,128)}), f32[32,2,128]{2,1,0:T(2,128)S(1)}, u32[]{:S(2)}, u32[]{:S(2)}) async-start(f32[32,2,128]{2,1,0:T(2,128)} %energy.1), calls=%async_computation | async-start | bytes 65536 | tf_op jit(solution)/shard_map/all_to_all | solution.py:388
  20.8 2.6 %rcv_inner.1 = (f32[4,1,128,128]{3,2,1,0:T(8,128)S(1)}, f32[4,1,128,128]{3,2,1,0:T(8,128)S(1)}) custom-call(s32[1]{0:T(128)S(6)} %copy.15.limit, bf16[4,1,128,128]{3,2,1,0:T(8,128)(2,1)S(1)} %copy-done.2, bf16[4,1,128,128]{3,2,1,0:T(8,128)(2,1)S(1)} %copy-done, s32[1,128,128]{2,1,0:T(8,128)S(1)} %copy-done.1), custom_call_target="tpu_custom_call" | custom-call | flops 21725184 | bytes 1048576 | tf_op jit(solution)/shard_map/rcv_inner/pallas_call | solution.py:351
  23.3 0.0 collective-permute-done.2.even_in
  23.3 0.0 collective-permute-done.3.odd_in
  23.3 1.3 %rcv_outer.1 = (f32[4,1,128,128]{3,2,1,0:T(8,128)S(1)}, f32[4,1,128,128]{3,2,1,0:T(8,128)S(1)}) custom-call(s32[1]{0:T(128)S(6)} %copy.15.limit, bf16[4,1,128,128]{3,2,1,0:T(8,128)(2,1)S(1)} %copy-done.2, s32[1,128,128]{2,1,0:T(8,128)S(1)} %copy-done.1, ...), custom_call_target="tpu_custom_call", output_to_operand_aliasing={{0}: (7, {}), {1}: (8, {})} | custom-call | flops 6389760 | bytes 1048576 | tf_op jit(solution)/shard_map/rcv_outer/pallas_call | solution.py:351
  24.7 3.3 %all-to-all-done.sums = f32[32,2,128]{2,1,0:T(2,128)S(1)} async-done(((f32[32,2,128]{2,1,0:T(2,128)}), f32[32,2,128]{2,1,0:T(2,128)S(1)}, u32[]{:S(2)}, u32[]{:S(2)}) %all-to-all-start) | async-done | bytes 32800 | tf_op jit(solution)/shard_map/all_to_all | solution.py:388
  28.0 0.9 %combine.1 = (bf16[4,1,128,128]{3,2,1,0:T(8,128)(2,1)}, bf16[4,1,128,128]{3,2,1,0:T(8,128)(2,1)}, f32[1,128]{1,0:T(1,128)}) custom-call(f32[32,2,128]{2,1,0:T(2,128)S(1)} %all-to-all-done.sums, f32[4,1,128,128]{3,2,1,0:T(8,128)S(1)} %get-tuple-element.35.src_heavy, f32[4,1,128,128]{3,2,1,0:T(8,128)S(1)} %get-tuple-element.36.src_plain, ...), custom_call_target="tpu_custom_call" | custom-call | bytes 1048576 | tf_op jit(solution)/shard_map/combine/pallas_call | solution.py:351
  (6 shorter events, 0.0 us)
Async XLA Ops:
  1.3 0.9 %copy-start.1 = (s32[1,128,128]{2,1,0:T(8,128)S(1)}, s32[1,128,128]{2,1,0:T(8,128)}, u32[]{:S(2)}) copy-start(s32[1,128,128]{2,1,0:T(8,128)} %sat.9) | copy-start | bytes 196612
  2.4 4.6 %copy-start = (bf16[4,1,128,128]{3,2,1,0:T(8,128)(2,1)S(1)}, bf16[4,1,128,128]{3,2,1,0:T(8,128)(2,1)}, u32[]{:S(2)}) copy-start(bf16[4,1,128,128]{3,2,1,0:T(8,128)(2,1)} %field.2) | copy-start | bytes 393220
  2.5 4.6 %copy-start.2 = (bf16[4,1,128,128]{3,2,1,0:T(8,128)(2,1)S(1)}, bf16[4,1,128,128]{3,2,1,0:T(8,128)(2,1)}, u32[]{:S(2)}) copy-start(bf16[4,1,128,128]{3,2,1,0:T(8,128)(2,1)} %middle.6) | copy-start | bytes 393220
  2.5 7.2 %collective-permute-start.1 = (bf16[304,128]{1,0:T(8,128)(2,1)S(1)}, bf16[304,128]{1,0:T(8,128)(2,1)S(1)}, u32[]{:S(2)}, u32[]{:S(2)}) collective-permute-start(bf16[304,128]{1,0:T(8,128)(2,1)S(1)} %get-tuple-element.49), channel_id=1, source_target_pairs={{0,1},{1,0},{2,4},{3,5},{4,2},{5,3},{6,8},{7,9},{8,6},{9,7},{10,12... | collective-permute-start | bytes 233480 | tf_op jit(solution)/shard_map/ppermute | solution.py:369
  3.0 8.4 %collective-permute-start = (bf16[304,128]{1,0:T(8,128)(2,1)S(1)}, bf16[304,128]{1,0:T(8,128)(2,1)S(1)}, u32[]{:S(2)}, u32[]{:S(2)}) collective-permute-start(bf16[304,128]{1,0:T(8,128)(2,1)S(1)} %get-tuple-element.50), channel_id=1, source_target_pairs={{0,2},{1,3},{2,0},{3,1},{4,6},{5,7},{6,4},{7,5},{8,10},{9,11},{10,... | collective-permute-start | bytes 233480 | tf_op jit(solution)/shard_map/ppermute | solution.py:368
  7.0 16.3 %collective-permute-start.2 = (bf16[256,128]{1,0:T(8,128)(2,1)S(1)}, bf16[256,128]{1,0:T(8,128)(2,1)S(1)}, u32[]{:S(2)}, u32[]{:S(2)}) collective-permute-start(bf16[256,128]{1,0:T(8,128)(2,1)S(1)} %bitcast.13), channel_id=1, source_target_pairs={{0,2},{1,3},{2,0},{3,1},{4,6},{5,7},{6,4},{7,5},{8,10},{9,11},{10,... | collective-permute-start | bytes 196616 | tf_op jit(solution)/shard_map/ppermute | solution.py:370
  14.1 9.2 %collective-permute-start.3 = (bf16[256,128]{1,0:T(8,128)(2,1)S(1)}, bf16[256,128]{1,0:T(8,128)(2,1)S(1)}, u32[]{:S(2)}, u32[]{:S(2)}) collective-permute-start(bf16[256,128]{1,0:T(8,128)(2,1)S(1)} %bitcast.14), channel_id=1, source_target_pairs={{0,1},{1,0},{2,4},{3,5},{4,2},{5,3},{6,8},{7,9},{8,6},{9,7},{10,12... | collective-permute-start | bytes 196616 | tf_op jit(solution)/shard_map/ppermute | solution.py:401
  14.2 13.8 %all-to-all-start = ((f32[32,2,128]{2,1,0:T(2,128)}), f32[32,2,128]{2,1,0:T(2,128)S(1)}, u32[]{:S(2)}, u32[]{:S(2)}) async-start(f32[32,2,128]{2,1,0:T(2,128)} %energy.1), calls=%async_computation | async-start | bytes 65536 | tf_op jit(solution)/shard_map/all_to_all | solution.py:388

commit v8 on v7

--- a/solution.py
+++ b/solution.py
@@ -356,7 +356,7 @@
             scratch_shapes=scratch,
             input_output_aliases=aliases,
             cost_estimate=pl.CostEstimate(
-                flops=int(24 * image_cells * share), bytes_accessed=1 << 20, transcendentals=0
+                flops=int(24 * image_cells * share), bytes_accessed=int(share * (1 << 20)), transcendentals=0
             ),
             compiler_params=grant,
             name=name,
@@ -394,7 +394,7 @@
         (total, total),
         (offset_range, ahead, sat, even, odd, even, odd, heavy, plain),
         [edge, edge, caps, limits],
-        0.25,
+        0.0,
         {7: 0, 8: 1},
     )
     heavy, plain, ahead = lax.optimization_barrier((heavy, plain, ahead))
@@ -405,7 +405,7 @@
         (total, total),
         (offset_range, rcv, ahead, sat),
         [extended, caps],
-        0.85,
+        0.0,
     )
     pieces = call(
         outer_kernel,
@@ -413,7 +413,7 @@
         (total, total),
         (offset_range, rcv, sat, even, odd, even_late, odd_late, *pieces),
         [edge, edge, caps, limits],
-        0.25,
+        0.0,
         {7: 0, 8: 1},
     )
 

time: 29.1 us -> 29.1 us (level)
  Pallas kernels: 9.98 us -> 11.2 us
  waiting for transfers between devices: 5.05 us -> 3.88 us
    pallas_call x6, Pallas kernels: 9.98 us -> 11.2 us  [call(): pl.pallas_call(kernel, out_shape=out_shape, in_specs=[SMEM if operand is...]
    ppermute x1, waiting for transfers between devices: 1.72 us -> 1.13 us  [local(): even = lax.ppermute(even, DEVICES, even_route)]
    all_to_all x1, waiting for transfers between devices: 3.32 us -> 2.74 us  [local(): gathered = lax.all_to_all(sums, DEVICES, 0, 0, tiled=True)]
  transfers between devices with their start and end apart: 5 -> 5, of which waited for: 2 -> 2; matrix products, arithmetic and copies ran while one was open for 0% -> 0% of each run, Pallas kernels for 32% -> 36%
where the time goes in v8:
time: 29.1 us; the launch traced here: 28.9 us
  starting transfers between devices  11.2 us (38%)
  Pallas kernels  11.2 us (38%)
  waiting for transfers between devices  3.88 us (13%)
  between operations  1.45 us (5%)
  other arithmetic  1.07 us (4%)
    pallas_call x6, Pallas kernels, call(): pl.pallas_call(kernel, out_shape=out_shape, in_specs=[SMEM if operand is...  11.2 us
    all_to_all x1, starting transfers between devices, local(): gathered = lax.all_to_all(sums, DEVICES, 0, 0, tiled=True)  6.58 us
    ppermute x1, starting transfers between devices, local(): even = lax.ppermute(even, DEVICES, even_route)  3.98 us
    all_to_all x1, waiting for transfers between devices, local(): gathered = lax.all_to_all(sums, DEVICES, 0, 0, tiled=True)  2.74 us
    ppermute x1, waiting for transfers between devices, local(): even = lax.ppermute(even, DEVICES, even_route)  1.13 us
    select_n x4, other arithmetic, for_even(): return jnp.where(lax.axis_index('inline') % 2 == 0, high, low)  0.95 us
  transfers between devices with their start and end apart: 5, of which 2 were waited for; matrix products, arithmetic and copies ran while one was open for 0% of the time, Pallas kernels for 36%

profile of v8, /device:TPU:0, one launch (start us, length us, event | category | flops | bytes accessed | tf_op | source)
XLA Modules:
  0.0 28.9 jit_solution(8396012164739347711)
XLA Ops:
  1.3 0.0 copy-start.1
  1.3 0.9 %broadcast_select_fusion = (bf16[4,1,64,128]{3,2,1,0:T(8,128)(2,1)S(1)}, bf16[4,1,64,128]{3,2,1,0:T(8,128)(2,1)S(1)}) fusion(pred[]{:T(512)S(6)} %eq.15, bf16[4,1,128,128]{3,2,1,0:T(8,128)(2,1)} %middle.6), kind=kLoop, calls=%fused_computation.5 | loop fusion | flops 65536 | bytes 262145 | tf_op jit(solution)/shard_map/jit(_where)/select_n | solution.py:64
  2.2 0.0 copy-done.1
  2.3 0.1 pad.5.clone
  2.4 0.1 maximum_maximum_fusion.1
  2.5 0.0 copy-start.2
  2.5 0.5 %collective-permute-start.1 = (bf16[304,128]{1,0:T(8,128)(2,1)S(1)}, bf16[304,128]{1,0:T(8,128)(2,1)S(1)}, u32[]{:S(2)}, u32[]{:S(2)}) collective-permute-start(bf16[304,128]{1,0:T(8,128)(2,1)S(1)} %get-tuple-element.49), channel_id=1, source_target_pairs={{0,1},{1,0},{2,4},{3,5},{4,2},{5,3},{6,8},{7,9},{8,6},{9,7},{10,12... | collective-permute-start | bytes 233480 | tf_op jit(solution)/shard_map/ppermute | solution.py:369
  3.0 4.0 %collective-permute-start = (bf16[304,128]{1,0:T(8,128)(2,1)S(1)}, bf16[304,128]{1,0:T(8,128)(2,1)S(1)}, u32[]{:S(2)}, u32[]{:S(2)}) collective-permute-start(bf16[304,128]{1,0:T(8,128)(2,1)S(1)} %get-tuple-element.50), channel_id=1, source_target_pairs={{0,2},{1,3},{2,0},{3,1},{4,6},{5,7},{6,4},{7,5},{8,10},{9,11},{10,... | collective-permute-start | bytes 233480 | tf_op jit(solution)/shard_map/ppermute | solution.py:368
  7.0 0.0 copy-done
  7.0 0.1 collective-permute-start.2
  7.1 0.0 copy-done.2
  7.1 3.2 %src_inner.1 = (f32[4,1,128,128]{3,2,1,0:T(8,128)S(1)}, f32[4,1,128,128]{3,2,1,0:T(8,128)S(1)}, f32[16,128]{1,0:T(8,128)S(1)}) custom-call(s32[1]{0:T(128)S(6)} %copy.15.limit, bf16[4,1,128,128]{3,2,1,0:T(8,128)(2,1)S(1)} %copy-done, bf16[4,1,128,128]{3,2,1,0:T(8,128)(2,1)S(1)} %copy-done.2, s32[1,128,128]{2,1,0:T(8,128)S(1)} %copy-done.1), custom_call_target="tpu_custom_call" | custom-call | flops 21725184 | bytes 891289 | tf_op jit(solution)/shard_map/src_inner/pallas_call | solution.py:351
  10.3 0.0 collective-permute-done.1.odd_in.odd_marks
  10.3 1.1 %collective-permute-done.even_in.even_marks = bf16[304,128]{1,0:T(8,128)(2,1)S(1)} collective-permute-done((bf16[304,128]{1,0:T(8,128)(2,1)S(1)}, bf16[304,128]{1,0:T(8,128)(2,1)S(1)}, u32[]{:S(2)}, u32[]{:S(2)}) %collective-permute-start) | collective-permute-done | bytes 77856 | tf_op jit(solution)/shard_map/ppermute | solution.py:368
  11.4 1.3 %energy.1 = f32[32,2,128]{2,1,0:T(2,128)} custom-call(s32[1]{0:T(128)S(6)} %copy.15.limit, bf16[4,1,128,128]{3,2,1,0:T(8,128)(2,1)S(1)} %copy-done, s32[1,128,128]{2,1,0:T(8,128)S(1)} %copy-done.1, bf16[304,128]{1,0:T(8,128)(2,1)S(1)} %collective-permute-done.even_in.even_marks, bf16[304,128]{1,0:T(8,128)(2,1)S(1)} %collective-permute-done.1.odd_in.odd_marks, ...), custom_call_target="tpu_custom_call" | custom-call | flops 3833856 | bytes 157286 | tf_op jit(solution)/shard_map/energy/pallas_call | solution.py:351
  12.8 1.3 %src_outer.1 = (f32[4,1,128,128]{3,2,1,0:T(8,128)S(1)}, f32[4,1,128,128]{3,2,1,0:T(8,128)S(1)}) custom-call(s32[1]{0:T(128)S(6)} %copy.15.limit, bf16[4,1,128,128]{3,2,1,0:T(8,128)(2,1)S(1)} %copy-done, s32[1,128,128]{2,1,0:T(8,128)S(1)} %copy-done.1, ...), custom_call_target="tpu_custom_call", output_to_operand_aliasing={{0}: (7, {}), {1}: (8, {})} | custom-call | tf_op jit(solution)/shard_map/src_outer/pallas_call | solution.py:351
  14.1 0.1 collective-permute-start.3
  14.2 6.6 %all-to-all-start = ((f32[32,2,128]{2,1,0:T(2,128)}), f32[32,2,128]{2,1,0:T(2,128)S(1)}, u32[]{:S(2)}, u32[]{:S(2)}) async-start(f32[32,2,128]{2,1,0:T(2,128)} %energy.1), calls=%async_computation | async-start | bytes 65536 | tf_op jit(solution)/shard_map/all_to_all | solution.py:388
  20.8 3.1 %rcv_inner.1 = (f32[4,1,128,128]{3,2,1,0:T(8,128)S(1)}, f32[4,1,128,128]{3,2,1,0:T(8,128)S(1)}) custom-call(s32[1]{0:T(128)S(6)} %copy.15.limit, bf16[4,1,128,128]{3,2,1,0:T(8,128)(2,1)S(1)} %copy-done.2, bf16[4,1,128,128]{3,2,1,0:T(8,128)(2,1)S(1)} %copy-done, s32[1,128,128]{2,1,0:T(8,128)S(1)} %copy-done.1), custom_call_target="tpu_custom_call" | custom-call | tf_op jit(solution)/shard_map/rcv_inner/pallas_call | solution.py:351
  23.9 0.0 collective-permute-done.2.even_in
  23.9 0.0 collective-permute-done.3.odd_in
  23.9 1.3 %rcv_outer.1 = (f32[4,1,128,128]{3,2,1,0:T(8,128)S(1)}, f32[4,1,128,128]{3,2,1,0:T(8,128)S(1)}) custom-call(s32[1]{0:T(128)S(6)} %copy.15.limit, bf16[4,1,128,128]{3,2,1,0:T(8,128)(2,1)S(1)} %copy-done.2, s32[1,128,128]{2,1,0:T(8,128)S(1)} %copy-done.1, ...), custom_call_target="tpu_custom_call", output_to_operand_aliasing={{0}: (7, {}), {1}: (8, {})} | custom-call | tf_op jit(solution)/shard_map/rcv_outer/pallas_call | solution.py:351
  25.3 2.7 %all-to-all-done.sums = f32[32,2,128]{2,1,0:T(2,128)S(1)} async-done(((f32[32,2,128]{2,1,0:T(2,128)}), f32[32,2,128]{2,1,0:T(2,128)S(1)}, u32[]{:S(2)}, u32[]{:S(2)}) %all-to-all-start) | async-done | bytes 32800 | tf_op jit(solution)/shard_map/all_to_all | solution.py:388
  28.0 0.9 %combine.1 = (bf16[4,1,128,128]{3,2,1,0:T(8,128)(2,1)}, bf16[4,1,128,128]{3,2,1,0:T(8,128)(2,1)}, f32[1,128]{1,0:T(1,128)}) custom-call(f32[32,2,128]{2,1,0:T(2,128)S(1)} %all-to-all-done.sums, f32[4,1,128,128]{3,2,1,0:T(8,128)S(1)} %get-tuple-element.35.src_heavy, f32[4,1,128,128]{3,2,1,0:T(8,128)S(1)} %get-tuple-element.36.src_plain, ...), custom_call_target="tpu_custom_call" | custom-call | tf_op jit(solution)/shard_map/combine/pallas_call | solution.py:351
  (6 shorter events, 0.0 us)
Async XLA Ops:
  1.3 0.9 %copy-start.1 = (s32[1,128,128]{2,1,0:T(8,128)S(1)}, s32[1,128,128]{2,1,0:T(8,128)}, u32[]{:S(2)}) copy-start(s32[1,128,128]{2,1,0:T(8,128)} %sat.9) | copy-start | bytes 196612
  2.4 4.6 %copy-start = (bf16[4,1,128,128]{3,2,1,0:T(8,128)(2,1)S(1)}, bf16[4,1,128,128]{3,2,1,0:T(8,128)(2,1)}, u32[]{:S(2)}) copy-start(bf16[4,1,128,128]{3,2,1,0:T(8,128)(2,1)} %field.2) | copy-start | bytes 393220
  2.5 4.6 %copy-start.2 = (bf16[4,1,128,128]{3,2,1,0:T(8,128)(2,1)S(1)}, bf16[4,1,128,128]{3,2,1,0:T(8,128)(2,1)}, u32[]{:S(2)}) copy-start(bf16[4,1,128,128]{3,2,1,0:T(8,128)(2,1)} %middle.6) | copy-start | bytes 393220
  2.5 7.8 %collective-permute-start.1 = (bf16[304,128]{1,0:T(8,128)(2,1)S(1)}, bf16[304,128]{1,0:T(8,128)(2,1)S(1)}, u32[]{:S(2)}, u32[]{:S(2)}) collective-permute-start(bf16[304,128]{1,0:T(8,128)(2,1)S(1)} %get-tuple-element.49), channel_id=1, source_target_pairs={{0,1},{1,0},{2,4},{3,5},{4,2},{5,3},{6,8},{7,9},{8,6},{9,7},{10,12... | collective-permute-start | bytes 233480 | tf_op jit(solution)/shard_map/ppermute | solution.py:369
  3.0 8.4 %collective-permute-start = (bf16[304,128]{1,0:T(8,128)(2,1)S(1)}, bf16[304,128]{1,0:T(8,128)(2,1)S(1)}, u32[]{:S(2)}, u32[]{:S(2)}) collective-permute-start(bf16[304,128]{1,0:T(8,128)(2,1)S(1)} %get-tuple-element.50), channel_id=1, source_target_pairs={{0,2},{1,3},{2,0},{3,1},{4,6},{5,7},{6,4},{7,5},{8,10},{9,11},{10,... | collective-permute-start | bytes 233480 | tf_op jit(solution)/shard_map/ppermute | solution.py:368
  7.0 16.9 %collective-permute-start.2 = (bf16[256,128]{1,0:T(8,128)(2,1)S(1)}, bf16[256,128]{1,0:T(8,128)(2,1)S(1)}, u32[]{:S(2)}, u32[]{:S(2)}) collective-permute-start(bf16[256,128]{1,0:T(8,128)(2,1)S(1)} %bitcast.13), channel_id=1, source_target_pairs={{0,2},{1,3},{2,0},{3,1},{4,6},{5,7},{6,4},{7,5},{8,10},{9,11},{10,... | collective-permute-start | bytes 196616 | tf_op jit(solution)/shard_map/ppermute | solution.py:370
  14.1 9.8 %collective-permute-start.3 = (bf16[256,128]{1,0:T(8,128)(2,1)S(1)}, bf16[256,128]{1,0:T(8,128)(2,1)S(1)}, u32[]{:S(2)}, u32[]{:S(2)}) collective-permute-start(bf16[256,128]{1,0:T(8,128)(2,1)S(1)} %bitcast.14), channel_id=1, source_target_pairs={{0,1},{1,0},{2,4},{3,5},{4,2},{5,3},{6,8},{7,9},{8,6},{9,7},{10,12... | collective-permute-start | bytes 196616 | tf_op jit(solution)/shard_map/ppermute | solution.py:401
  14.2 13.8 %all-to-all-start = ((f32[32,2,128]{2,1,0:T(2,128)}), f32[32,2,128]{2,1,0:T(2,128)S(1)}, u32[]{:S(2)}, u32[]{:S(2)}) async-start(f32[32,2,128]{2,1,0:T(2,128)} %energy.1), calls=%async_computation | async-start | bytes 65536 | tf_op jit(solution)/shard_map/all_to_all | solution.py:388

commit v9 on v7

--- a/solution.py
+++ b/solution.py
@@ -356,7 +356,7 @@
             scratch_shapes=scratch,
             input_output_aliases=aliases,
             cost_estimate=pl.CostEstimate(
-                flops=int(24 * image_cells * share), bytes_accessed=1 << 20, transcendentals=0
+                flops=int(24 * image_cells * share), bytes_accessed=int(share * (1 << 20)), transcendentals=0
             ),
             compiler_params=grant,
             name=name,
@@ -377,6 +377,8 @@
         [extended, caps],
         0.85,
     )
+    inner, ahead = lax.optimization_barrier((inner, src))
+    odd_late = lax.ppermute(for_odd(*edges(ahead, 2, REACH)), DEVICES, odd_route)
     sums = call(
         energy_kernel,
         "energy",
@@ -387,7 +389,7 @@
     )
     gathered = lax.all_to_all(sums, DEVICES, 0, 0, tiled=True)
 
-    sums, heavy, plain, ahead = lax.optimization_barrier((sums, heavy, plain, src))
+    sums, heavy, plain, ahead, odd_late = lax.optimization_barrier((sums, heavy, plain, src, odd_late))
     heavy, plain = call(
         outer_kernel,
         "src_outer",
@@ -397,8 +399,6 @@
         0.25,
         {7: 0, 8: 1},
     )
-    heavy, plain, ahead = lax.optimization_barrier((heavy, plain, ahead))
-    odd_late = lax.ppermute(for_odd(*edges(ahead, 2, REACH)), DEVICES, odd_route)
     pieces = call(
         inner_kernel,
         "rcv_inner",

time: 29.1 us -> 27.4 us (0.942); the launches traced: 28.9 us -> 27.5 us
  waiting for transfers between devices: 5.05 us -> 1.41 us
  Pallas kernels: 9.98 us -> 11.2 us
  starting transfers between devices: 11.2 us -> 12.3 us
    ppermute x1, starting transfers between devices: 0.07 us -> 3.03 us  [local(): lax.ppermute(for_even(*edges(src, 2, REACH)), DEVICES, even_route)]
    all_to_all x1, waiting for transfers between devices: 3.32 us -> 1.4 us  [local(): gathered = lax.all_to_all(sums, DEVICES, 0, 0, tiled=True)]
    all_to_all x1, starting transfers between devices: 6.58 us -> 4.71 us  [local(): gathered = lax.all_to_all(sums, DEVICES, 0, 0, tiled=True)]
    ppermute x1, waiting for transfers between devices: 1.72 us -> 0.01 us  [local(): even = lax.ppermute(even, DEVICES, even_route)]
    pallas_call x6, Pallas kernels: 9.98 us -> 11.2 us  [call(): pl.pallas_call(kernel, out_shape=out_shape, in_specs=[SMEM if operand is...]
  transfers between devices with their start and end apart: 5 -> 5, of which waited for: 2 -> 1; matrix products, arithmetic and copies ran while one was open for 0% -> 0% of each run, Pallas kernels for 32% -> 38%
where the time goes in v9:
time: 27.4 us; the launch traced here: 27.5 us
  starting transfers between devices  12.3 us (45%)
  Pallas kernels  11.2 us (41%)
  between operations  1.43 us (5%)
  waiting for transfers between devices  1.41 us (5%)
  other arithmetic  1.07 us (4%)
    pallas_call x6, Pallas kernels, call(): pl.pallas_call(kernel, out_shape=out_shape, in_specs=[SMEM if operand is...  11.2 us
    all_to_all x1, starting transfers between devices, local(): gathered = lax.all_to_all(sums, DEVICES, 0, 0, tiled=True)  4.71 us
    ppermute x1, starting transfers between devices, local(): even = lax.ppermute(even, DEVICES, even_route)  3.98 us
    ppermute x1, starting transfers between devices, local(): lax.ppermute(for_even(*edges(src, 2, REACH)), DEVICES, even_route)  3.03 us
    all_to_all x1, waiting for transfers between devices, local(): gathered = lax.all_to_all(sums, DEVICES, 0, 0, tiled=True)  1.4 us
    select_n x4, other arithmetic, for_even(): return jnp.where(lax.axis_index('inline') % 2 == 0, high, low)  0.95 us
  transfers between devices with their start and end apart: 5, of which 1 were waited for; matrix products, arithmetic and copies ran while one was open for 0% of the time, Pallas kernels for 38%

profile of v9, /device:TPU:0, one launch (start us, length us, event | category | flops | bytes accessed | tf_op | source)
XLA Modules:
  0.0 27.5 jit_solution(43812155684251855)
XLA Ops:
  1.3 0.0 copy-start.1
  1.3 0.9 %broadcast_select_fusion = (bf16[4,1,64,128]{3,2,1,0:T(8,128)(2,1)S(1)}, bf16[4,1,64,128]{3,2,1,0:T(8,128)(2,1)S(1)}) fusion(pred[]{:T(512)S(6)} %eq.15, bf16[4,1,128,128]{3,2,1,0:T(8,128)(2,1)} %middle.6), kind=kLoop, calls=%fused_computation.5 | loop fusion | flops 65536 | bytes 262145 | tf_op jit(solution)/shard_map/jit(_where)/select_n | solution.py:64
  2.2 0.0 copy-done.1
  2.3 0.1 pad.5.clone
  2.4 0.0 copy-start
  2.4 0.1 maximum_maximum_fusion.1
  2.5 0.5 %collective-permute-start.1 = (bf16[304,128]{1,0:T(8,128)(2,1)S(1)}, bf16[304,128]{1,0:T(8,128)(2,1)S(1)}, u32[]{:S(2)}, u32[]{:S(2)}) collective-permute-start(bf16[304,128]{1,0:T(8,128)(2,1)S(1)} %get-tuple-element.49), channel_id=1, source_target_pairs={{0,1},{1,0},{2,4},{3,5},{4,2},{5,3},{6,8},{7,9},{8,6},{9,7},{10,12... | collective-permute-start | bytes 233480 | tf_op jit(solution)/shard_map/ppermute | solution.py:369
  3.0 4.0 %collective-permute-start = (bf16[304,128]{1,0:T(8,128)(2,1)S(1)}, bf16[304,128]{1,0:T(8,128)(2,1)S(1)}, u32[]{:S(2)}, u32[]{:S(2)}) collective-permute-start(bf16[304,128]{1,0:T(8,128)(2,1)S(1)} %get-tuple-element.50), channel_id=1, source_target_pairs={{0,2},{1,3},{2,0},{3,1},{4,6},{5,7},{6,4},{7,5},{8,10},{9,11},{10,... | collective-permute-start | bytes 233480 | tf_op jit(solution)/shard_map/ppermute | solution.py:368
  7.0 0.0 copy-done
  7.0 0.0 copy-done.2
  7.0 3.2 %src_inner.1 = (f32[4,1,128,128]{3,2,1,0:T(8,128)S(1)}, f32[4,1,128,128]{3,2,1,0:T(8,128)S(1)}, f32[16,128]{1,0:T(8,128)S(1)}) custom-call(s32[1]{0:T(128)S(6)} %copy.15.limit, bf16[4,1,128,128]{3,2,1,0:T(8,128)(2,1)S(1)} %copy-done, bf16[4,1,128,128]{3,2,1,0:T(8,128)(2,1)S(1)} %copy-done.2, s32[1,128,128]{2,1,0:T(8,128)S(1)} %copy-done.1), custom_call_target="tpu_custom_call" | custom-call | flops 21725184 | bytes 891289 | tf_op jit(solution)/shard_map/src_inner/pallas_call | solution.py:351
  10.2 0.1 collective-permute-start.2
  10.3 3.0 %collective-permute-start.3 = (bf16[256,128]{1,0:T(8,128)(2,1)S(1)}, bf16[256,128]{1,0:T(8,128)(2,1)S(1)}, u32[]{:S(2)}, u32[]{:S(2)}) collective-permute-start(bf16[256,128]{1,0:T(8,128)(2,1)S(1)} %bitcast.13), channel_id=1, source_target_pairs={{0,2},{1,3},{2,0},{3,1},{4,6},{5,7},{6,4},{7,5},{8,10},{9,11},{10,... | collective-permute-start | bytes 196616 | tf_op jit(solution)/shard_map/ppermute | solution.py:370
  13.3 0.0 collective-permute-done.1.odd_in.odd_marks
  13.3 0.0 collective-permute-done.even_in.even_marks
  13.3 1.3 %energy.1 = f32[32,2,128]{2,1,0:T(2,128)} custom-call(s32[1]{0:T(128)S(6)} %copy.15.limit, bf16[4,1,128,128]{3,2,1,0:T(8,128)(2,1)S(1)} %copy-done, s32[1,128,128]{2,1,0:T(8,128)S(1)} %copy-done.1, bf16[304,128]{1,0:T(8,128)(2,1)S(1)} %collective-permute-done.even_in.even_marks, bf16[304,128]{1,0:T(8,128)(2,1)S(1)} %collective-permute-done.1.odd_in.odd_marks, ...), custom_call_target="tpu_custom_call" | custom-call | flops 3833856 | bytes 157286 | tf_op jit(solution)/shard_map/energy/pallas_call | solution.py:351
  14.7 4.7 %all-to-all-start = ((f32[32,2,128]{2,1,0:T(2,128)}), f32[32,2,128]{2,1,0:T(2,128)S(1)}, u32[]{:S(2)}, u32[]{:S(2)}) async-start(f32[32,2,128]{2,1,0:T(2,128)} %energy.1), calls=%async_computation | async-start | bytes 65536 | tf_op jit(solution)/shard_map/all_to_all | solution.py:390
  19.4 0.0 collective-permute-done.2.odd_in
  19.4 1.3 %src_outer.1 = (f32[4,1,128,128]{3,2,1,0:T(8,128)S(1)}, f32[4,1,128,128]{3,2,1,0:T(8,128)S(1)}) custom-call(s32[1]{0:T(128)S(6)} %copy.15.limit, bf16[4,1,128,128]{3,2,1,0:T(8,128)(2,1)S(1)} %copy-done, s32[1,128,128]{2,1,0:T(8,128)S(1)} %copy-done.1, ...), custom_call_target="tpu_custom_call", output_to_operand_aliasing={{0}: (7, {}), {1}: (8, {})} | custom-call | flops 6389760 | bytes 262144 | tf_op jit(solution)/shard_map/src_outer/pallas_call | solution.py:351
  20.7 3.1 %rcv_inner.1 = (f32[4,1,128,128]{3,2,1,0:T(8,128)S(1)}, f32[4,1,128,128]{3,2,1,0:T(8,128)S(1)}) custom-call(s32[1]{0:T(128)S(6)} %copy.15.limit, bf16[4,1,128,128]{3,2,1,0:T(8,128)(2,1)S(1)} %copy-done.2, bf16[4,1,128,128]{3,2,1,0:T(8,128)(2,1)S(1)} %copy-done, s32[1,128,128]{2,1,0:T(8,128)S(1)} %copy-done.1), custom_call_target="tpu_custom_call" | custom-call | flops 21725184 | bytes 891289 | tf_op jit(solution)/shard_map/rcv_inner/pallas_call | solution.py:351
  23.9 0.0 collective-permute-done.3.even_in
  23.9 1.3 %rcv_outer.1 = (f32[4,1,128,128]{3,2,1,0:T(8,128)S(1)}, f32[4,1,128,128]{3,2,1,0:T(8,128)S(1)}) custom-call(s32[1]{0:T(128)S(6)} %copy.15.limit, bf16[4,1,128,128]{3,2,1,0:T(8,128)(2,1)S(1)} %copy-done.2, s32[1,128,128]{2,1,0:T(8,128)S(1)} %copy-done.1, ...), custom_call_target="tpu_custom_call", output_to_operand_aliasing={{0}: (7, {}), {1}: (8, {})} | custom-call | flops 6389760 | bytes 262144 | tf_op jit(solution)/shard_map/rcv_outer/pallas_call | solution.py:351
  25.2 1.4 %all-to-all-done.sums = f32[32,2,128]{2,1,0:T(2,128)S(1)} async-done(((f32[32,2,128]{2,1,0:T(2,128)}), f32[32,2,128]{2,1,0:T(2,128)S(1)}, u32[]{:S(2)}, u32[]{:S(2)}) %all-to-all-start) | async-done | bytes 32800 | tf_op jit(solution)/shard_map/all_to_all | solution.py:390
  26.6 0.9 %combine.1 = (bf16[4,1,128,128]{3,2,1,0:T(8,128)(2,1)}, bf16[4,1,128,128]{3,2,1,0:T(8,128)(2,1)}, f32[1,128]{1,0:T(1,128)}) custom-call(f32[32,2,128]{2,1,0:T(2,128)S(1)} %all-to-all-done.sums, f32[4,1,128,128]{3,2,1,0:T(8,128)S(1)} %get-tuple-element.35.src_heavy, f32[4,1,128,128]{3,2,1,0:T(8,128)S(1)} %get-tuple-element.36.src_plain, ...), custom_call_target="tpu_custom_call" | custom-call | tf_op jit(solution)/shard_map/combine/pallas_call | solution.py:351
  (6 shorter events, 0.0 us)
Async XLA Ops:
  1.3 0.9 %copy-start.1 = (s32[1,128,128]{2,1,0:T(8,128)S(1)}, s32[1,128,128]{2,1,0:T(8,128)}, u32[]{:S(2)}) copy-start(s32[1,128,128]{2,1,0:T(8,128)} %sat.9) | copy-start | bytes 196612
  2.4 4.6 %copy-start = (bf16[4,1,128,128]{3,2,1,0:T(8,128)(2,1)S(1)}, bf16[4,1,128,128]{3,2,1,0:T(8,128)(2,1)}, u32[]{:S(2)}) copy-start(bf16[4,1,128,128]{3,2,1,0:T(8,128)(2,1)} %field.2) | copy-start | bytes 393220
  2.4 4.6 %copy-start.2 = (bf16[4,1,128,128]{3,2,1,0:T(8,128)(2,1)S(1)}, bf16[4,1,128,128]{3,2,1,0:T(8,128)(2,1)}, u32[]{:S(2)}) copy-start(bf16[4,1,128,128]{3,2,1,0:T(8,128)(2,1)} %middle.6) | copy-start | bytes 393220
  2.5 10.8 %collective-permute-start.1 = (bf16[304,128]{1,0:T(8,128)(2,1)S(1)}, bf16[304,128]{1,0:T(8,128)(2,1)S(1)}, u32[]{:S(2)}, u32[]{:S(2)}) collective-permute-start(bf16[304,128]{1,0:T(8,128)(2,1)S(1)} %get-tuple-element.49), channel_id=1, source_target_pairs={{0,1},{1,0},{2,4},{3,5},{4,2},{5,3},{6,8},{7,9},{8,6},{9,7},{10,12... | collective-permute-start | bytes 233480 | tf_op jit(solution)/shard_map/ppermute | solution.py:369
  3.0 10.3 %collective-permute-start = (bf16[304,128]{1,0:T(8,128)(2,1)S(1)}, bf16[304,128]{1,0:T(8,128)(2,1)S(1)}, u32[]{:S(2)}, u32[]{:S(2)}) collective-permute-start(bf16[304,128]{1,0:T(8,128)(2,1)S(1)} %get-tuple-element.50), channel_id=1, source_target_pairs={{0,2},{1,3},{2,0},{3,1},{4,6},{5,7},{6,4},{7,5},{8,10},{9,11},{10,... | collective-permute-start | bytes 233480 | tf_op jit(solution)/shard_map/ppermute | solution.py:368
  10.2 9.2 %collective-permute-start.2 = (bf16[256,128]{1,0:T(8,128)(2,1)S(1)}, bf16[256,128]{1,0:T(8,128)(2,1)S(1)}, u32[]{:S(2)}, u32[]{:S(2)}) collective-permute-start(bf16[256,128]{1,0:T(8,128)(2,1)S(1)} %bitcast.14), channel_id=1, source_target_pairs={{0,1},{1,0},{2,4},{3,5},{4,2},{5,3},{6,8},{7,9},{8,6},{9,7},{10,12... | collective-permute-start | bytes 196616 | tf_op jit(solution)/shard_map/ppermute | solution.py:381
  10.3 13.6 %collective-permute-start.3 = (bf16[256,128]{1,0:T(8,128)(2,1)S(1)}, bf16[256,128]{1,0:T(8,128)(2,1)S(1)}, u32[]{:S(2)}, u32[]{:S(2)}) collective-permute-start(bf16[256,128]{1,0:T(8,128)(2,1)S(1)} %bitcast.13), channel_id=1, source_target_pairs={{0,2},{1,3},{2,0},{3,1},{4,6},{5,7},{6,4},{7,5},{8,10},{9,11},{10,... | collective-permute-start | bytes 196616 | tf_op jit(solution)/shard_map/ppermute | solution.py:370
  14.7 12.0 %all-to-all-start = ((f32[32,2,128]{2,1,0:T(2,128)}), f32[32,2,128]{2,1,0:T(2,128)S(1)}, u32[]{:S(2)}, u32[]{:S(2)}) async-start(f32[32,2,128]{2,1,0:T(2,128)} %energy.1), calls=%async_computation | async-start | bytes 65536 | tf_op jit(solution)/shard_map/all_to_all | solution.py:390

commit v10 on v9

--- a/solution.py
+++ b/solution.py
@@ -34,7 +34,8 @@
 
 def payload_layout(times, lines):
     mask_at = times * lines * REACH
-    return mask_at, mask_at + lines * H
+    limit_at = mask_at + lines * H
+    return mask_at, limit_at, limit_at + LIMIT_ROWS
 
 
 def by_parity(even, odd, work):
@@ -68,21 +69,20 @@
     return for_even(high, low)
 
 
-def payloads(rcv, sat, limit):
+def payloads(src, rcv, sat, limit):
     depth = rcv.shape[-1]
     rows = edges(rcv, 2, REACH)
     rows = for_even(*rows), for_odd(*rows)
-    *rows, sat = lax.optimization_barrier((*rows, sat))
+    *rows, sat, src = lax.optimization_barrier((*rows, sat, src))
     masks = edges((sat != 0).astype(jnp.bfloat16), 1, H)
     limits = jnp.full((LIMIT_ROWS, depth), limit[0]).astype(jnp.bfloat16)
-    return [
-        jnp.concatenate([part, choose(*masks), limits], axis=0) for part, choose in zip(rows, (for_even, for_odd))
-    ]
+    odd = jnp.concatenate([rows[1], for_odd(*masks), limits], axis=0)
+    return jnp.concatenate([rows[0], for_even(*masks), limits, for_even(*edges(src, 2, REACH))], axis=0), odd
 
 
 def unpack_marks(times, limit, sat, even_in, odd_in, caps, limits):
     lines, cells, depth = sat.shape
-    mask_at, limit_at = payload_layout(times, lines)
+    mask_at, limit_at, _ = payload_layout(times, lines)
 
     def halo(arrived, low, there):
         row_at = 0 if low else H + cells
@@ -98,15 +98,16 @@
     limits[pl.ds(H, cells), :] = jnp.full((cells, depth), limit[0], jnp.int32).astype(jnp.float32)
 
 
-def unpack_halo(even_in, odd_in, low_out, high_out):
+def unpack_halo(even_in, odd_in, low_out, high_out, even_at=0):
     times, lines, _, depth = low_out.shape
     blank = jnp.zeros((ROWS, depth), jnp.float32)
 
     def halo(arrived, low, there):
         out, field_at, blank_at = (low_out, 0, REACH) if low else (high_out, ROWS, 0)
+        start = even_at if arrived is even_in else 0
         for t in range(times):
             for y in range(lines):
-                at = (t * lines + y) * REACH
+                at = start + (t * lines + y) * REACH
                 out[t, y, pl.ds(field_at, REACH), :] = arrived[pl.ds(at, REACH), :].astype(jnp.float32) * there
                 out[t, y, pl.ds(blank_at, ROWS), :] = blank
 
@@ -275,11 +276,14 @@
     sums[...] = jnp.broadcast_to(jnp.concatenate(rows, axis=0)[None], sums.shape)
 
 
-def outer_kernel(limit, middle, sat, even_marks, odd_marks, even_in, odd_in, heavy_in, plain_in, heavy, plain, *scratch):
-    low, high, caps, limits = scratch
+def outer_kernel(source, limit, middle, sat, even_in, odd_in, *refs):
+    heavy, plain, low, high, caps, limits = refs[-6:]
     times, lines, cells, depth = middle.shape
-    unpack_marks(times, limit, sat, even_marks, odd_marks, caps, limits)
-    unpack_halo(even_in, odd_in, low, high)
+    unpack_marks(times, limit, sat, even_in, odd_in, caps, limits)
+    if source:
+        unpack_halo(even_in, refs[0], low, high, payload_layout(times, lines)[2])
+    else:
+        unpack_halo(even_in, odd_in, low, high)
 
     def visit(y, at, center, offsets, far_at):
         rows = pl.ds(at, ROWS)
@@ -363,11 +367,10 @@
         )(*operands)
 
     src, rcv, sat = source_field, receiver_field, sat_mask
-    even, odd = payloads(rcv, sat, offset_range)
+    even, odd = payloads(src, rcv, sat, offset_range)
     even_route, odd_route = exchanges(size, lax.axis_size("xline"))
     even = lax.ppermute(even, DEVICES, even_route)
     odd = lax.ppermute(odd, DEVICES, odd_route)
-    even_late = lax.ppermute(for_even(*edges(src, 2, REACH)), DEVICES, even_route)
 
     heavy, plain, inner = call(
         inner_kernel,
@@ -391,13 +394,13 @@
 
     sums, heavy, plain, ahead, odd_late = lax.optimization_barrier((sums, heavy, plain, src, odd_late))
     heavy, plain = call(
-        outer_kernel,
+        functools.partial(outer_kernel, False),
         "src_outer",
         (total, total),
-        (offset_range, ahead, sat, even, odd, even, odd, heavy, plain),
+        (offset_range, ahead, sat, even, odd, heavy, plain),
         [edge, edge, caps, limits],
         0.25,
-        {7: 0, 8: 1},
+        {5: 0, 6: 1},
     )
     pieces = call(
         inner_kernel,
@@ -408,13 +411,13 @@
         0.85,
     )
     pieces = call(
-        outer_kernel,
+        functools.partial(outer_kernel, True),
         "rcv_outer",
         (total, total),
-        (offset_range, rcv, sat, even, odd, even_late, odd_late, *pieces),
+        (offset_range, rcv, sat, even, odd, odd_late, *pieces),
         [edge, edge, caps, limits],
         0.25,
-        {7: 0, 8: 1},
+        {6: 0, 7: 1},
     )
 
     cell_count = float(lines * lax.axis_size("xline") * cells * size * depth * (2 * H + 1))

time: 27.4 us -> 26.6 us (0.971); the launches traced: 27.5 us -> 26.3 us
  starting transfers between devices: 12.3 us -> 9.1 us
  waiting for transfers between devices: 1.41 us -> 4.48 us
  Pallas kernels: 11.2 us -> 9.99 us
    ppermute x1 -> x0, starting transfers between devices: 3.03 us -> none  [local(): lax.ppermute(for_even(*edges(src, 2, REACH)), DEVICES, even_route)]
    ppermute x1, waiting for transfers between devices: 0.01 us -> 2.48 us  [local(): even = lax.ppermute(even, DEVICES, even_route)]
    pallas_call x6, Pallas kernels: 11.2 us -> 9.99 us  [call(): pl.pallas_call(kernel, out_shape=out_shape, in_specs=[SMEM if operand is...]
    all_to_all x1, waiting for transfers between devices: 1.4 us -> 2 us  [local(): gathered = lax.all_to_all(sums, DEVICES, 0, 0, tiled=True)]
    unnamed x6, local copies, waits for them, and re-layouts: 0.01 us -> 0.33 us
  transfers between devices with their start and end apart: 5 -> 4, of which waited for: 1 -> 2; matrix products, arithmetic and copies ran while one was open for 0% -> 0% of each run, Pallas kernels for 38% -> 35%
where the time goes in v10:
time: 26.6 us; the launch traced here: 26.3 us
  Pallas kernels  9.99 us (38%)
  starting transfers between devices  9.1 us (34%)
  waiting for transfers between devices  4.48 us (17%)
  between operations  1.44 us (5%)
  other arithmetic  0.98 us (4%)
  local copies, waits for them, and re-layouts  0.34 us (1%)
    pallas_call x6, Pallas kernels, call(): pl.pallas_call(kernel, out_shape=out_shape, in_specs=[SMEM if operand is...  9.99 us
    all_to_all x1, starting transfers between devices, local(): gathered = lax.all_to_all(sums, DEVICES, 0, 0, tiled=True)  4.79 us
    ppermute x1, starting transfers between devices, local(): even = lax.ppermute(even, DEVICES, even_route)  3.73 us
    ppermute x1, waiting for transfers between devices, local(): even = lax.ppermute(even, DEVICES, even_route)  2.48 us
    all_to_all x1, waiting for transfers between devices, local(): gathered = lax.all_to_all(sums, DEVICES, 0, 0, tiled=True)  2 us
    select_n x4, other arithmetic, for_even(): return jnp.where(lax.axis_index('inline') % 2 == 0, high, low)  0.95 us
  transfers between devices with their start and end apart: 4, of which 2 were waited for; matrix products, arithmetic and copies ran while one was open for 0% of the time, Pallas kernels for 35%

profile of v10, /device:TPU:0, one launch (start us, length us, event | category | flops | bytes accessed | tf_op | source)
XLA Modules:
  0.0 26.3 jit_solution(14329979060328699117)
XLA Ops:
  1.3 0.0 copy-start.1
  1.3 0.9 %broadcast_select_fusion = (bf16[4,1,64,128]{3,2,1,0:T(8,128)(2,1)S(1)}, bf16[4,1,64,128]{3,2,1,0:T(8,128)(2,1)S(1)}) fusion(pred[]{:T(512)S(6)} %eq.15, bf16[4,1,128,128]{3,2,1,0:T(8,128)(2,1)} %middle.6), kind=kLoop, calls=%fused_computation.5 | loop fusion | flops 65536 | bytes 262145 | tf_op jit(solution)/shard_map/jit(_where)/select_n | solution.py:65
  2.2 0.0 copy-done.1
  2.2 0.0 copy-start
  2.3 0.5 %collective-permute-start.1 = (bf16[304,128]{1,0:T(8,128)(2,1)S(1)}, bf16[304,128]{1,0:T(8,128)(2,1)S(1)}, u32[]{:S(2)}, u32[]{:S(2)}) collective-permute-start(bf16[304,128]{1,0:T(8,128)(2,1)S(1)} %pad_maximum_fusion.1), channel_id=1, source_target_pairs={{0,1},{1,0},{2,4},{3,5},{4,2},{5,3},{6,8},{7,9},{8,6},{9,7},{10,12... | collective-permute-start | bytes 233480 | tf_op jit(solution)/shard_map/ppermute | solution.py:373
  2.8 0.3 %copy-done = bf16[4,1,128,128]{3,2,1,0:T(8,128)(2,1)S(1)} copy-done((bf16[4,1,128,128]{3,2,1,0:T(8,128)(2,1)S(1)}, bf16[4,1,128,128]{3,2,1,0:T(8,128)(2,1)}, u32[]{:S(2)}) %copy-start) | copy-done | bytes 131096
  3.2 0.0 copy-start.2
  3.2 3.7 %collective-permute-start = (bf16[560,128]{1,0:T(8,128)(2,1)S(1)}, bf16[560,128]{1,0:T(8,128)(2,1)S(1)}, u32[]{:S(2)}, u32[]{:S(2)}) collective-permute-start(bf16[560,128]{1,0:T(8,128)(2,1)S(1)} %pad_maximum_fusion), channel_id=1, source_target_pairs={{0,2},{1,3},{2,0},{3,1},{4,6},{5,7},{6,4},{7,5},{8,10},{9,11},{10,... | collective-permute-start | bytes 430088 | tf_op jit(solution)/shard_map/ppermute | solution.py:372
  6.9 0.0 copy-done.2
  6.9 2.6 %src_inner.1 = (f32[4,1,128,128]{3,2,1,0:T(8,128)S(1)}, f32[4,1,128,128]{3,2,1,0:T(8,128)S(1)}, f32[16,128]{1,0:T(8,128)S(1)}) custom-call(s32[1]{0:T(128)S(6)} %copy.15.limit, bf16[4,1,128,128]{3,2,1,0:T(8,128)(2,1)S(1)} %copy-done, bf16[4,1,128,128]{3,2,1,0:T(8,128)(2,1)S(1)} %copy-done.2, s32[1,128,128]{2,1,0:T(8,128)S(1)} %copy-done.1), custom_call_target="tpu_custom_call" | custom-call | flops 21725184 | bytes 891289 | tf_op jit(solution)/shard_map/src_inner/pallas_call | solution.py:355
  9.5 0.1 collective-permute-start.2
  9.6 0.0 collective-permute-done.1.odd_in
  9.6 2.5 %collective-permute-done.even_in = bf16[560,128]{1,0:T(8,128)(2,1)S(1)} collective-permute-done((bf16[560,128]{1,0:T(8,128)(2,1)S(1)}, bf16[560,128]{1,0:T(8,128)(2,1)S(1)}, u32[]{:S(2)}, u32[]{:S(2)}) %collective-permute-start) | collective-permute-done | bytes 143392 | tf_op jit(solution)/shard_map/ppermute | solution.py:372
  12.1 1.3 %energy.1 = f32[32,2,128]{2,1,0:T(2,128)} custom-call(s32[1]{0:T(128)S(6)} %copy.15.limit, bf16[4,1,128,128]{3,2,1,0:T(8,128)(2,1)S(1)} %copy-done, s32[1,128,128]{2,1,0:T(8,128)S(1)} %copy-done.1, bf16[560,128]{1,0:T(8,128)(2,1)S(1)} %collective-permute-done.even_in, bf16[304,128]{1,0:T(8,128)(2,1)S(1)} %collective-permute-done.1.odd_in, ...), custom_call_target="tpu_custom_call" | custom-call | flops 3833856 | bytes 157286 | tf_op jit(solution)/shard_map/energy/pallas_call | solution.py:355
  13.4 4.8 %all-to-all-start = ((f32[32,2,128]{2,1,0:T(2,128)}), f32[32,2,128]{2,1,0:T(2,128)S(1)}, u32[]{:S(2)}, u32[]{:S(2)}) async-start(f32[32,2,128]{2,1,0:T(2,128)} %energy.1), calls=%async_computation | async-start | bytes 65536 | tf_op jit(solution)/shard_map/all_to_all | solution.py:393
  18.2 0.0 collective-permute-done.2.refs_0_
  18.2 1.3 %src_outer.1 = (f32[4,1,128,128]{3,2,1,0:T(8,128)S(1)}, f32[4,1,128,128]{3,2,1,0:T(8,128)S(1)}) custom-call(s32[1]{0:T(128)S(6)} %copy.15.limit, bf16[4,1,128,128]{3,2,1,0:T(8,128)(2,1)S(1)} %copy-done, s32[1,128,128]{2,1,0:T(8,128)S(1)} %copy-done.1, ...), custom_call_target="tpu_custom_call", output_to_operand_aliasing={{0}: (5, {}), {1}: (6, {})} | custom-call | flops 6389760 | bytes 262144 | tf_op jit(solution)/shard_map/src_outer/pallas_call | solution.py:355
  19.6 2.6 %rcv_inner.1 = (f32[4,1,128,128]{3,2,1,0:T(8,128)S(1)}, f32[4,1,128,128]{3,2,1,0:T(8,128)S(1)}) custom-call(s32[1]{0:T(128)S(6)} %copy.15.limit, bf16[4,1,128,128]{3,2,1,0:T(8,128)(2,1)S(1)} %copy-done.2, bf16[4,1,128,128]{3,2,1,0:T(8,128)(2,1)S(1)} %copy-done, s32[1,128,128]{2,1,0:T(8,128)S(1)} %copy-done.1), custom_call_target="tpu_custom_call" | custom-call | flops 21725184 | bytes 891289 | tf_op jit(solution)/shard_map/rcv_inner/pallas_call | solution.py:355
  22.1 1.3 %rcv_outer.1 = (f32[4,1,128,128]{3,2,1,0:T(8,128)S(1)}, f32[4,1,128,128]{3,2,1,0:T(8,128)S(1)}) custom-call(s32[1]{0:T(128)S(6)} %copy.15.limit, bf16[4,1,128,128]{3,2,1,0:T(8,128)(2,1)S(1)} %copy-done.2, s32[1,128,128]{2,1,0:T(8,128)S(1)} %copy-done.1, ...), custom_call_target="tpu_custom_call", output_to_operand_aliasing={{0}: (6, {}), {1}: (7, {})} | custom-call | flops 6389760 | bytes 262144 | tf_op jit(solution)/shard_map/rcv_outer/pallas_call | solution.py:355
  23.5 2.0 %all-to-all-done.sums = f32[32,2,128]{2,1,0:T(2,128)S(1)} async-done(((f32[32,2,128]{2,1,0:T(2,128)}), f32[32,2,128]{2,1,0:T(2,128)S(1)}, u32[]{:S(2)}, u32[]{:S(2)}) %all-to-all-start) | async-done | bytes 32800 | tf_op jit(solution)/shard_map/all_to_all | solution.py:393
  25.5 0.9 %combine.1 = (bf16[4,1,128,128]{3,2,1,0:T(8,128)(2,1)}, bf16[4,1,128,128]{3,2,1,0:T(8,128)(2,1)}, f32[1,128]{1,0:T(1,128)}) custom-call(f32[32,2,128]{2,1,0:T(2,128)S(1)} %all-to-all-done.sums, f32[4,1,128,128]{3,2,1,0:T(8,128)S(1)} %get-tuple-element.37.src_heavy, f32[4,1,128,128]{3,2,1,0:T(8,128)S(1)} %get-tuple-element.38.src_plain, ...), custom_call_target="tpu_custom_call" | custom-call | tf_op jit(solution)/shard_map/combine/pallas_call | solution.py:355
  (7 shorter events, 0.1 us)
Async XLA Ops:
  1.3 0.9 %copy-start.1 = (s32[1,128,128]{2,1,0:T(8,128)S(1)}, s32[1,128,128]{2,1,0:T(8,128)}, u32[]{:S(2)}) copy-start(s32[1,128,128]{2,1,0:T(8,128)} %sat.9) | copy-start | bytes 196612
  2.2 0.9 %copy-start = (bf16[4,1,128,128]{3,2,1,0:T(8,128)(2,1)S(1)}, bf16[4,1,128,128]{3,2,1,0:T(8,128)(2,1)}, u32[]{:S(2)}) copy-start(bf16[4,1,128,128]{3,2,1,0:T(8,128)(2,1)} %field.2) | copy-start | bytes 393220
  2.3 7.3 %collective-permute-start.1 = (bf16[304,128]{1,0:T(8,128)(2,1)S(1)}, bf16[304,128]{1,0:T(8,128)(2,1)S(1)}, u32[]{:S(2)}, u32[]{:S(2)}) collective-permute-start(bf16[304,128]{1,0:T(8,128)(2,1)S(1)} %pad_maximum_fusion.1), channel_id=1, source_target_pairs={{0,1},{1,0},{2,4},{3,5},{4,2},{5,3},{6,8},{7,9},{8,6},{9,7},{10,12... | collective-permute-start | bytes 233480 | tf_op jit(solution)/shard_map/ppermute | solution.py:373
  3.2 3.8 %copy-start.2 = (bf16[4,1,128,128]{3,2,1,0:T(8,128)(2,1)S(1)}, bf16[4,1,128,128]{3,2,1,0:T(8,128)(2,1)}, u32[]{:S(2)}) copy-start(bf16[4,1,128,128]{3,2,1,0:T(8,128)(2,1)} %middle.6) | copy-start | bytes 393220
  3.2 8.9 %collective-permute-start = (bf16[560,128]{1,0:T(8,128)(2,1)S(1)}, bf16[560,128]{1,0:T(8,128)(2,1)S(1)}, u32[]{:S(2)}, u32[]{:S(2)}) collective-permute-start(bf16[560,128]{1,0:T(8,128)(2,1)S(1)} %pad_maximum_fusion), channel_id=1, source_target_pairs={{0,2},{1,3},{2,0},{3,1},{4,6},{5,7},{6,4},{7,5},{8,10},{9,11},{10,... | collective-permute-start | bytes 430088 | tf_op jit(solution)/shard_map/ppermute | solution.py:372
  9.5 8.7 %collective-permute-start.2 = (bf16[256,128]{1,0:T(8,128)(2,1)S(1)}, bf16[256,128]{1,0:T(8,128)(2,1)S(1)}, u32[]{:S(2)}, u32[]{:S(2)}) collective-permute-start(bf16[256,128]{1,0:T(8,128)(2,1)S(1)} %bitcast.14), channel_id=1, source_target_pairs={{0,1},{1,0},{2,4},{3,5},{4,2},{5,3},{6,8},{7,9},{8,6},{9,7},{10,12... | collective-permute-start | bytes 196616 | tf_op jit(solution)/shard_map/ppermute | solution.py:384
  13.4 12.0 %all-to-all-start = ((f32[32,2,128]{2,1,0:T(2,128)}), f32[32,2,128]{2,1,0:T(2,128)S(1)}, u32[]{:S(2)}, u32[]{:S(2)}) async-start(f32[32,2,128]{2,1,0:T(2,128)} %energy.1), calls=%async_computation | async-start | bytes 65536 | tf_op jit(solution)/shard_map/all_to_all | solution.py:393

commit v11 on v10

--- a/solution.py
+++ b/solution.py
@@ -80,7 +80,20 @@
     return jnp.concatenate([rows[0], for_even(*masks), limits, for_even(*edges(src, 2, REACH))], axis=0), odd
 
 
-def unpack_marks(times, limit, sat, even_in, odd_in, caps, limits):
+def one_pair(even, arrived, work):
+    here, size = lax.axis_index("inline"), lax.axis_size("inline")
+    above = lax.rem(here + (1 if even else 0), 2)
+
+    @pl.when(above != 0)
+    def _():
+        work(arrived, False, (here < size - 1).astype(jnp.float32))
+
+    @pl.when(above == 0)
+    def _():
+        work(arrived, True, (here > 0).astype(jnp.float32))
+
+
+def unpack_marks(times, limit, sat, caps, limits, over_halos):
     lines, cells, depth = sat.shape
     mask_at, limit_at, _ = payload_layout(times, lines)
 
@@ -92,13 +105,13 @@
         for part in range(H // LIMIT_ROWS):
             limits[pl.ds(row_at + part * LIMIT_ROWS, LIMIT_ROWS), :] = value
 
-    by_parity(even_in, odd_in, halo)
+    over_halos(halo)
     for y in range(lines):
         caps[y, pl.ds(H, cells), :] = cap_of(sat[y])
     limits[pl.ds(H, cells), :] = jnp.full((cells, depth), limit[0], jnp.int32).astype(jnp.float32)
 
 
-def unpack_halo(even_in, odd_in, low_out, high_out, even_at=0):
+def unpack_halo(low_out, high_out, over_halos, even_in=None, even_at=0):
     times, lines, _, depth = low_out.shape
     blank = jnp.zeros((ROWS, depth), jnp.float32)
 
@@ -111,7 +124,7 @@
                 out[t, y, pl.ds(field_at, REACH), :] = arrived[pl.ds(at, REACH), :].astype(jnp.float32) * there
                 out[t, y, pl.ds(blank_at, ROWS), :] = blank
 
-    by_parity(even_in, odd_in, halo)
+    over_halos(halo)
 
 
 def image_of(center, far):
@@ -220,7 +233,7 @@
     return masked
 
 
-def each_outer_tile(middle, low, high, visit):
+def each_outer_tile(middle, low, high, visit, sides=(0, 2)):
     times, lines, cells, depth = middle.shape
 
     for group in range(REACH // PAIR):
@@ -248,14 +261,15 @@
 
             return carry
 
-        lax.fori_loop(0, 2, tile, 0)
-
-
-def energy_kernel(limit, src, sat, even_in, odd_in, inner, sums, total, low, high, caps, limits):
+        lax.fori_loop(*sides, tile, 0)
+
+
+def energy_kernel(even, limit, src, sat, arrived, before, sums, total, low, high, caps, limits):
     times, lines, cells, depth = src.shape
-    unpack_marks(times, limit, sat, even_in, odd_in, caps, limits)
-    unpack_halo(even_in, odd_in, low, high)
-    total[...] = inner[...]
+    unpack_marks(times, limit, sat, caps, limits, functools.partial(one_pair, even, arrived))
+    above = lax.rem(lax.axis_index("inline") + (1 if even else 0), 2)
+    unpack_halo(low, high, functools.partial(one_pair, even, arrived))
+    total[...] = before[...]
 
     def visit(y, at, center, offsets, far_at):
         energy, weighted = total[:ROWS, :], total[ROWS:, :]
@@ -271,7 +285,10 @@
         total[:ROWS, :] = energy
         total[ROWS:, :] = weighted
 
-    each_outer_tile(src, low, high, visit)
+    each_outer_tile(src, low, high, visit, (above, above + 1))
+    if sums.shape == total.shape:
+        sums[...] = total[...]
+        return
     rows = [jnp.sum(total[pl.ds(part * ROWS, ROWS), :], axis=0, keepdims=True) for part in range(2)]
     sums[...] = jnp.broadcast_to(jnp.concatenate(rows, axis=0)[None], sums.shape)
 
@@ -279,11 +296,12 @@
 def outer_kernel(source, limit, middle, sat, even_in, odd_in, *refs):
     heavy, plain, low, high, caps, limits = refs[-6:]
     times, lines, cells, depth = middle.shape
-    unpack_marks(times, limit, sat, even_in, odd_in, caps, limits)
+    unpack_marks(times, limit, sat, caps, limits, functools.partial(by_parity, even_in, odd_in))
     if source:
-        unpack_halo(even_in, refs[0], low, high, payload_layout(times, lines)[2])
+        late = functools.partial(by_parity, even_in, refs[0])
+        unpack_halo(low, high, late, even_in, payload_layout(times, lines)[2])
     else:
-        unpack_halo(even_in, odd_in, low, high)
+        unpack_halo(low, high, functools.partial(by_parity, even_in, odd_in))
 
     def visit(y, at, center, offsets, far_at):
         rows = pl.ds(at, ROWS)
@@ -382,14 +400,18 @@
     )
     inner, ahead = lax.optimization_barrier((inner, src))
     odd_late = lax.ppermute(for_odd(*edges(ahead, 2, REACH)), DEVICES, odd_route)
-    sums = call(
-        energy_kernel,
-        "energy",
-        shape((size * lax.axis_size("xline"), 2, depth), jnp.float32),
-        (offset_range, src, sat, even, odd, inner),
-        [pltpu.VMEM((2 * ROWS, depth), jnp.float32), edge, edge, caps, limits],
-        0.15,
-    )
+    by_row = shape((2 * ROWS, depth), jnp.float32)
+    by_device = shape((size * lax.axis_size("xline"), 2, depth), jnp.float32)
+    sums = inner
+    for is_even, arrived, out_shape in ((False, odd, by_row), (True, even, by_device)):
+        sums = call(
+            functools.partial(energy_kernel, is_even),
+            "energy",
+            out_shape,
+            (offset_range, src, sat, arrived, sums),
+            [pltpu.VMEM(by_row.shape, jnp.float32), edge, edge, caps, limits],
+            0.07,
+        )
     gathered = lax.all_to_all(sums, DEVICES, 0, 0, tiled=True)
 
     sums, heavy, plain, ahead, odd_late = lax.optimization_barrier((sums, heavy, plain, src, odd_late))

time: 26.6 us -> 26.5 us (level)
  waiting for transfers between devices: 4.48 us -> 2.92 us
  Pallas kernels: 9.99 us -> 11.2 us
  starting transfers between devices: 9.1 us -> 9.47 us
    pallas_call x6 -> x7, Pallas kernels: 9.99 us -> 11.2 us  [call(): pl.pallas_call(kernel, out_shape=out_shape, in_specs=[SMEM if operand is...]
    ppermute x1, waiting for transfers between devices: 2.48 us -> 1.5 us  [local(): even = lax.ppermute(even, DEVICES, even_route)]
    all_to_all x1, waiting for transfers between devices: 2 us -> 1.42 us  [local(): gathered = lax.all_to_all(sums, DEVICES, 0, 0, tiled=True)]
    all_to_all x1, starting transfers between devices: 4.79 us -> 5.16 us  [local(): gathered = lax.all_to_all(sums, DEVICES, 0, 0, tiled=True)]
  transfers between devices with their start and end apart: 4 -> 4, of which waited for: 2 -> 2; matrix products, arithmetic and copies ran while one was open for 0% -> 0% of each run, Pallas kernels for 35% -> 39%
where the time goes in v11:
time: 26.5 us; the launch traced here: 26.4 us
  Pallas kernels  11.2 us (42%)
  starting transfers between devices  9.47 us (36%)
  waiting for transfers between devices  2.92 us (11%)
  between operations  1.45 us (5%)
  other arithmetic  0.98 us (4%)
  local copies, waits for them, and re-layouts  0.34 us (1%)
    pallas_call x7, Pallas kernels, call(): pl.pallas_call(kernel, out_shape=out_shape, in_specs=[SMEM if operand is...  11.2 us
    all_to_all x1, starting transfers between devices, local(): gathered = lax.all_to_all(sums, DEVICES, 0, 0, tiled=True)  5.16 us
    ppermute x1, starting transfers between devices, local(): even = lax.ppermute(even, DEVICES, even_route)  3.73 us
    ppermute x1, waiting for transfers between devices, local(): even = lax.ppermute(even, DEVICES, even_route)  1.5 us
    all_to_all x1, waiting for transfers between devices, local(): gathered = lax.all_to_all(sums, DEVICES, 0, 0, tiled=True)  1.42 us
    select_n x4, other arithmetic, for_even(): return jnp.where(lax.axis_index('inline') % 2 == 0, high, low)  0.95 us
  transfers between devices with their start and end apart: 4, of which 2 were waited for; matrix products, arithmetic and copies ran while one was open for 0% of the time, Pallas kernels for 39%

profile of v11, /device:TPU:0, one launch (start us, length us, event | category | flops | bytes accessed | tf_op | source)
XLA Modules:
  0.0 26.4 jit_solution(412226079565493683)
XLA Ops:
  1.3 0.0 copy-start.1
  1.3 0.9 %broadcast_select_fusion = (bf16[4,1,64,128]{3,2,1,0:T(8,128)(2,1)S(1)}, bf16[4,1,64,128]{3,2,1,0:T(8,128)(2,1)S(1)}) fusion(pred[]{:T(512)S(6)} %eq.15, bf16[4,1,128,128]{3,2,1,0:T(8,128)(2,1)} %middle.6), kind=kLoop, calls=%fused_computation.5 | loop fusion | flops 65536 | bytes 262145 | tf_op jit(solution)/shard_map/jit(_where)/select_n | solution.py:65
  2.2 0.0 copy-done.1
  2.2 0.0 copy-start
  2.3 0.5 %collective-permute-start.1 = (bf16[304,128]{1,0:T(8,128)(2,1)S(1)}, bf16[304,128]{1,0:T(8,128)(2,1)S(1)}, u32[]{:S(2)}, u32[]{:S(2)}) collective-permute-start(bf16[304,128]{1,0:T(8,128)(2,1)S(1)} %pad_maximum_fusion.1), channel_id=1, source_target_pairs={{0,1},{1,0},{2,4},{3,5},{4,2},{5,3},{6,8},{7,9},{8,6},{9,7},{10,12... | collective-permute-start | bytes 233480 | tf_op jit(solution)/shard_map/ppermute | solution.py:391
  2.8 0.3 %copy-done = bf16[4,1,128,128]{3,2,1,0:T(8,128)(2,1)S(1)} copy-done((bf16[4,1,128,128]{3,2,1,0:T(8,128)(2,1)S(1)}, bf16[4,1,128,128]{3,2,1,0:T(8,128)(2,1)}, u32[]{:S(2)}) %copy-start) | copy-done | bytes 131096
  3.2 0.0 copy-start.2
  3.2 3.7 %collective-permute-start = (bf16[560,128]{1,0:T(8,128)(2,1)S(1)}, bf16[560,128]{1,0:T(8,128)(2,1)S(1)}, u32[]{:S(2)}, u32[]{:S(2)}) collective-permute-start(bf16[560,128]{1,0:T(8,128)(2,1)S(1)} %pad_maximum_fusion), channel_id=1, source_target_pairs={{0,2},{1,3},{2,0},{3,1},{4,6},{5,7},{6,4},{7,5},{8,10},{9,11},{10,... | collective-permute-start | bytes 430088 | tf_op jit(solution)/shard_map/ppermute | solution.py:390
  6.9 0.0 copy-done.2
  6.9 3.2 %src_inner.1 = (f32[4,1,128,128]{3,2,1,0:T(8,128)S(1)}, f32[4,1,128,128]{3,2,1,0:T(8,128)S(1)}, f32[16,128]{1,0:T(8,128)S(1)}) custom-call(s32[1]{0:T(128)S(6)} %copy.15.limit, bf16[4,1,128,128]{3,2,1,0:T(8,128)(2,1)S(1)} %copy-done, bf16[4,1,128,128]{3,2,1,0:T(8,128)(2,1)S(1)} %copy-done.2, s32[1,128,128]{2,1,0:T(8,128)S(1)} %copy-done.1), custom_call_target="tpu_custom_call" | custom-call | flops 21725184 | bytes 891289 | tf_op jit(solution)/shard_map/src_inner/pallas_call | solution.py:373
  10.1 0.1 collective-permute-start.2
  10.2 0.0 collective-permute-done.1.arrived.odd_in
  10.2 0.4 %energy.2.before = f32[16,128]{1,0:T(8,128)S(1)} custom-call(s32[1]{0:T(128)S(6)} %copy.15.limit, bf16[4,1,128,128]{3,2,1,0:T(8,128)(2,1)S(1)} %copy-done, s32[1,128,128]{2,1,0:T(8,128)S(1)} %copy-done.1, bf16[304,128]{1,0:T(8,128)(2,1)S(1)} %collective-permute-done.1.arrived.odd_in, f32[16,128]{1,0:T(8,128)S(1)} %get-tuple-element.30.before), custom_call_target="tpu_custom_call" | custom-call | flops 1789132 | bytes 73400 | tf_op jit(solution)/shard_map/energy/pallas_call | solution.py:373
  10.6 1.5 %collective-permute-done.arrived.even_in = bf16[560,128]{1,0:T(8,128)(2,1)S(1)} collective-permute-done((bf16[560,128]{1,0:T(8,128)(2,1)S(1)}, bf16[560,128]{1,0:T(8,128)(2,1)S(1)}, u32[]{:S(2)}, u32[]{:S(2)}) %collective-permute-start) | collective-permute-done | bytes 143392 | tf_op jit(solution)/shard_map/ppermute | solution.py:390
  12.1 1.0 %energy.3 = f32[32,2,128]{2,1,0:T(2,128)} custom-call(s32[1]{0:T(128)S(6)} %copy.15.limit, bf16[4,1,128,128]{3,2,1,0:T(8,128)(2,1)S(1)} %copy-done, s32[1,128,128]{2,1,0:T(8,128)S(1)} %copy-done.1, bf16[560,128]{1,0:T(8,128)(2,1)S(1)} %collective-permute-done.arrived.even_in, f32[16,128]{1,0:T(8,128)S(1)} %energy.2.before), custom_call_target="tpu_custom_call" | custom-call | flops 1789132 | bytes 73400 | tf_op jit(solution)/shard_map/energy/pallas_call | solution.py:373
  13.1 5.2 %all-to-all-start = ((f32[32,2,128]{2,1,0:T(2,128)}), f32[32,2,128]{2,1,0:T(2,128)S(1)}, u32[]{:S(2)}, u32[]{:S(2)}) async-start(f32[32,2,128]{2,1,0:T(2,128)} %energy.3), calls=%async_computation | async-start | bytes 65536 | tf_op jit(solution)/shard_map/all_to_all | solution.py:415
  18.3 0.0 collective-permute-done.2.refs_0_
  18.3 1.3 %src_outer.1 = (f32[4,1,128,128]{3,2,1,0:T(8,128)S(1)}, f32[4,1,128,128]{3,2,1,0:T(8,128)S(1)}) custom-call(s32[1]{0:T(128)S(6)} %copy.15.limit, bf16[4,1,128,128]{3,2,1,0:T(8,128)(2,1)S(1)} %copy-done, s32[1,128,128]{2,1,0:T(8,128)S(1)} %copy-done.1, ...), custom_call_target="tpu_custom_call", output_to_operand_aliasing={{0}: (5, {}), {1}: (6, {})} | custom-call | flops 6389760 | bytes 262144 | tf_op jit(solution)/shard_map/src_outer/pallas_call | solution.py:373
  19.6 3.1 %rcv_inner.1 = (f32[4,1,128,128]{3,2,1,0:T(8,128)S(1)}, f32[4,1,128,128]{3,2,1,0:T(8,128)S(1)}) custom-call(s32[1]{0:T(128)S(6)} %copy.15.limit, bf16[4,1,128,128]{3,2,1,0:T(8,128)(2,1)S(1)} %copy-done.2, bf16[4,1,128,128]{3,2,1,0:T(8,128)(2,1)S(1)} %copy-done, s32[1,128,128]{2,1,0:T(8,128)S(1)} %copy-done.1), custom_call_target="tpu_custom_call" | custom-call | flops 21725184 | bytes 891289 | tf_op jit(solution)/shard_map/rcv_inner/pallas_call | solution.py:373
  22.8 1.3 %rcv_outer.1 = (f32[4,1,128,128]{3,2,1,0:T(8,128)S(1)}, f32[4,1,128,128]{3,2,1,0:T(8,128)S(1)}) custom-call(s32[1]{0:T(128)S(6)} %copy.15.limit, bf16[4,1,128,128]{3,2,1,0:T(8,128)(2,1)S(1)} %copy-done.2, s32[1,128,128]{2,1,0:T(8,128)S(1)} %copy-done.1, ...), custom_call_target="tpu_custom_call", output_to_operand_aliasing={{0}: (6, {}), {1}: (7, {})} | custom-call | flops 6389760 | bytes 262144 | tf_op jit(solution)/shard_map/rcv_outer/pallas_call | solution.py:373
  24.1 1.4 %all-to-all-done.sums = f32[32,2,128]{2,1,0:T(2,128)S(1)} async-done(((f32[32,2,128]{2,1,0:T(2,128)}), f32[32,2,128]{2,1,0:T(2,128)S(1)}, u32[]{:S(2)}, u32[]{:S(2)}) %all-to-all-start) | async-done | bytes 32800 | tf_op jit(solution)/shard_map/all_to_all | solution.py:415
  25.5 0.9 %combine.1 = (bf16[4,1,128,128]{3,2,1,0:T(8,128)(2,1)}, bf16[4,1,128,128]{3,2,1,0:T(8,128)(2,1)}, f32[1,128]{1,0:T(1,128)}) custom-call(f32[32,2,128]{2,1,0:T(2,128)S(1)} %all-to-all-done.sums, f32[4,1,128,128]{3,2,1,0:T(8,128)S(1)} %get-tuple-element.37.src_heavy, f32[4,1,128,128]{3,2,1,0:T(8,128)S(1)} %get-tuple-element.38.src_plain, ...), custom_call_target="tpu_custom_call" | custom-call | tf_op jit(solution)/shard_map/combine/pallas_call | solution.py:373
  (7 shorter events, 0.1 us)
Async XLA Ops:
  1.3 0.9 %copy-start.1 = (s32[1,128,128]{2,1,0:T(8,128)S(1)}, s32[1,128,128]{2,1,0:T(8,128)}, u32[]{:S(2)}) copy-start(s32[1,128,128]{2,1,0:T(8,128)} %sat.11) | copy-start | bytes 196612
  2.2 0.9 %copy-start = (bf16[4,1,128,128]{3,2,1,0:T(8,128)(2,1)S(1)}, bf16[4,1,128,128]{3,2,1,0:T(8,128)(2,1)}, u32[]{:S(2)}) copy-start(bf16[4,1,128,128]{3,2,1,0:T(8,128)(2,1)} %field.2) | copy-start | bytes 393220
  2.3 7.9 %collective-permute-start.1 = (bf16[304,128]{1,0:T(8,128)(2,1)S(1)}, bf16[304,128]{1,0:T(8,128)(2,1)S(1)}, u32[]{:S(2)}, u32[]{:S(2)}) collective-permute-start(bf16[304,128]{1,0:T(8,128)(2,1)S(1)} %pad_maximum_fusion.1), channel_id=1, source_target_pairs={{0,1},{1,0},{2,4},{3,5},{4,2},{5,3},{6,8},{7,9},{8,6},{9,7},{10,12... | collective-permute-start | bytes 233480 | tf_op jit(solution)/shard_map/ppermute | solution.py:391
  3.2 3.8 %copy-start.2 = (bf16[4,1,128,128]{3,2,1,0:T(8,128)(2,1)S(1)}, bf16[4,1,128,128]{3,2,1,0:T(8,128)(2,1)}, u32[]{:S(2)}) copy-start(bf16[4,1,128,128]{3,2,1,0:T(8,128)(2,1)} %middle.6) | copy-start | bytes 393220
  3.2 8.9 %collective-permute-start = (bf16[560,128]{1,0:T(8,128)(2,1)S(1)}, bf16[560,128]{1,0:T(8,128)(2,1)S(1)}, u32[]{:S(2)}, u32[]{:S(2)}) collective-permute-start(bf16[560,128]{1,0:T(8,128)(2,1)S(1)} %pad_maximum_fusion), channel_id=1, source_target_pairs={{0,2},{1,3},{2,0},{3,1},{4,6},{5,7},{6,4},{7,5},{8,10},{9,11},{10,... | collective-permute-start | bytes 430088 | tf_op jit(solution)/shard_map/ppermute | solution.py:390
  10.1 8.1 %collective-permute-start.2 = (bf16[256,128]{1,0:T(8,128)(2,1)S(1)}, bf16[256,128]{1,0:T(8,128)(2,1)S(1)}, u32[]{:S(2)}, u32[]{:S(2)}) collective-permute-start(bf16[256,128]{1,0:T(8,128)(2,1)S(1)} %bitcast.14), channel_id=1, source_target_pairs={{0,1},{1,0},{2,4},{3,5},{4,2},{5,3},{6,8},{7,9},{8,6},{9,7},{10,12... | collective-permute-start | bytes 196616 | tf_op jit(solution)/shard_map/ppermute | solution.py:402
  13.1 12.4 %all-to-all-start = ((f32[32,2,128]{2,1,0:T(2,128)}), f32[32,2,128]{2,1,0:T(2,128)S(1)}, u32[]{:S(2)}, u32[]{:S(2)}) async-start(f32[32,2,128]{2,1,0:T(2,128)} %energy.3), calls=%async_computation | async-start | bytes 65536 | tf_op jit(solution)/shard_map/all_to_all | solution.py:415

commit v12 on v11

--- a/solution.py
+++ b/solution.py
@@ -20,6 +20,7 @@
 GROUP = 8
 GRANT = 12 << 20
 VMEM = pl.BlockSpec(memory_space=pltpu.VMEM)
+HBM = pl.BlockSpec(memory_space=pltpu.HBM)
 SMEM = pl.BlockSpec(memory_space=pltpu.SMEM)
 
 
@@ -316,27 +317,24 @@
     each_outer_tile(middle, low, high, visit)
 
 
-def combine_kernel(cell_count, sums, src_heavy, src_plain, *refs):
-    pieces, (src_out, rcv_out, semblance_out) = refs[:-3], refs[-3:]
+def combine_kernel(cell_count, sums, src_heavy, src_plain, rcv_heavy, rcv_plain, src_far, rcv_far, semblance_out, near, sems):
     total = jnp.sum(sums[...], axis=0)
     total = jnp.broadcast_to(jnp.sum(total, axis=1, keepdims=True), total.shape)
     energy, weighted = total[0:1], total[1:2]
     semblance = weighted / energy
     inverse_rms = 1.0 / jnp.sqrt(energy / cell_count + EPSILON)
     semblance_out[...] = semblance
-
-    def put(out, start, heavy, plain):
-        times, lines, count, _ = heavy.shape
+    copies = []
+    for position, (heavy, plain, far) in enumerate(((src_heavy, src_plain, src_far), (rcv_heavy, rcv_plain, rcv_far))):
+        times, lines, _, _ = heavy.shape
         for t in range(times):
             for y in range(lines):
                 value = inverse_rms * (heavy[t, y] - semblance * plain[t, y])
-                out[t, y, pl.ds(start, count), :] = value.astype(jnp.bfloat16)
-
-    put(src_out, 0, src_heavy, src_plain)
-    start = 0
-    for heavy, plain in zip(pieces[::2], pieces[1::2]):
-        put(rcv_out, start, heavy, plain)
-        start += heavy.shape[2]
+                near[position, t, y] = value.astype(jnp.bfloat16)
+            copies.append(pltpu.make_async_copy(near.at[position, t], far.at[t], sems.at[position, t]))
+            copies[-1].start()
+    for copy in copies:
+        copy.wait()
 
 
 def exchanges(size, lines):
@@ -443,12 +441,18 @@
     )
 
     cell_count = float(lines * lax.axis_size("xline") * cells * size * depth * (2 * H + 1))
-    src_adj, rcv_adj, semblance = call(
+    src_adj, rcv_adj, semblance = pl.pallas_call(
         functools.partial(combine_kernel, cell_count),
-        "combine",
-        (field_out, field_out, shape((1, depth), jnp.float32)),
-        (gathered, heavy, plain, *pieces),
-    )
+        out_shape=(field_out, field_out, shape((1, depth), jnp.float32)),
+        in_specs=[VMEM] * 5,
+        out_specs=(HBM, HBM, VMEM),
+        scratch_shapes=[
+            pltpu.VMEM((2, *source_field.shape), jnp.bfloat16),
+            pltpu.SemaphoreType.DMA((2, times)),
+        ],
+        compiler_params=grant,
+        name="combine",
+    )(gathered, heavy, plain, *pieces)
     return src_adj, rcv_adj, semblance[0, 0]
 
 

time: 26.5 us -> 26.9 us (1.015)
  waiting for transfers between devices: 2.92 us -> 5.34 us
  Pallas kernels: 11.2 us -> 9.17 us
    pallas_call x7 -> x6, Pallas kernels: 11.2 us -> 7.77 us  [call(): pl.pallas_call(kernel, out_shape=out_shape, in_specs=[SMEM if operand is...]
    pallas_call x0 -> x1, Pallas kernels: none -> 1.4 us  [local(): pl.pallas_call(functools.partial(combine_kernel, cell_count), out_shape=(...]
    all_to_all x1, waiting for transfers between devices: 1.42 us -> 2.7 us  [local(): gathered = lax.all_to_all(sums, DEVICES, 0, 0, tiled=True)]
    ppermute x1, waiting for transfers between devices: 1.5 us -> 2.63 us  [local(): even = lax.ppermute(even, DEVICES, even_route)]
  transfers between devices with their start and end apart: 4 -> 4, of which waited for: 2 -> 2; matrix products, arithmetic and copies ran while one was open for 0% -> 0% of each run, Pallas kernels for 39% -> 29%
where the time goes in v12:
time: 26.9 us; the launch traced here: 26.7 us
  starting transfers between devices  9.45 us (35%)
  Pallas kernels  9.17 us (34%)
  waiting for transfers between devices  5.34 us (20%)
  between operations  1.45 us (5%)
  other arithmetic  0.98 us (4%)
  local copies, waits for them, and re-layouts  0.34 us (1%)
    pallas_call x6, Pallas kernels, call(): pl.pallas_call(kernel, out_shape=out_shape, in_specs=[SMEM if operand is...  7.77 us
    all_to_all x1, starting transfers between devices, local(): gathered = lax.all_to_all(sums, DEVICES, 0, 0, tiled=True)  5.13 us
    ppermute x1, starting transfers between devices, local(): even = lax.ppermute(even, DEVICES, even_route)  3.73 us
    all_to_all x1, waiting for transfers between devices, local(): gathered = lax.all_to_all(sums, DEVICES, 0, 0, tiled=True)  2.7 us
    ppermute x1, waiting for transfers between devices, local(): even = lax.ppermute(even, DEVICES, even_route)  2.63 us
    pallas_call x1, Pallas kernels, local(): pl.pallas_call(functools.partial(combine_kernel, cell_count), out_shape=(...  1.4 us
    select_n x4, other arithmetic, for_even(): return jnp.where(lax.axis_index('inline') % 2 == 0, high, low)  0.95 us
  transfers between devices with their start and end apart: 4, of which 2 were waited for; matrix products, arithmetic and copies ran while one was open for 0% of the time, Pallas kernels for 29%

profile of v12, /device:TPU:0, one launch (start us, length us, event | category | flops | bytes accessed | tf_op | source)
XLA Modules:
  0.0 26.7 jit_solution(15758058256699834767)
XLA Ops:
  1.3 0.0 copy-start.1
  1.3 0.9 %broadcast_select_fusion = (bf16[4,1,64,128]{3,2,1,0:T(8,128)(2,1)S(1)}, bf16[4,1,64,128]{3,2,1,0:T(8,128)(2,1)S(1)}) fusion(pred[]{:T(512)S(6)} %eq.15, bf16[4,1,128,128]{3,2,1,0:T(8,128)(2,1)} %middle.6), kind=kLoop, calls=%fused_computation.5 | loop fusion | flops 65536 | bytes 262145 | tf_op jit(solution)/shard_map/jit(_where)/select_n | solution.py:66
  2.2 0.0 copy-done.1
  2.2 0.0 copy-start
  2.3 0.5 %collective-permute-start.1 = (bf16[304,128]{1,0:T(8,128)(2,1)S(1)}, bf16[304,128]{1,0:T(8,128)(2,1)S(1)}, u32[]{:S(2)}, u32[]{:S(2)}) collective-permute-start(bf16[304,128]{1,0:T(8,128)(2,1)S(1)} %pad_maximum_fusion.1), channel_id=1, source_target_pairs={{0,1},{1,0},{2,4},{3,5},{4,2},{5,3},{6,8},{7,9},{8,6},{9,7},{10,12... | collective-permute-start | bytes 233480 | tf_op jit(solution)/shard_map/ppermute | solution.py:389
  2.8 0.3 %copy-done = bf16[4,1,128,128]{3,2,1,0:T(8,128)(2,1)S(1)} copy-done((bf16[4,1,128,128]{3,2,1,0:T(8,128)(2,1)S(1)}, bf16[4,1,128,128]{3,2,1,0:T(8,128)(2,1)}, u32[]{:S(2)}) %copy-start) | copy-done | bytes 131096
  3.2 0.0 copy-start.2
  3.2 3.7 %collective-permute-start = (bf16[560,128]{1,0:T(8,128)(2,1)S(1)}, bf16[560,128]{1,0:T(8,128)(2,1)S(1)}, u32[]{:S(2)}, u32[]{:S(2)}) collective-permute-start(bf16[560,128]{1,0:T(8,128)(2,1)S(1)} %pad_maximum_fusion), channel_id=1, source_target_pairs={{0,2},{1,3},{2,0},{3,1},{4,6},{5,7},{6,4},{7,5},{8,10},{9,11},{10,... | collective-permute-start | bytes 430088 | tf_op jit(solution)/shard_map/ppermute | solution.py:388
  6.9 0.0 copy-done.2
  6.9 1.9 %src_inner.1 = (f32[4,1,128,128]{3,2,1,0:T(8,128)S(1)}, f32[4,1,128,128]{3,2,1,0:T(8,128)S(1)}, f32[16,128]{1,0:T(8,128)S(1)}) custom-call(s32[1]{0:T(128)S(6)} %copy.15.limit, bf16[4,1,128,128]{3,2,1,0:T(8,128)(2,1)S(1)} %copy-done, bf16[4,1,128,128]{3,2,1,0:T(8,128)(2,1)S(1)} %copy-done.2, s32[1,128,128]{2,1,0:T(8,128)S(1)} %copy-done.1), custom_call_target="tpu_custom_call" | custom-call | flops 21725184 | bytes 891289 | tf_op jit(solution)/shard_map/src_inner/pallas_call | solution.py:371
  8.8 0.1 collective-permute-start.2
  8.9 0.0 collective-permute-done.1.arrived.odd_in
  8.9 0.4 %energy.2.before = f32[16,128]{1,0:T(8,128)S(1)} custom-call(s32[1]{0:T(128)S(6)} %copy.15.limit, bf16[4,1,128,128]{3,2,1,0:T(8,128)(2,1)S(1)} %copy-done, s32[1,128,128]{2,1,0:T(8,128)S(1)} %copy-done.1, bf16[304,128]{1,0:T(8,128)(2,1)S(1)} %collective-permute-done.1.arrived.odd_in, f32[16,128]{1,0:T(8,128)S(1)} %get-tuple-element.30.before), custom_call_target="tpu_custom_call" | custom-call | flops 1789132 | bytes 73400 | tf_op jit(solution)/shard_map/energy/pallas_call | solution.py:371
  9.3 2.6 %collective-permute-done.arrived.even_in = bf16[560,128]{1,0:T(8,128)(2,1)S(1)} collective-permute-done((bf16[560,128]{1,0:T(8,128)(2,1)S(1)}, bf16[560,128]{1,0:T(8,128)(2,1)S(1)}, u32[]{:S(2)}, u32[]{:S(2)}) %collective-permute-start) | collective-permute-done | bytes 143392 | tf_op jit(solution)/shard_map/ppermute | solution.py:388
  11.9 1.0 %energy.3 = f32[32,2,128]{2,1,0:T(2,128)} custom-call(s32[1]{0:T(128)S(6)} %copy.15.limit, bf16[4,1,128,128]{3,2,1,0:T(8,128)(2,1)S(1)} %copy-done, s32[1,128,128]{2,1,0:T(8,128)S(1)} %copy-done.1, bf16[560,128]{1,0:T(8,128)(2,1)S(1)} %collective-permute-done.arrived.even_in, f32[16,128]{1,0:T(8,128)S(1)} %energy.2.before), custom_call_target="tpu_custom_call" | custom-call | flops 1789132 | bytes 73400 | tf_op jit(solution)/shard_map/energy/pallas_call | solution.py:371
  12.9 5.1 %all-to-all-start = ((f32[32,2,128]{2,1,0:T(2,128)}), f32[32,2,128]{2,1,0:T(2,128)S(1)}, u32[]{:S(2)}, u32[]{:S(2)}) async-start(f32[32,2,128]{2,1,0:T(2,128)} %energy.3), calls=%async_computation | async-start | bytes 65536 | tf_op jit(solution)/shard_map/all_to_all | solution.py:413
  18.1 0.0 collective-permute-done.2.refs_0_
  18.1 1.3 %src_outer.1 = (f32[4,1,128,128]{3,2,1,0:T(8,128)S(1)}, f32[4,1,128,128]{3,2,1,0:T(8,128)S(1)}) custom-call(s32[1]{0:T(128)S(6)} %copy.15.limit, bf16[4,1,128,128]{3,2,1,0:T(8,128)(2,1)S(1)} %copy-done, s32[1,128,128]{2,1,0:T(8,128)S(1)} %copy-done.1, ...), custom_call_target="tpu_custom_call", output_to_operand_aliasing={{0}: (5, {}), {1}: (6, {})} | custom-call | flops 6389760 | bytes 262144 | tf_op jit(solution)/shard_map/src_outer/pallas_call | solution.py:371
  19.4 1.9 %rcv_inner.1 = (f32[4,1,128,128]{3,2,1,0:T(8,128)S(1)}, f32[4,1,128,128]{3,2,1,0:T(8,128)S(1)}) custom-call(s32[1]{0:T(128)S(6)} %copy.15.limit, bf16[4,1,128,128]{3,2,1,0:T(8,128)(2,1)S(1)} %copy-done.2, bf16[4,1,128,128]{3,2,1,0:T(8,128)(2,1)S(1)} %copy-done, s32[1,128,128]{2,1,0:T(8,128)S(1)} %copy-done.1), custom_call_target="tpu_custom_call" | custom-call | flops 21725184 | bytes 891289 | tf_op jit(solution)/shard_map/rcv_inner/pallas_call | solution.py:371
  21.3 1.3 %rcv_outer.1 = (f32[4,1,128,128]{3,2,1,0:T(8,128)S(1)}, f32[4,1,128,128]{3,2,1,0:T(8,128)S(1)}) custom-call(s32[1]{0:T(128)S(6)} %copy.15.limit, bf16[4,1,128,128]{3,2,1,0:T(8,128)(2,1)S(1)} %copy-done.2, s32[1,128,128]{2,1,0:T(8,128)S(1)} %copy-done.1, ...), custom_call_target="tpu_custom_call", output_to_operand_aliasing={{0}: (6, {}), {1}: (7, {})} | custom-call | flops 6389760 | bytes 262144 | tf_op jit(solution)/shard_map/rcv_outer/pallas_call | solution.py:371
  22.6 2.7 %all-to-all-done.sums = f32[32,2,128]{2,1,0:T(2,128)S(1)} async-done(((f32[32,2,128]{2,1,0:T(2,128)}), f32[32,2,128]{2,1,0:T(2,128)S(1)}, u32[]{:S(2)}, u32[]{:S(2)}) %all-to-all-start) | async-done | bytes 32800 | tf_op jit(solution)/shard_map/all_to_all | solution.py:413
  25.3 1.4 %combine.1 = (bf16[4,1,128,128]{3,2,1,0:T(8,128)(2,1)}, bf16[4,1,128,128]{3,2,1,0:T(8,128)(2,1)}, f32[1,128]{1,0:T(1,128)}) custom-call(f32[32,2,128]{2,1,0:T(2,128)S(1)} %all-to-all-done.sums, f32[4,1,128,128]{3,2,1,0:T(8,128)S(1)} %get-tuple-element.37.src_heavy, f32[4,1,128,128]{3,2,1,0:T(8,128)S(1)} %get-tuple-element.38.src_plain, ...), custom_call_target="tpu_custom_call" | custom-call | tf_op jit(solution)/shard_map/combine/pallas_call | solution.py:444
  (7 shorter events, 0.1 us)
Async XLA Ops:
  1.3 0.9 %copy-start.1 = (s32[1,128,128]{2,1,0:T(8,128)S(1)}, s32[1,128,128]{2,1,0:T(8,128)}, u32[]{:S(2)}) copy-start(s32[1,128,128]{2,1,0:T(8,128)} %sat.11) | copy-start | bytes 196612
  2.2 0.9 %copy-start = (bf16[4,1,128,128]{3,2,1,0:T(8,128)(2,1)S(1)}, bf16[4,1,128,128]{3,2,1,0:T(8,128)(2,1)}, u32[]{:S(2)}) copy-start(bf16[4,1,128,128]{3,2,1,0:T(8,128)(2,1)} %field.2) | copy-start | bytes 393220
  2.3 6.6 %collective-permute-start.1 = (bf16[304,128]{1,0:T(8,128)(2,1)S(1)}, bf16[304,128]{1,0:T(8,128)(2,1)S(1)}, u32[]{:S(2)}, u32[]{:S(2)}) collective-permute-start(bf16[304,128]{1,0:T(8,128)(2,1)S(1)} %pad_maximum_fusion.1), channel_id=1, source_target_pairs={{0,1},{1,0},{2,4},{3,5},{4,2},{5,3},{6,8},{7,9},{8,6},{9,7},{10,12... | collective-permute-start | bytes 233480 | tf_op jit(solution)/shard_map/ppermute | solution.py:389
  3.2 3.8 %copy-start.2 = (bf16[4,1,128,128]{3,2,1,0:T(8,128)(2,1)S(1)}, bf16[4,1,128,128]{3,2,1,0:T(8,128)(2,1)}, u32[]{:S(2)}) copy-start(bf16[4,1,128,128]{3,2,1,0:T(8,128)(2,1)} %middle.6) | copy-start | bytes 393220
  3.2 8.8 %collective-permute-start = (bf16[560,128]{1,0:T(8,128)(2,1)S(1)}, bf16[560,128]{1,0:T(8,128)(2,1)S(1)}, u32[]{:S(2)}, u32[]{:S(2)}) collective-permute-start(bf16[560,128]{1,0:T(8,128)(2,1)S(1)} %pad_maximum_fusion), channel_id=1, source_target_pairs={{0,2},{1,3},{2,0},{3,1},{4,6},{5,7},{6,4},{7,5},{8,10},{9,11},{10,... | collective-permute-start | bytes 430088 | tf_op jit(solution)/shard_map/ppermute | solution.py:388
  8.8 9.2 %collective-permute-start.2 = (bf16[256,128]{1,0:T(8,128)(2,1)S(1)}, bf16[256,128]{1,0:T(8,128)(2,1)S(1)}, u32[]{:S(2)}, u32[]{:S(2)}) collective-permute-start(bf16[256,128]{1,0:T(8,128)(2,1)S(1)} %bitcast.14), channel_id=1, source_target_pairs={{0,1},{1,0},{2,4},{3,5},{4,2},{5,3},{6,8},{7,9},{8,6},{9,7},{10,12... | collective-permute-start | bytes 196616 | tf_op jit(solution)/shard_map/ppermute | solution.py:400
  12.9 12.4 %all-to-all-start = ((f32[32,2,128]{2,1,0:T(2,128)}), f32[32,2,128]{2,1,0:T(2,128)S(1)}, u32[]{:S(2)}, u32[]{:S(2)}) async-start(f32[32,2,128]{2,1,0:T(2,128)} %energy.3), calls=%async_computation | async-start | bytes 65536 | tf_op jit(solution)/shard_map/all_to_all | solution.py:413
